TPU v7x, 32 devices: a whole 2x2x4 slice. The times are simulated.
32 devices in a mesh: batch: 8 (over y, x, core), expert: 4 (over z).
Axes of the slice: x: 2, y: 2, z: 4, core: 2. Of those that a mesh axis runs over, the one named last changes fastest.
Arguments:
- tokens: float32 [2, 16, 1024, 512], P(None, 'batch', 'expert'), may hold values from -6 to 6
- cotangent: float32 [2, 16, 1024, 512], P(None, 'batch', 'expert'), may hold values from -6 to 6
- query_key_value_weight: bfloat16 [512, 1536], replicated, may hold values from -0.25 to 0.25
- output_weight: bfloat16 [512, 512], replicated, may hold values from -2 to 2
- controller_weight: bfloat16 [512, 16], replicated, may hold values from -0.1875 to 0.1875
- w_first: bfloat16 [16, 512, 2048], P('expert'), may hold values from -0.5 to 0.5
- w_second: bfloat16 [16, 2048, 512], P('expert'), may hold values from -0.5 to 0.5
- gain_one: float32 [512], replicated, may hold values from 0.5 to 1.5
- gain_two: float32 [512], replicated, may hold values from 0.5 to 1.5
- group_sizes: int32 [2, 3], replicated, may hold values from 4 to 8, as said below
- live: int32 [2, 16], replicated, may hold values from 0 to 1, as said below
Outputs:
- out: float32 [2, 16, 1024, 512], P(None, 'batch', 'expert')
- grad_input: float32 [2, 16, 1024, 512], P(None, 'batch', 'expert')
- grad_qkv: float32 [512, 1536], P(('batch', 'expert'))
- grad_out: float32 [512, 512], P(('batch', 'expert'))
- grad_ctrl: float32 [512, 16], P(('batch', 'expert'))
- grad_first: float32 [16, 512, 2048], P('expert', None, 'batch')
- grad_second: float32 [16, 2048, 512], P('expert', 'batch')
- grad_gain_one: float32 [512], P(('batch', 'expert'))
- grad_gain_two: float32 [512], P(('batch', 'expert'))
Inputs may be any that keep to these rules, and one draw needn't show every extreme that they name: `group_sizes`: each row sums to 16; one size is exactly 8, the others 4. `live`: each row has at least one 0, among its last 3 sequences.
All inputs are finite; a program needn't handle non-finite values.
Results may differ from a plain program's by a relative error of at most 0.019.
Values may be sent and summed in bfloat16 or wider, within the bound.
No kernel may reach another device: no remote copies, remote signals or barrier semaphores. Data moves between devices by JAX's collectives and lax.ppermute only.
A program may use at most 320 MiB of HBM per device.

v0:
```python
import functools

import jax
import jax.numpy as jnp
from jax import lax
from jax.sharding import PartitionSpec as P

HEADS = 8


HIGH_PRECISION = lax.Precision.HIGHEST
NEG_FILL = -1e30


def group_tables(group_row, live_row):
    seq_count = live_row.shape[0]
    group_ends = jnp.cumsum(group_row)
    group_starts = group_ends - group_row
    numbers = jnp.arange(seq_count, dtype=jnp.int32)
    member = (numbers[:, None] >= group_starts[None, :]) & (numbers[:, None] < group_ends[None, :])
    leading = jnp.any(numbers[:, None] == group_starts[None, :], axis=1)
    taking = (live_row > 0) | leading
    return (member, taking)


def group_softmax(router_logits, member, taking):
    inside = member[:, :, None, None]
    masked = jnp.where(taking[:, None, None], router_logits, NEG_FILL)
    highest = jnp.max(jnp.where(inside, masked[:, None], NEG_FILL), axis=0)
    row_high = jnp.sum(jnp.where(inside, highest[None], 0.0), axis=1)
    scaled = jnp.where(taking[:, None, None], jnp.exp(router_logits - row_high), 0.0)
    group_sums = jnp.sum(jnp.where(inside, scaled[:, None], 0.0), axis=0)
    row_sums = jnp.sum(jnp.where(inside, group_sums[None], 0.0), axis=1)
    return scaled / row_sums


def norm_forward(values_in, scaling):
    centred = values_in - jnp.mean(values_in, -1, keepdims=True)
    inverse = lax.rsqrt(jnp.mean(centred * centred, -1, keepdims=True) + 1e-05)
    normed = centred * inverse
    return (normed * scaling, normed, inverse)


def norm_backward(incoming, normed, inverse, scaling):
    scaled_grad = incoming * scaling
    returned_grad = inverse * (
        scaled_grad
        - jnp.mean(scaled_grad, -1, keepdims=True)
        - normed * jnp.mean(scaled_grad * normed, -1, keepdims=True)
    )
    return (returned_grad, jnp.sum(incoming * normed, axis=(0, 1)))


def attention_probs(query_heads, key_heads, causal, logsum, factor):
    scores = (
        jnp.einsum("sqhc,skhc->shqk", query_heads, key_heads, preferred_element_type=jnp.float32)
        * factor
    )
    return jnp.where(causal, jnp.exp(scores - logsum), 0.0)


def body(
    tokens,
    cotangent,
    query_key_value_weight,
    output_weight,
    controller_weight,
    w_first,
    w_second,
    gain_one,
    gain_two,
    group_sizes,
    live,
):
    micro_count, seq_here, local_len, model_width = tokens.shape
    head_dim = model_width // HEADS
    factor = head_dim ** (-0.5)
    length = local_len * lax.axis_size("expert")
    query_pos = lax.axis_index("expert") * local_len + jnp.arange(local_len, dtype=jnp.int32)
    key_pos = jnp.arange(length, dtype=jnp.int32)
    causal = key_pos[None, :] <= query_pos[:, None]
    ctrl_wide = controller_weight.astype(jnp.float32)
    sum_first = jnp.zeros(w_first.shape, jnp.float32)
    sum_second = jnp.zeros(w_second.shape, jnp.float32)
    sum_qkv = jnp.zeros(query_key_value_weight.shape, jnp.float32)
    sum_out = jnp.zeros(output_weight.shape, jnp.float32)
    sum_ctrl = jnp.zeros(controller_weight.shape, jnp.float32)
    sum_gain_one = jnp.zeros(gain_one.shape, jnp.float32)
    sum_gain_two = jnp.zeros(gain_two.shape, jnp.float32)
    outputs = []
    grads_in = []
    for micro_step in range(micro_count):
        member, taking = group_tables(group_sizes[micro_step], live[micro_step])
        input_rows = tokens[micro_step]
        attn_norm, normed_one, inverse_one = norm_forward(input_rows, gain_one)
        attention_input = attn_norm.astype(jnp.bfloat16)
        projected_rows = jnp.einsum(
            "mtg,gj->mtj",
            attention_input,
            query_key_value_weight,
            preferred_element_type=jnp.float32,
        ).astype(jnp.bfloat16)
        queries = projected_rows[..., :model_width]
        keys_here = projected_rows[..., model_width : 2 * model_width]
        values_here = projected_rows[..., 2 * model_width :]
        keys_all, values_all = (
            lax.all_gather(keys_here, "expert", axis=1, tiled=True),
            lax.all_gather(values_here, "expert", axis=1, tiled=True),
        )
        query_heads = queries.reshape(seq_here, local_len, HEADS, head_dim)
        key_heads = keys_all.reshape(seq_here, length, HEADS, head_dim)
        value_heads = values_all.reshape(seq_here, length, HEADS, head_dim)
        scores = (
            jnp.einsum(
                "sqhc,skhc->shqk", query_heads, key_heads, preferred_element_type=jnp.float32
            )
            * factor
        )
        scores = jnp.where(causal, scores, NEG_FILL)
        highest = jnp.max(scores, -1, keepdims=True)
        logsum = highest + jnp.log(jnp.sum(jnp.exp(scores - highest), -1, keepdims=True))
        probs_low = jnp.exp(scores - logsum).astype(jnp.bfloat16)
        context_rows = jnp.einsum(
            "shqk,skhc->sqhc", probs_low, value_heads, preferred_element_type=jnp.float32
        )
        context_rows = context_rows.reshape(seq_here, local_len, model_width).astype(jnp.bfloat16)
        residual_stream = input_rows + jnp.einsum(
            "mtg,gj->mtj", context_rows, output_weight, preferred_element_type=jnp.float32
        )
        mix_norm, normed_two, inverse_two = norm_forward(residual_stream, gain_two)
        mix_low = mix_norm.astype(jnp.bfloat16)
        mix_pos = lax.all_to_all(mix_low, "batch", split_axis=1, concat_axis=0, tiled=True)
        router_logits = jnp.einsum(
            "spd,de->spe", mix_pos, controller_weight, preferred_element_type=jnp.float32
        )
        gate_vals, gate_pull = jax.vjp(
            functools.partial(group_softmax, member=member, taking=taking), router_logits
        )
        weights_low = jnp.where(
            member[:, None, :, None],
            gate_vals.astype(jnp.bfloat16)[:, :, None, :],
            jnp.zeros((), jnp.bfloat16),
        )
        blended_rows = jnp.einsum(
            "spke,spd->pked", weights_low, mix_pos, preferred_element_type=jnp.float32
        ).astype(jnp.bfloat16)
        mixed_recv = lax.all_to_all(blended_rows, "expert", split_axis=2, concat_axis=0, tiled=True)
        pre_act = jnp.einsum(
            "pked,edf->pkef", mixed_recv, w_first, preferred_element_type=jnp.float32
        )
        activated, gelu_pull = jax.vjp(jax.nn.gelu, pre_act)
        act_low = activated.astype(jnp.bfloat16)
        expert_output = jnp.einsum(
            "pkef,efd->pked", act_low, w_second, preferred_element_type=jnp.float32
        ).astype(jnp.bfloat16)
        returned = lax.all_to_all(expert_output, "expert", split_axis=0, concat_axis=2, tiled=True)
        dispersed_rows = jnp.einsum(
            "spke,pked->spd", weights_low, returned, preferred_element_type=jnp.float32
        ).astype(jnp.bfloat16)
        spread_seq = lax.all_to_all(
            dispersed_rows, "batch", split_axis=0, concat_axis=1, tiled=True
        )
        outputs.append(residual_stream + spread_seq.astype(jnp.float32))
        cot_here = cotangent[micro_step]
        grad_spread = lax.all_to_all(
            cot_here.astype(jnp.bfloat16), "batch", split_axis=1, concat_axis=0, tiled=True
        )
        grad_weights = jnp.einsum(
            "spd,pked->spke", grad_spread, returned, preferred_element_type=jnp.float32
        )
        grad_eout = jnp.einsum(
            "spke,spd->pked", weights_low, grad_spread, preferred_element_type=jnp.float32
        ).astype(jnp.bfloat16)
        grad_eout_recv = lax.all_to_all(
            grad_eout, "expert", split_axis=2, concat_axis=0, tiled=True
        )
        grad_hidden = jnp.einsum(
            "pked,efd->pkef", grad_eout_recv, w_second, preferred_element_type=jnp.float32
        )
        step_second = jnp.einsum(
            "pkef,pked->efd", act_low, grad_eout_recv, preferred_element_type=jnp.float32
        )
        grad_pre = gelu_pull(grad_hidden)[0].astype(jnp.bfloat16)
        step_first = jnp.einsum(
            "pked,pkef->edf", mixed_recv, grad_pre, preferred_element_type=jnp.float32
        )
        sum_first = sum_first + step_first
        sum_second = sum_second + step_second
        grad_mixed = jnp.einsum(
            "pkef,edf->pked", grad_pre, w_first, preferred_element_type=jnp.float32
        ).astype(jnp.bfloat16)
        grad_mix_groups = lax.all_to_all(
            grad_mixed, "expert", split_axis=0, concat_axis=2, tiled=True
        )
        grad_weights = grad_weights + jnp.einsum(
            "pked,spd->spke", grad_mix_groups, mix_pos, preferred_element_type=jnp.float32
        )
        grad_gates = jnp.sum(jnp.where(member[:, None, :, None], grad_weights, 0.0), axis=2)
        grad_logits = gate_pull(grad_gates)[0]
        sum_ctrl = sum_ctrl + jnp.einsum(
            "spd,spe->de", mix_pos.astype(jnp.float32), grad_logits, precision=HIGH_PRECISION
        )
        grad_mix = jnp.einsum(
            "spke,pked->spd", weights_low, grad_mix_groups, preferred_element_type=jnp.float32
        )
        grad_mix = grad_mix + jnp.einsum(
            "spe,de->spd", grad_logits, ctrl_wide, precision=HIGH_PRECISION
        )
        grad_mix_seq = lax.all_to_all(
            grad_mix.astype(jnp.bfloat16), "batch", split_axis=0, concat_axis=1, tiled=True
        )
        grad_norm_two, gain_two_step = norm_backward(
            grad_mix_seq.astype(jnp.float32), normed_two, inverse_two, gain_two
        )
        sum_gain_two = sum_gain_two + gain_two_step
        grad_resid = cot_here + grad_norm_two
        attention_gradient = grad_resid.astype(jnp.bfloat16)
        sum_out = sum_out + jnp.einsum(
            "hui,huq->iq", context_rows, attention_gradient, preferred_element_type=jnp.float32
        )
        grad_context = jnp.einsum(
            "wfh,yh->wfy", attention_gradient, output_weight, preferred_element_type=jnp.float32
        ).astype(jnp.bfloat16)
        context_heads = grad_context.reshape(seq_here, local_len, HEADS, head_dim)
        probs_full = attention_probs(query_heads, key_heads, causal, logsum, factor)
        grad_probs = jnp.einsum(
            "sqhc,skhc->shqk", context_heads, value_heads, preferred_element_type=jnp.float32
        )
        row_dots = jnp.sum(grad_probs * probs_full, -1, keepdims=True)
        grad_scores = (probs_full * (grad_probs - row_dots)).astype(jnp.bfloat16)
        grad_query = (
            jnp.einsum(
                "shqk,skhc->sqhc", grad_scores, key_heads, preferred_element_type=jnp.float32
            )
            * factor
        )
        grad_query = grad_query.reshape(seq_here, local_len, model_width)
        key_terms = (
            jnp.einsum(
                "shqk,sqhc->skhc", grad_scores, query_heads, preferred_element_type=jnp.float32
            )
            * factor
        )
        value_terms = jnp.einsum(
            "shqk,sqhc->skhc",
            probs_full.astype(jnp.bfloat16),
            context_heads,
            preferred_element_type=jnp.float32,
        )
        grad_key, grad_value = (
            lax.psum_scatter(
                key_terms.reshape(seq_here, length, model_width).astype(jnp.bfloat16),
                "expert",
                scatter_dimension=1,
                tiled=True,
            ).astype(jnp.float32),
            lax.psum_scatter(
                value_terms.reshape(seq_here, length, model_width).astype(jnp.bfloat16),
                "expert",
                scatter_dimension=1,
                tiled=True,
            ).astype(jnp.float32),
        )
        query_key_value_row_gradient = jnp.concatenate(
            [grad_query, grad_key, grad_value], axis=-1
        ).astype(jnp.bfloat16)
        sum_qkv = sum_qkv + jnp.einsum(
            "hui,huq->iq",
            attention_input,
            query_key_value_row_gradient,
            preferred_element_type=jnp.float32,
        )
        grad_attn_in = jnp.einsum(
            "wfh,yh->wfy",
            query_key_value_row_gradient,
            query_key_value_weight,
            preferred_element_type=jnp.float32,
        )
        grad_norm_one, gain_one_step = norm_backward(
            grad_attn_in, normed_one, inverse_one, gain_one
        )
        sum_gain_one = sum_gain_one + gain_one_step
        grads_in.append(grad_resid + grad_norm_one)
    grad_first, grad_second = (
        lax.psum_scatter(
            sum_first.astype(jnp.bfloat16), "batch", scatter_dimension=2, tiled=True
        ).astype(jnp.float32),
        lax.psum_scatter(
            sum_second.astype(jnp.bfloat16), "batch", scatter_dimension=1, tiled=True
        ).astype(jnp.float32),
    )
    grad_qkv, grad_out, grad_ctrl, grad_gain_one, grad_gain_two = (
        lax.psum_scatter(sum_qkv, ("batch", "expert"), scatter_dimension=0, tiled=True),
        lax.psum_scatter(sum_out, ("batch", "expert"), scatter_dimension=0, tiled=True),
        lax.psum_scatter(sum_ctrl, ("batch", "expert"), scatter_dimension=0, tiled=True),
        lax.psum_scatter(sum_gain_one, ("batch", "expert"), scatter_dimension=0, tiled=True),
        lax.psum_scatter(sum_gain_two, ("batch", "expert"), scatter_dimension=0, tiled=True),
    )
    return (
        jnp.stack(outputs),
        jnp.stack(grads_in),
        grad_qkv,
        grad_out,
        grad_ctrl,
        grad_first,
        grad_second,
        grad_gain_one,
        grad_gain_two,
    )


def solution(mesh):
    placed = (
        P(None, "batch", "expert", None),
        P(None, "batch", "expert", None),
        P(),
        P(),
        P(),
        P("expert", None, None),
        P("expert", None, None),
        P(),
        P(),
        P(),
        P(),
    )
    return jax.shard_map(
        body,
        mesh=mesh,
        in_specs=placed,
        out_specs=(
            P(None, "batch", "expert", None),
            P(None, "batch", "expert", None),
            P(("batch", "expert"), None),
            P(("batch", "expert"), None),
            P(("batch", "expert"), None),
            P("expert", None, "batch"),
            P("expert", "batch", None),
            P(("batch", "expert")),
            P(("batch", "expert")),
        ),
        check_vma=False,
    )
```

profile of v0, /device:TPU:0, one launch (start us, length us, event | category | flops | bytes accessed | tf_op | source)
XLA Modules:
  0.0 1477.9 jit_solution(9478584086364784576)
XLA Ops:
  19.7 5.2 all-to-all-start.8
  25.7 38.1 %all-gather.7.cloned.1.call-done = bf16[2,1024,512]{2,1,0:T(8,128)(2,1)} async-done(((bf16[2,256,512]{2,1,0:T(8,128)(2,1)}), bf16[2,1024,512]{2,1,0:T(8,128)(2,1)}) %all-gather.7.cloned.1.call-update) | async-done | bytes 2097168 | tf_op jit(solution)/shard_map/all_gather | solution.py:107
  67.7 4.5 fusion.2
  72.2 4.4 exponential_reduce_fusion.1
  77.9 32.8 %all-gather.5.cloned.1.call-done = bf16[2,1024,512]{2,1,0:T(8,128)(2,1)} async-done(((bf16[2,256,512]{2,1,0:T(8,128)(2,1)}), bf16[2,1024,512]{2,1,0:T(8,128)(2,1)}) %all-gather.5.cloned.1.call-update) | async-done | bytes 2097168 | tf_op jit(solution)/shard_map/all_gather | solution.py:108
  114.6 8.7 fusion.99
  126.0 4.3 all-to-all-start
  150.7 4.3 all-to-all-start.9
  162.9 54.5 %all-to-all-done.9 = bf16[32,3,16,512]{3,0,1,2:T(8,128)(2,1)} async-done(((bf16[32,3,16,512]{3,0,1,2:T(8,128)(2,1)}), bf16[32,3,16,512]{3,0,1,2:T(8,128)(2,1)}, u32[]{:S(2)}, u32[]{:S(2)}) %all-to-all-start.9) | async-done | bytes 1572896 | tf_op jit(solution)/shard_map/all_to_all | solution.py:174
  217.4 4.4 all-to-all-start.1
  225.0 53.4 %all-to-all-done.1 = bf16[32,3,16,512]{3,0,1,2:T(8,128)(2,1)} async-done(((bf16[32,3,16,512]{3,0,1,2:T(8,128)(2,1)}), bf16[32,3,16,512]{3,0,1,2:T(8,128)(2,1)}, u32[]{:S(2)}, u32[]{:S(2)}) %all-to-all-start.1) | async-done | bytes 1572896 | tf_op jit(solution)/shard_map/all_to_all | solution.py:147
  281.2 6.2 fusion.42
  287.5 4.3 fusion.86
  294.3 4.6 all-to-all-start.2
  298.9 14.1 fusion.10
  313.0 9.1 fusion.92
  324.5 8.3 all-to-all-done.2
  332.8 4.8 all-to-all-start.10
  362.7 11.4 all-to-all-done.10
  374.1 8.8 all-to-all-start.3
  408.9 4.2 all-to-all-start.11
  413.1 9.9 fusion.220
  425.1 4.4 all-to-all-start.12
  441.6 19.0 %multiply_reduce_fusion.1 = (f32[2,8,256]{2,1,0:T(8,128)}, f32[2,8,256]{2,1,0:T(8,128)S(1)}, f32[2,8,256,1024]{3,2,1,0:T(8,128)}) fusion(f32[2,8,256,1024]{3,2,1,0:T(8,128)} %copy-done.1, f32[2,8,256]{2,1,0:T(8,128)S(1)} %copy-done.50, pred[256,1024]{1,0:T(8,128)(4,1)S(1)} %iota_compare_fusion, f32[2,8,256,1024]{3,2,1,0:T(8,128)} %fusion.220, ...), kind=kOutput, calls=%fused_computation.12 | convolution fusion | flops 570417152 | bytes 53264384 | tf_op jit(solution)/shard_map/sqhc,skhc->shqk/dot_general | solution.py:226
  460.7 8.1 exponential_reduce_fusion
  468.9 8.2 fusion.98
  479.8 4.5 all-to-all-start.4
  488.8 5.3 all-to-all-done.4
  504.6 4.3 all-to-all-start.13
  512.6 31.3 %all-to-all-done.13 = bf16[32,3,16,512]{3,0,1,2:T(8,128)(2,1)} async-done(((bf16[32,3,16,512]{3,0,1,2:T(8,128)(2,1)}), bf16[32,3,16,512]{3,0,1,2:T(8,128)(2,1)}, u32[]{:S(2)}, u32[]{:S(2)}) %all-to-all-start.13) | async-done | bytes 1572896 | tf_op jit(solution)/shard_map/all_to_all | solution.py:174
  543.9 4.4 all-to-all-start.5
  551.0 33.8 %all-to-all-done.5 = bf16[32,3,16,512]{3,0,1,2:T(8,128)(2,1)} async-done(((bf16[32,3,16,512]{3,0,1,2:T(8,128)(2,1)}), bf16[32,3,16,512]{3,0,1,2:T(8,128)(2,1)}, u32[]{:S(2)}, u32[]{:S(2)}) %all-to-all-start.5) | async-done | bytes 1572896 | tf_op jit(solution)/shard_map/all_to_all | solution.py:147
  587.4 6.0 fusion.40
  593.5 10.2 fusion.83
  606.0 4.8 all-to-all-start.6
  610.8 14.1 fusion.17
  624.9 9.1 fusion.89
  636.4 10.9 all-to-all-done.6
  647.3 4.5 all-to-all-start.14
  658.8 29.6 %all-to-all-done.14 = bf16[128,3,4,512]{3,2,1,0:T(4,128)(2,1)} async-done(((bf16[128,3,4,512]{3,2,1,0:T(4,128)(2,1)}), bf16[128,3,4,512]{3,2,1,0:T(4,128)(2,1)}, u32[]{:S(2)}, u32[]{:S(2)}) %all-to-all-start.14) | async-done | bytes 1572896 | tf_op jit(solution)/shard_map/all_to_all | solution.py:192
  717.4 4.5 all-to-all-start.15
  724.8 6.9 all-to-all-done.15
  731.7 4.1 all-to-all-start.7
  740.4 5.3 all-to-all-done.7
  753.0 9.4 fusion.62
  766.8 26.6 %multiply_convert_fusion.1 = (bf16[2,8,256,1024]{3,2,1,0:T(8,128)(2,1)}, f32[2,8,256]{2,1,0:T(8,128)S(1)}, f32[2,8,256,1024]{3,2,1,0:T(8,128)}) fusion(f32[2,8,256,1024]{3,2,1,0:T(8,128)} %get-tuple-element.69, f32[2,8,256,1024]{3,2,1,0:T(8,128)} %copy-done.1, f32[2,8,256]{2,1,0:T(8,128)S(1)} %copy-done.58, f32[2,8,256]{2,1,0:T(8,128)S(1)} %copy-done.51, ...), kind=kOutput, calls=%fused_computation.11 | convolution fusion | flops 583004160 | bytes 78446592 | tf_op jit(solution)/shard_map/sqhc,skhc->shqk/dot_general | solution.py:226
  793.4 12.4 multiply_convert_fusion
  813.7 9.8 fusion.59
  827.6 6.3 multiply_convert_fusion.3
  837.9 11.9 fusion.209
  849.8 15.0 %fusion = bf16[4,2048,512]{2,1,0:T(8,128)(2,1)} fusion(f32[4,2048,512,1]{2,1,3,0:T(8,128)} %fusion.209, bf16[128,3,4,512]{3,0,1,2:T(8,128)(2,1)S(1)} %bitcast.538, f32[4,128,3,2048]{3,1,2,0:T(8,128)} %copy-done.13), kind=kOutput, calls=%fused_computation.5 | convolution fusion | flops 3257925632 | bytes 39321600 | tf_op jit(solution)/shard_map/pkef,pked->efd/dot_general | solution.py:180
  865.1 13.6 fusion.221
  878.8 12.1 fusion.1
  902.8 7.5 fusion.102
  911.5 7.5 fusion.103
  921.1 4.5 convolution_bitcast_fusion
  925.7 20.3 %reduce-scatter.10.cloned.1.call-done = bf16[2,256,512]{2,1,0:T(8,128)(2,1)} async-done(((bf16[2,1024,512]{2,1,0:T(8,128)(2,1)}), bf16[2,256,512]{2,1,0:T(8,128)(2,1)}) %reduce-scatter.10.cloned.1.call-update) | async-done | bytes 524304 | tf_op jit(solution)/shard_map/reduce_scatter | solution.py:251
  946.0 5.4 fusion.58
  959.6 40.1 %all-reduce.2 = (f32[512]{0:T(512)S(1)}, f32[512]{0:T(512)S(1)}) all-reduce(f32[512]{0:T(512)S(1)} %add.180, f32[512]{0:T(512)S(1)} %add.181), channel_id=11, replica_groups=mesh['batch'=8,'expert'=4] {'batch','expert'}, use_global_device_ids=true, to_apply=%region_57.58.clone | all-reduce | flops 1024 | bytes 8192
  1005.3 15.3 %reduce-scatter.26.cloned.1.call-done = bf16[4,256,512]{2,1,0:T(8,128)(2,1)} async-done(((bf16[4,2048,512]{2,1,0:T(8,128)(2,1)}), bf16[4,256,512]{2,1,0:T(8,128)(2,1)}) %reduce-scatter.26.cloned.1.call-update) | async-done | bytes 1048592 | tf_op jit(solution)/shard_map/reduce_scatter | solution.py:288
  1023.5 72.2 %reduce-scatter.24.cloned.1.call-done = bf16[4,512,256]{2,1,0:T(8,128)(2,1)} async-done(((bf16[4,512,2048]{2,1,0:T(8,128)(2,1)}), bf16[4,512,256]{2,1,0:T(8,128)(2,1)}) %reduce-scatter.24.cloned.1.call-update) | async-done | bytes 1048592 | tf_op jit(solution)/shard_map/reduce_scatter | solution.py:285
  1098.4 133.6 %reduce-scatter.22.cloned.1.call-done = f32[16,16]{1,0:T(8,128)} async-done(((f32[512,16]{1,0:T(8,128)}), f32[16,16]{1,0:T(8,128)}) %reduce-scatter.22.cloned.1.call-update) | async-done | bytes 1040 | tf_op jit(solution)/shard_map/reduce_scatter | solution.py:295
  1232.0 134.7 %reduce-scatter.20.cloned.1.call-done = f32[16,512]{1,0:T(8,128)} async-done(((f32[512,512]{1,0:T(8,128)}), f32[16,512]{1,0:T(8,128)}) %reduce-scatter.20.cloned.1.call-update) | async-done | bytes 32784 | tf_op jit(solution)/shard_map/reduce_scatter | solution.py:294
  1366.7 104.5 %reduce-scatter.18.cloned.1.call-done = f32[16,1536]{1,0:T(8,128)} async-done(((f32[512,1536]{1,0:T(8,128)}), f32[16,1536]{1,0:T(8,128)}) %reduce-scatter.18.cloned.1.call-update) | async-done | bytes 98320 | tf_op jit(solution)/shard_map/reduce_scatter | solution.py:293
  (378 shorter events, 266.0 us)
Async XLA Ops:
  7.2 17.6 %copy-start.79 = (s32[2,3]{1,0:T(2,128)S(1)}, s32[2,3]{1,0:T(2,128)}, u32[]{:S(2)}) copy-start(s32[2,3]{1,0:T(2,128)} %param.20) | copy-start | bytes 76
  7.2 56.6 %all-gather.7.cloned.1.call-start = ((), (), s32[]{:S(2)}) async-start(), calls=%async_computation.26 | async-start | bytes 2621440 | tf_op jit(solution)/shard_map/all_gather | solution.py:107
  15.1 95.6 %all-gather.5.cloned.1.call-start = ((), (), s32[]{:S(2)}) async-start(), calls=%async_computation.25 | async-start | bytes 2621440 | tf_op jit(solution)/shard_map/all_gather | solution.py:108
  19.7 106.4 %all-to-all-start.8 = ((bf16[2,256,512]{2,0,1:T(2,128)(2,1)}), bf16[2,256,512]{2,0,1:T(2,128)(2,1)}, u32[]{:S(2)}, u32[]{:S(2)}) async-start(bf16[2,256,512]{2,0,1:T(2,128)(2,1)} %copy.594), calls=%async_computation.8 | async-start | bytes 1048576 | tf_op jit(solution)/shard_map/all_to_all | solution.py:165
  25.4 46.8 %copy-start.16 = (bf16[2,256,512]{1,2,0:T(8,128)(2,1)}, bf16[2,256,512]{1,2,0:T(8,128)(2,1)S(1)}, u32[]{:S(2)}) copy-start(bf16[2,256,512]{1,2,0:T(8,128)(2,1)S(1)} %copy.563) | copy-start | bytes 1572868
  77.9 45.5 %copy-start.49 = (f32[2,8,256]{2,1,0:T(8,128)}, f32[2,8,256]{2,1,0:T(8,128)S(1)}, u32[]{:S(2)}) copy-start(f32[2,8,256]{2,1,0:T(8,128)S(1)} %log_add_fusion.1) | copy-start | bytes 49156
  114.6 9.8 copy-start.54
  114.6 16.5 %copy-start.80 = (s32[2,16]{1,0:T(2,128)S(1)}, s32[2,16]{1,0:T(2,128)}, u32[]{:S(2)}) copy-start(s32[2,16]{1,0:T(2,128)} %param.21) | copy-start | bytes 388
  123.4 18.7 %copy-start.44 = (bf16[512,16]{0,1:T(8,128)(2,1)S(1)}, bf16[512,16]{0,1:T(8,128)(2,1)}, u32[]{:S(2)}) copy-start(bf16[512,16]{0,1:T(8,128)(2,1)} %param.15) | copy-start | bytes 49156
  124.2 19.3 %copy-start.59 = (f32[2,256]{1,0:T(2,128)}, f32[2,256]{1,0:T(2,128)S(1)}, u32[]{:S(2)}) copy-start(f32[2,256]{1,0:T(2,128)S(1)} %broadcast_multiply_fusion.8) | copy-start | bytes 6148
  124.5 19.0 %copy-start.67 = (f32[2,256]{1,0:T(2,128)}, f32[2,256]{1,0:T(2,128)S(1)}, u32[]{:S(2)}) copy-start(f32[2,256]{1,0:T(2,128)S(1)} %add_rsqrt_fusion.2) | copy-start | bytes 6148
  126.0 14.1 all-to-all-start
  130.5 13.0 copy-start.71
  130.6 13.8 copy-start.47
  131.7 11.8 copy-start.75
  150.7 66.7 %all-to-all-start.9 = ((bf16[32,3,16,512]{3,0,1,2:T(8,128)(2,1)}), bf16[32,3,16,512]{3,0,1,2:T(8,128)(2,1)}, u32[]{:S(2)}, u32[]{:S(2)}) async-start(bf16[32,3,16,512]{3,0,1,2:T(8,128)(2,1)} %copy.596), calls=%async_computation.9 | async-start | bytes 3145728 | tf_op jit(solution)/shard_map/all_to_all | solution.py:174
  155.0 187.0 %all-gather.11.cloned.1.call-start = ((), (), s32[]{:S(2)}) async-start(), calls=%async_computation.28 | async-start | bytes 2621440 | tf_op jit(solution)/shard_map/all_gather | solution.py:107
  217.4 61.1 %all-to-all-start.1 = ((bf16[32,3,16,512]{3,0,1,2:T(8,128)(2,1)}), bf16[32,3,16,512]{3,0,1,2:T(8,128)(2,1)}, u32[]{:S(2)}, u32[]{:S(2)}) async-start(bf16[32,3,16,512]{3,0,1,2:T(8,128)(2,1)} %copy.571), calls=%async_computation.1 | async-start | bytes 3145728 | tf_op jit(solution)/shard_map/all_to_all | solution.py:147
  221.7 124.2 %all-gather.9.cloned.1.call-start = ((), (), s32[]{:S(2)}) async-start(), calls=%async_computation.27 | async-start | bytes 2621440 | tf_op jit(solution)/shard_map/all_gather | solution.py:108
  294.3 38.5 %all-to-all-start.2 = ((bf16[128,3,4,512]{3,2,1,0:T(4,128)(2,1)}), bf16[128,3,4,512]{3,2,1,0:T(4,128)(2,1)}, u32[]{:S(2)}, u32[]{:S(2)}) async-start(bf16[128,3,4,512]{3,2,1,0:T(4,128)(2,1)} %copy.573), calls=%async_computation.2 | async-start | bytes 3145728 | tf_op jit(solution)/shard_map/all_to_all | solution.py:156
  332.8 41.3 %all-to-all-start.10 = ((bf16[128,3,4,512]{3,2,1,0:T(4,128)(2,1)}), bf16[128,3,4,512]{3,2,1,0:T(4,128)(2,1)}, u32[]{:S(2)}, u32[]{:S(2)}) async-start(bf16[128,3,4,512]{3,2,1,0:T(4,128)(2,1)} %copy.598), calls=%async_computation.10 | async-start | bytes 3145728 | tf_op jit(solution)/shard_map/all_to_all | solution.py:192
  374.1 34.8 %all-to-all-start.3 = ((bf16[16,32,512]{2,1,0:T(8,128)(2,1)}), bf16[16,32,512]{2,1,0:T(8,128)(2,1)}, u32[]{:S(2)}, u32[]{:S(2)}) async-start(bf16[16,32,512]{2,1,0:T(8,128)(2,1)} %copy.576), calls=%async_computation.3 | async-start | bytes 1048576 | tf_op jit(solution)/shard_map/all_to_all | solution.py:160
  408.9 16.2 %all-to-all-start.11 = ((bf16[16,32,512]{2,1,0:T(8,128)(2,1)}), bf16[16,32,512]{2,1,0:T(8,128)(2,1)}, u32[]{:S(2)}, u32[]{:S(2)}) async-start(bf16[16,32,512]{2,1,0:T(8,128)(2,1)} %copy.606), calls=%async_computation.11 | async-start | bytes 1048576 | tf_op jit(solution)/shard_map/all_to_all | solution.py:209
  413.1 16.4 %copy-start.55 = (f32[512]{0:T(512)S(1)}, f32[512]{0:T(512)}, u32[]{:S(2)}) copy-start(f32[512]{0:T(512)} %param.19) | copy-start | bytes 6148
  425.1 54.7 %all-to-all-start.12 = ((bf16[2,256,512]{2,0,1:T(2,128)(2,1)}), bf16[2,256,512]{2,0,1:T(2,128)(2,1)}, u32[]{:S(2)}, u32[]{:S(2)}) async-start(bf16[2,256,512]{2,0,1:T(2,128)(2,1)} %copy.614), calls=%async_computation.14 | async-start | bytes 1048576 | tf_op jit(solution)/shard_map/all_to_all | solution.py:165
  441.6 19.1 %copy-start.24 = (bf16[2,256,512]{1,2,0:T(8,128)(2,1)}, bf16[2,256,512]{1,2,0:T(8,128)(2,1)S(1)}, u32[]{:S(2)}) copy-start(bf16[2,256,512]{1,2,0:T(8,128)(2,1)S(1)} %copy.610) | copy-start | bytes 1572868
  468.9 9.3 copy-start.56
  468.9 15.4 %copy-start.70 = (pred[16,3]{0,1:T(4,128)(4,1)S(1)}, pred[16,3]{0,1:T(4,128)(4,1)}, u32[]{:S(2)}) copy-start(pred[16,3]{0,1:T(4,128)(4,1)} %get-tuple-element.60) | copy-start | bytes 148
  477.1 18.9 %copy-start.74 = (pred[16]{0:T(512)(128)(4,1)S(1)}, pred[16]{0:T(512)(128)(4,1)}, u32[]{:S(2)}) copy-start(pred[16]{0:T(512)(128)(4,1)} %get-tuple-element.53) | copy-start | bytes 52
  477.9 19.5 %copy-start.60 = (f32[2,256]{1,0:T(2,128)}, f32[2,256]{1,0:T(2,128)S(1)}, u32[]{:S(2)}) copy-start(f32[2,256]{1,0:T(2,128)S(1)} %broadcast_multiply_fusion.6) | copy-start | bytes 6148
  478.2 19.2 %copy-start.68 = (f32[2,256]{1,0:T(2,128)}, f32[2,256]{1,0:T(2,128)S(1)}, u32[]{:S(2)}) copy-start(f32[2,256]{1,0:T(2,128)S(1)} %add_rsqrt_fusion) | copy-start | bytes 6148
  479.8 14.3 all-to-all-start.4
  484.4 13.9 copy-start.48
  504.6 39.3 %all-to-all-start.13 = ((bf16[32,3,16,512]{3,0,1,2:T(8,128)(2,1)}), bf16[32,3,16,512]{3,0,1,2:T(8,128)(2,1)}, u32[]{:S(2)}, u32[]{:S(2)}) async-start(bf16[32,3,16,512]{3,0,1,2:T(8,128)(2,1)} %copy.616), calls=%async_computation.15 | async-start | bytes 3145728 | tf_op jit(solution)/shard_map/all_to_all | solution.py:174
  543.9 40.9 %all-to-all-start.5 = ((bf16[32,3,16,512]{3,0,1,2:T(8,128)(2,1)}), bf16[32,3,16,512]{3,0,1,2:T(8,128)(2,1)}, u32[]{:S(2)}, u32[]{:S(2)}) async-start(bf16[32,3,16,512]{3,0,1,2:T(8,128)(2,1)} %copy.587), calls=%async_computation.5 | async-start | bytes 3145728 | tf_op jit(solution)/shard_map/all_to_all | solution.py:147
  593.5 10.2 copy-start.13
  606.0 41.3 %all-to-all-start.6 = ((bf16[128,3,4,512]{3,2,1,0:T(4,128)(2,1)}), bf16[128,3,4,512]{3,2,1,0:T(4,128)(2,1)}, u32[]{:S(2)}, u32[]{:S(2)}) async-start(bf16[128,3,4,512]{3,2,1,0:T(4,128)(2,1)} %copy.589), calls=%async_computation.6 | async-start | bytes 3145728 | tf_op jit(solution)/shard_map/all_to_all | solution.py:156
  647.3 41.1 %all-to-all-start.14 = ((bf16[128,3,4,512]{3,2,1,0:T(4,128)(2,1)}), bf16[128,3,4,512]{3,2,1,0:T(4,128)(2,1)}, u32[]{:S(2)}, u32[]{:S(2)}) async-start(bf16[128,3,4,512]{3,2,1,0:T(4,128)(2,1)} %copy.618), calls=%async_computation.16 | async-start | bytes 3145728 | tf_op jit(solution)/shard_map/all_to_all | solution.py:192
  716.3 31.8 %copy-start.57 = (f32[512]{0:T(512)S(1)}, f32[512]{0:T(512)}, u32[]{:S(2)}) copy-start(f32[512]{0:T(512)} %param.19) | copy-start | bytes 6148
  716.3 31.8 %copy-start.61 = (f32[2,256]{1,0:T(2,128)S(1)}, f32[2,256]{1,0:T(2,128)}, u32[]{:S(2)}) copy-start(f32[2,256]{1,0:T(2,128)} %copy-done.60) | copy-start | bytes 6148
  716.3 31.8 %copy-start.69 = (f32[2,256]{1,0:T(2,128)S(1)}, f32[2,256]{1,0:T(2,128)}, u32[]{:S(2)}) copy-start(f32[2,256]{1,0:T(2,128)} %copy-done.68) | copy-start | bytes 6148
  717.4 14.3 all-to-all-start.15
  731.7 13.9 all-to-all-start.7
  735.9 185.2 %reduce-scatter.16.cloned.1.call-start = ((), (), s32[]{:S(2)}) async-start(), calls=%async_computation.32 | async-start | bytes 2621440 | tf_op jit(solution)/shard_map/reduce_scatter | solution.py:257
  753.0 13.8 copy-start.51
  753.0 13.8 copy-start.58
  766.3 154.8 %reduce-scatter.14.cloned.1.call-start = ((), (), s32[]{:S(2)}) async-start(), calls=%async_computation.31 | async-start | bytes 2621440 | tf_op jit(solution)/shard_map/reduce_scatter | solution.py:251
  793.4 12.4 copy-start.18
  813.6 13.9 copy-start.17
  813.6 112.0 %reduce-scatter.12.cloned.1.call-start = ((), (), s32[]{:S(2)}) async-start(), calls=%async_computation.30 | async-start | bytes 2621440 | tf_op jit(solution)/shard_map/reduce_scatter | solution.py:257
  827.5 118.4 %reduce-scatter.10.cloned.1.call-start = ((), (), s32[]{:S(2)}) async-start(), calls=%async_computation.29 | async-start | bytes 2621440 | tf_op jit(solution)/shard_map/reduce_scatter | solution.py:251
  837.9 12.0 copy-start.34
  837.9 182.8 %reduce-scatter.26.cloned.1.call-start = ((), (), s32[]{:S(2)}) async-start(), calls=%async_computation.37 | async-start | bytes 9437184 | tf_op jit(solution)/shard_map/reduce_scatter | solution.py:288
  864.9 13.9 copy-start.10
  864.9 230.8 %reduce-scatter.24.cloned.1.call-start = ((), (), s32[]{:S(2)}) async-start(), calls=%async_computation.36 | async-start | bytes 9437184 | tf_op jit(solution)/shard_map/reduce_scatter | solution.py:285
  890.9 341.1 %reduce-scatter.22.cloned.1.call-start = ((), (), s32[]{:S(2)}) async-start(), calls=%async_computation.35 | async-start | bytes 270336 | tf_op jit(solution)/shard_map/reduce_scatter | solution.py:295
  898.1 468.6 %reduce-scatter.20.cloned.1.call-start = ((), (), s32[]{:S(2)}) async-start(), calls=%async_computation.34 | async-start | bytes 1081344 | tf_op jit(solution)/shard_map/reduce_scatter | solution.py:294
  902.5 568.7 %reduce-scatter.18.cloned.1.call-start = ((), (), s32[]{:S(2)}) async-start(), calls=%async_computation.33 | async-start | bytes 3244032 | tf_op jit(solution)/shard_map/reduce_scatter | solution.py:293
  910.2 10.9 copy-start.64
  910.2 10.9 copy-start.73
  910.2 10.9 copy-start.78
  911.5 34.4 %copy-start.63 = (f32[2,256]{1,0:T(2,128)S(1)}, f32[2,256]{1,0:T(2,128)}, u32[]{:S(2)}) copy-start(f32[2,256]{1,0:T(2,128)} %copy-done.62) | copy-start | bytes 6148
  911.5 34.4 %copy-start.66 = (f32[2,256]{1,0:T(2,128)S(1)}, f32[2,256]{1,0:T(2,128)}, u32[]{:S(2)}) copy-start(f32[2,256]{1,0:T(2,128)} %copy-done.65) | copy-start | bytes 6148
  921.1 30.3 %copy-start.76 = (f32[512]{0:T(512)S(1)}, f32[512]{0:T(512)}, u32[]{:S(2)}) copy-start(f32[512]{0:T(512)} %get-tuple-element.15) | copy-start | bytes 6148
  (48 other events, 191.8 us)
Sparse Core Ops, SparseCore 0:
  15.2 48.5 all-gather.6
  65.9 44.7 all-gather.4
  159.4 79.2 all-gather.10
  240.1 51.6 all-gather.8
  766.5 41.0 reduce-scatter.15
  813.8 41.0 reduce-scatter.13
  857.1 43.1 reduce-scatter.11
  902.7 43.1 reduce-scatter.9
  949.4 71.1 reduce-scatter.25
  1024.3 71.2 reduce-scatter.23
  1098.5 133.4 reduce-scatter.21
  1234.7 131.9 reduce-scatter.19
  1372.7 98.4 reduce-scatter.17
where the time goes:
time: 1490 us; the launch traced here: 1480 us
  waiting for transfers between devices  808 us (54%)
  matrix products  309 us (21%)
  local copies, waits for them, and re-layouts  148 us (10%)
  other arithmetic  80.6 us (5%)
  starting transfers between devices  77.4 us (5%)
  blocking collectives  40.1 us (3%)
  between operations  15.6 us (1%)
    reduce_scatter x1, waiting for transfers between devices, body(): lax.psum_scatter(sum_out, ('batch', 'expert'), scatter_dimension=0, tiled...  135 us
    reduce_scatter x1, waiting for transfers between devices, body(): lax.psum_scatter(sum_ctrl, ('batch', 'expert'), scatter_dimension=0, tile...  134 us
    reduce_scatter x1, waiting for transfers between devices, body(): lax.psum_scatter(sum_qkv, ('batch', 'expert'), scatter_dimension=0, tiled...  104 us
    all_to_all x2, waiting for transfers between devices, body(): lax.all_to_all(blended_rows, 'expert', split_axis=2, concat_axis=0, tiled...  87.2 us
    all_to_all x2, waiting for transfers between devices, body(): lax.all_to_all(grad_eout, 'expert', split_axis=2, concat_axis=0, tiled=True)  85.7 us
    reduce_scatter x1, waiting for transfers between devices, body(): lax.psum_scatter(sum_first.astype(jnp.bfloat16), 'batch', scatter_dimensi...  72.2 us
    dot_general x2, matrix products, body(): jnp.einsum('sqhc,skhc->shqk', context_heads, value_heads, preferred_eleme...  45.6 us
    all_to_all x2, waiting for transfers between devices, body(): lax.all_to_all(grad_mixed, 'expert', split_axis=0, concat_axis=2, tiled=T...  41 us
  transfers between devices with their start and end apart: 29, of which 20 were waited for; matrix products, arithmetic and copies ran while one was open for 29% of the time, Pallas kernels for 0%

commit v1 on v0

--- a/solution.py
+++ b/solution.py
@@ -3,6 +3,8 @@
 import jax
 import jax.numpy as jnp
 from jax import lax
+from jax.experimental import pallas as pl
+from jax.experimental.pallas import tpu as pltpu
 from jax.sharding import PartitionSpec as P
 
 HEADS = 8
@@ -59,7 +61,7 @@
     return jnp.where(causal, jnp.exp(scores - logsum), 0.0)
 
 
-def body(
+def body_by_position(
     tokens,
     cotangent,
     query_key_value_weight,
@@ -309,6 +311,581 @@
     )
 
 
+F32 = jnp.float32
+BF16 = jnp.bfloat16
+PB = 16
+CHUNKS = 2
+VMEM_LIMIT = 60 * 1024 * 1024
+
+
+def dot_nn(a, b):
+    return lax.dot_general(a, b, (((1,), (0,)), ((), ())), preferred_element_type=F32)
+
+
+def dot_nt(a, b):
+    return lax.dot_general(a, b, (((1,), (1,)), ((), ())), preferred_element_type=F32)
+
+
+def dot_tn(a, b):
+    return lax.dot_general(a, b, (((0,), (0,)), ((), ())), preferred_element_type=F32)
+
+
+def row_norm(rows):
+    centred = rows - jnp.mean(rows, -1, keepdims=True)
+    inverse = lax.rsqrt(jnp.mean(centred * centred, -1, keepdims=True) + 1e-05)
+    return centred * inverse, inverse
+
+
+def row_norm_back(incoming, normed, inverse, gain):
+    scaled = incoming * gain
+    return inverse * (
+        scaled
+        - jnp.mean(scaled, -1, keepdims=True)
+        - normed * jnp.mean(scaled * normed, -1, keepdims=True)
+    )
+
+
+def head_lanes(rows, lanes, head):
+    lane = lax.broadcasted_iota(jnp.int32, (rows, lanes), 1)
+    return (lane < lanes // 2) if head == 0 else (lane >= lanes // 2)
+
+
+def causal_tile(size):
+    key = lax.broadcasted_iota(jnp.int32, (size, size), 0)
+    query = lax.broadcasted_iota(jnp.int32, (size, size), 1)
+    return key <= query
+
+
+def attention_forward_kernel(x_ref, wqkv_ref, wo_ref, g1_ref, g2_ref,
+                             qkv_ref, lse_ref, ctx_ref, attn_ref, mix_ref, ctx_pairs):
+    length, width = x_ref.shape
+    pairs = HEADS // 2
+    lanes = width // pairs
+    half = lanes // 2
+    nb, quarters, piece, _ = mix_ref.shape
+    tile = length // quarters
+    factor = half ** (-0.5)
+
+    def project(i, carry):
+        rows = pl.ds(pl.multiple_of(i * tile, tile), tile)
+        normed, _ = row_norm(x_ref[rows, :].astype(F32))
+        attn_in = (normed * g1_ref[...]).astype(BF16)
+        for part in range(3):
+            out = dot_nn(attn_in, wqkv_ref[:, part * width:(part + 1) * width]).astype(BF16)
+            for p in range(pairs):
+                qkv_ref[part * pairs + p, rows, :] = out[:, p * lanes:(p + 1) * lanes]
+        return carry
+
+    lax.fori_loop(0, quarters, project, 0)
+
+    def attend(p, carry):
+        values_t = qkv_ref[2 * pairs + p].T
+        for j in range(quarters):
+            seen = (j + 1) * tile
+            queries = qkv_ref[p, j * tile:seen, :] * jnp.asarray(factor, BF16)
+            outs = []
+            for h in range(2):
+                masked = jnp.where(head_lanes(tile, lanes, h), queries, jnp.zeros((), BF16))
+                scores = dot_nt(qkv_ref[pairs + p, :seen, :], masked)
+                last = jnp.where(causal_tile(tile), scores[j * tile:], NEG_FILL)
+                scores = jnp.concatenate([scores[:j * tile], last], 0) if j else last
+                high = jnp.max(scores, 0, keepdims=True)
+                weights = jnp.exp(scores - high)
+                total = jnp.sum(weights, 0, keepdims=True)
+                out = dot_nn(values_t[h * half:(h + 1) * half, :seen], weights.astype(BF16))
+                outs.append(out / total)
+                lse_ref[2 * p + h, :, j * tile:seen] = high + jnp.log(total)
+            ctx_pairs[p, j * tile:seen, :] = jnp.concatenate(outs, 0).T.astype(BF16)
+        return carry
+
+    lax.fori_loop(0, pairs, attend, 0)
+
+    def finish(i, carry):
+        rows = pl.ds(pl.multiple_of(i * tile, tile), tile)
+        context = jnp.concatenate([ctx_pairs[p, rows, :] for p in range(pairs)], -1)
+        ctx_ref[rows, :] = context
+        attn = dot_nn(context, wo_ref[...])
+        attn_ref[rows, :] = attn
+        normed, _ = row_norm(x_ref[rows, :].astype(F32) + attn)
+        mix = (normed * g2_ref[...]).astype(BF16)
+        for b in range(nb):
+            mix_ref[b, i, :, :] = mix[b * piece:(b + 1) * piece]
+        return carry
+
+    lax.fori_loop(0, quarters, finish, 0)
+
+
+def attention_forward(x, wqkv, wo, g1, g2, nb, quarters):
+    length, width = x.shape
+    pairs = HEADS // 2
+    lanes = width // pairs
+    return pl.pallas_call(
+        attention_forward_kernel,
+        out_shape=(
+            jax.ShapeDtypeStruct((3 * pairs, length, lanes), BF16),
+            jax.ShapeDtypeStruct((HEADS, 1, length), F32),
+            jax.ShapeDtypeStruct((length, width), BF16),
+            jax.ShapeDtypeStruct((length, width), F32),
+            jax.ShapeDtypeStruct((nb, quarters, length // quarters // nb, width), BF16),
+        ),
+        scratch_shapes=[pltpu.VMEM((pairs, length, lanes), BF16)],
+        compiler_params=pltpu.CompilerParams(vmem_limit_bytes=VMEM_LIMIT),
+        cost_estimate=pl.CostEstimate(flops=15_000_000_000, bytes_accessed=12_000_000, transcendentals=5_000_000),
+        name="attention_forward",
+    )(x, wqkv, wo, g1, g2)
+
+
+def attention_backward_kernel(gm_ref, cot_ref, x_ref, attn_ref, ctx_ref, qkv_ref, lse_ref,
+                              wqkv_ref, wo_ref, g1_ref, g2_ref,
+                              gin_ref, dqkv_ref, dwo_ref, dg1_ref, dg2_ref,
+                              delta, ga_rows, dctx, gqkv, attn_in, dk_sum, dv_sum):
+    length, width = x_ref.shape
+    pairs = HEADS // 2
+    lanes = width // pairs
+    half = lanes // 2
+    nb, quarters, piece, _ = gm_ref.shape
+    tile = length // quarters
+    factor = half ** (-0.5)
+    dg2_ref[...] = jnp.zeros_like(dg2_ref)
+    dg1_ref[...] = jnp.zeros_like(dg1_ref)
+
+    def first(i, carry):
+        rows = pl.ds(pl.multiple_of(i * tile, tile), tile)
+        normed, inverse = row_norm(x_ref[rows, :].astype(F32) + attn_ref[rows, :])
+        grad = jnp.concatenate([gm_ref[b, i] for b in range(nb)], 0).astype(F32)
+        dg2_ref[...] += jnp.sum(grad * normed, 0, keepdims=True)
+        back = row_norm_back(grad, normed, inverse, g2_ref[...])
+        delta[rows, :] = back
+        cot = jnp.concatenate([cot_ref[b, i] for b in range(nb)], 0).astype(F32)
+        grad_attn = (cot + back).astype(BF16)
+        ga_rows[rows, :] = grad_attn
+        grad_ctx = dot_nt(grad_attn, wo_ref[...]).astype(BF16)
+        for p in range(pairs):
+            dctx[p, rows, :] = grad_ctx[:, p * lanes:(p + 1) * lanes]
+        return carry
+
+    lax.fori_loop(0, quarters, first, 0)
+
+    dwo_ref[...] = dot_tn(ctx_ref[...], ga_rows[...])
+
+    def attend(p, carry):
+        lane0 = pl.multiple_of(p * lanes, lanes)
+        keys_t = qkv_ref[pairs + p].T
+        dk_sum[...] = jnp.zeros_like(dk_sum)
+        dv_sum[...] = jnp.zeros_like(dv_sum)
+        for j in range(quarters):
+            seen = (j + 1) * tile
+            queries = qkv_ref[p, j * tile:seen, :] * jnp.asarray(factor, BF16)
+            grads = dctx[p, j * tile:seen, :]
+            context = ctx_ref[j * tile:seen, pl.ds(lane0, lanes)]
+            products = (grads.astype(F32) * context.astype(F32)).T
+            outs = []
+            for h in range(2):
+                inside = head_lanes(tile, lanes, h)
+                q_masked = jnp.where(inside, queries, jnp.zeros((), BF16))
+                g_masked = jnp.where(inside, grads, jnp.zeros((), BF16))
+                dots = jnp.sum(products[h * half:(h + 1) * half], 0, keepdims=True)
+                scores = dot_nt(qkv_ref[pairs + p, :seen, :], q_masked)
+                probs = jnp.exp(scores - lse_ref[2 * p + h, :, j * tile:seen])
+                last = jnp.where(causal_tile(tile), probs[j * tile:], 0.0)
+                probs = jnp.concatenate([probs[:j * tile], last], 0) if j else last
+                grad_probs = dot_nt(qkv_ref[2 * pairs + p, :seen, :], g_masked)
+                grad_scores = (probs * (grad_probs - dots)).astype(BF16)
+                dv_sum[:seen, :] += dot_nn(probs.astype(BF16), g_masked)
+                dk_sum[:seen, :] += dot_nn(grad_scores, q_masked)
+                outs.append(dot_nn(keys_t[h * half:(h + 1) * half, :seen], grad_scores))
+            gqkv[p, j * tile:seen, :] = (jnp.concatenate(outs, 0).T * factor).astype(BF16)
+        gqkv[pairs + p] = dk_sum[...].astype(BF16)
+        gqkv[2 * pairs + p] = dv_sum[...].astype(BF16)
+        return carry
+
+    lax.fori_loop(0, pairs, attend, 0)
+
+    def last(i, carry):
+        rows = pl.ds(pl.multiple_of(i * tile, tile), tile)
+        normed, inverse = row_norm(x_ref[rows, :].astype(F32))
+        attn_in[rows, :] = (normed * g1_ref[...]).astype(BF16)
+        grads = jnp.concatenate([gqkv[c, rows, :] for c in range(3 * pairs)], -1)
+        grad = dot_nt(grads, wqkv_ref[...])
+        dg1_ref[...] += jnp.sum(grad * normed, 0, keepdims=True)
+        gin_ref[rows, :] = (delta[rows, :] + row_norm_back(grad, normed, inverse, g1_ref[...])).astype(BF16)
+        return carry
+
+    lax.fori_loop(0, quarters, last, 0)
+
+    for c in range(3):
+        grads = jnp.concatenate([gqkv[c * pairs + p] for p in range(pairs)], -1)
+        dqkv_ref[:, c * width:(c + 1) * width] = dot_tn(attn_in[...], grads)
+
+
+def attention_backward(gm, cot, x, attn, ctx, qkv, lse, wqkv, wo, g1, g2):
+    length, width = x.shape
+    pairs = HEADS // 2
+    lanes = width // pairs
+    return pl.pallas_call(
+        attention_backward_kernel,
+        out_shape=(
+            jax.ShapeDtypeStruct((length, width), BF16),
+            jax.ShapeDtypeStruct((width, 3 * width), F32),
+            jax.ShapeDtypeStruct((width, width), F32),
+            jax.ShapeDtypeStruct((1, width), F32),
+            jax.ShapeDtypeStruct((1, width), F32),
+        ),
+        scratch_shapes=[
+            pltpu.VMEM((length, width), F32),
+            pltpu.VMEM((length, width), BF16),
+            pltpu.VMEM((pairs, length, lanes), BF16),
+            pltpu.VMEM((3 * pairs, length, lanes), BF16),
+            pltpu.VMEM((length, width), BF16),
+            pltpu.VMEM((length, lanes), F32),
+            pltpu.VMEM((length, lanes), F32),
+        ],
+        compiler_params=pltpu.CompilerParams(vmem_limit_bytes=VMEM_LIMIT),
+        cost_estimate=pl.CostEstimate(flops=35_000_000_000, bytes_accessed=20_000_000, transcendentals=5_000_000),
+        name="attention_backward",
+    )(gm, cot, x, attn, ctx, qkv, lse, wqkv, wo, g1, g2)
+
+
+def group_reduce(rows, mem, op, fill):
+    result = jnp.zeros_like(rows)
+    for k in range(mem.shape[0]):
+        inside = mem[k:k + 1, :] > 0
+        part = jnp.where(inside, rows, fill)
+        shift = rows.shape[1] // 2
+        while shift >= PB:
+            part = op(part, pltpu.roll(part, shift, 1))
+            shift //= 2
+        result = jnp.where(inside, part, result)
+    return result
+
+
+def gelu_both(v):
+    square = v * v
+    tanh = jnp.tanh(0.7978845608028654 * v * (1.0 + 0.044715 * square))
+    half = 0.5 * (1.0 + tanh)
+    slope = half + v * (1.0 - tanh * tanh) * (0.3989422804014327 + 0.0535161223274472 * square)
+    return v * half, slope
+
+
+def moe_kernel(chunk, z_ref, *refs):
+    n = 4
+    xs_in, gs_in = refs[:n], refs[n:2 * n]
+    (ctrl_ref, mem_ref, mkl_ref, take_ref, w1_ref, w2_ref,
+     spread_ref, gm_ref, mixed_ref, geo_ref, hid_ref, gpre_ref, dctrl_ref,
+     xs, gs, logits, gates, weights, eo, gmx, sems) = refs[2 * n:]
+    planes, nb, quarters, piece, width = xs.shape
+    micro = mem_ref.shape[0]
+    sl = planes // micro
+    lanes = mem_ref.shape[2]
+    experts = mixed_ref.shape[0]
+    rows = mkl_ref.shape[1]
+    halves = piece // PB
+    per_micro = quarters * halves
+    e = pl.program_id(0)
+
+    def x_block(m, q, h):
+        at = pl.ds(pl.multiple_of(h * PB, PB), PB)
+        return jnp.concatenate(
+            [xs[m * sl + s, :, q, at, :].reshape(nb * PB, width) for s in range(sl)], 0)
+
+    def g_block(m, q, h):
+        at = pl.ds(pl.multiple_of(h * PB, PB), PB)
+        return jnp.concatenate(
+            [gs[q, :, m * sl + s, at, :].reshape(nb * PB, width) for s in range(sl)], 0)
+
+    def store_block(ref, m, q, h, value):
+        at = pl.ds(pl.multiple_of(h * PB, PB), PB)
+        for s in range(sl):
+            part = value[s * nb * PB:(s + 1) * nb * PB].reshape(nb, PB, width)
+            ref[m * sl + s, :, q, at, :] = part
+
+    @pl.when(e == 0)
+    def _():
+        z = z_ref[0]
+        for k in range(n):
+            source = lax.rem(z - k + n, n)
+            pltpu.make_async_copy(xs_in[k], xs.at[source], sems.at[k]).start()
+        for k in range(n):
+            source = lax.rem(z - k + n, n)
+
+            @pl.when(source // quarters == chunk)
+            def _():
+                slot = gs.at[lax.rem(source, quarters)]
+                pltpu.make_async_copy(gs_in[k], slot, sems.at[n + k]).start()
+
+        for k in range(n):
+            source = lax.rem(z - k + n, n)
+            pltpu.make_async_copy(xs_in[k], xs.at[source], sems.at[k]).wait()
+
+        for m in range(micro):
+            def score(i, carry):
+                block = x_block(m, i // halves, lax.rem(i, halves))
+                at = pl.ds(pl.multiple_of(i * 8, 8), 8)
+                logits[m, at, :] = dot_nt(ctrl_ref[...], block)[:8]
+                return carry
+
+            lax.fori_loop(0, per_micro, score, 0)
+            mem = mem_ref[m]
+            taking = take_ref[m] > 0
+            values = logits[m]
+            high = group_reduce(jnp.where(taking, values, NEG_FILL), mem, jnp.maximum, NEG_FILL)
+            scaled = jnp.where(taking, jnp.exp(values - high), 0.0)
+            gates[m] = scaled / group_reduce(scaled, mem, jnp.add, 0.0)
+
+        for k in range(n):
+            source = lax.rem(z - k + n, n)
+
+            @pl.when(source // quarters == chunk)
+            def _():
+                slot = gs.at[lax.rem(source, quarters)]
+                pltpu.make_async_copy(gs_in[k], slot, sems.at[n + k]).wait()
+
+        for m in range(micro):
+            def blend(i, carry):
+                q, h = i // halves, lax.rem(i, halves)
+                block = m * per_micro + i
+                own = gates[m, pl.ds(pl.multiple_of(i * 8, 8), 8), :]
+                w = jnp.concatenate(
+                    [(mkl_ref[m] * own[j:j + 1, :]).astype(BF16) for j in range(experts)], 0)
+                weights[block] = w
+                blended = dot_nn(w, x_block(m, q, h)).astype(BF16)
+                grads = dot_nn(w, g_block(m, q, h)).astype(BF16)
+                at = pl.ds(pl.multiple_of(block * rows, rows), rows)
+                for j in range(experts):
+                    mixed_ref[j, at, :] = blended[j * rows:(j + 1) * rows]
+                    geo_ref[j, at, :] = grads[j * rows:(j + 1) * rows]
+                return carry
+
+            lax.fori_loop(0, per_micro, blend, 0)
+
+    hidden_size = w1_ref.shape[2]
+    step = 512
+    blended, grads = mixed_ref[e], geo_ref[e]
+    out_sum = jnp.zeros(blended.shape, F32)
+    back_sum = jnp.zeros(blended.shape, F32)
+    for f in range(0, hidden_size, step):
+        first, second = w1_ref[0, :, f:f + step], w2_ref[0, f:f + step, :]
+        value, slope = gelu_both(dot_nn(blended, first))
+        hidden = value.astype(BF16)
+        hid_ref[0, :, f:f + step] = hidden
+        out_sum += dot_nn(hidden, second)
+        grad_pre = (dot_nt(grads, second) * slope).astype(BF16)
+        gpre_ref[0, :, f:f + step] = grad_pre
+        back_sum += dot_nt(grad_pre, first)
+    eo[e] = out_sum.astype(BF16)
+    gmx[e] = back_sum.astype(BF16)
+
+    @pl.when(e == experts - 1)
+    def _():
+        dctrl_ref[...] = jnp.zeros_like(dctrl_ref)
+        ctrl8 = ctrl_ref[:8, :]
+        ctrl_twice = jnp.concatenate([ctrl8.astype(F32), ctrl8.astype(F32)], 0).astype(BF16)
+        for m in range(micro):
+            def spread_out(i, carry):
+                q, h = i // halves, lax.rem(i, halves)
+                block = m * per_micro + i
+                at = pl.ds(pl.multiple_of(block * rows, rows), rows)
+                outs = jnp.concatenate([eo[j, at, :] for j in range(experts)], 0)
+                backs = jnp.concatenate([gmx[j, at, :] for j in range(experts)], 0)
+                w = weights[block]
+                x_rows, g_rows = x_block(m, q, h), g_block(m, q, h)
+                store_block(spread_ref, m, q, h, dot_tn(w, outs).astype(BF16))
+                dots = dot_nt(outs, g_rows) + dot_nt(backs, x_rows)
+                grad_gates = [
+                    jnp.sum(dots[j * rows:(j + 1) * rows] * mkl_ref[m], 0, keepdims=True)
+                    for j in range(experts)]
+                if experts < 8:
+                    grad_gates.append(jnp.zeros((8 - experts, lanes), F32))
+                grad_gates = jnp.concatenate(grad_gates, 0)
+                own = gates[m, pl.ds(pl.multiple_of(i * 8, 8), 8), :]
+                inner = group_reduce(own * grad_gates, mem_ref[m], jnp.add, 0.0)
+                grad_logits = own * (grad_gates - inner)
+                upper = grad_logits.astype(BF16).astype(F32)
+                both = jnp.concatenate([upper, grad_logits - upper], 0).astype(BF16)
+                grad_mix = dot_tn(w, backs) + dot_tn(both, ctrl_twice)
+                store_block(gm_ref, m, q, h, grad_mix.astype(BF16))
+                dctrl_ref[...] += dot_nn(both, x_rows)
+                return carry
+
+            lax.fori_loop(0, per_micro, spread_out, 0)
+
+
+def moe(chunk, z, x_parts, g_parts, ctrl, mem, mkl, take, w1, w2):
+    planes = len(x_parts)
+    nb, quarters, piece, width = x_parts[0].shape
+    micro, groups, lanes = mem.shape
+    experts, _, hidden_size = w1.shape
+    rows = mkl.shape[1]
+    blocks = micro * quarters * (piece // PB)
+    total = blocks * rows
+    whole = lambda shape: pl.BlockSpec(shape, lambda e: (0,) * len(shape))
+    back_shape = (planes, nb, quarters, piece, width)
+    any_spec = pl.BlockSpec(memory_space=pl.ANY)
+    flops = experts * total * width * hidden_size * 8 + 4_000_000_000
+    return pl.pallas_call(
+        functools.partial(moe_kernel, chunk),
+        grid=(experts,),
+        out_shape=(
+            jax.ShapeDtypeStruct(back_shape, BF16),
+            jax.ShapeDtypeStruct(back_shape, BF16),
+            jax.ShapeDtypeStruct((experts, total, width), BF16),
+            jax.ShapeDtypeStruct((experts, total, width), BF16),
+            jax.ShapeDtypeStruct((experts, total, hidden_size), BF16),
+            jax.ShapeDtypeStruct((experts, total, hidden_size), BF16),
+            jax.ShapeDtypeStruct((16, width), F32),
+        ),
+        in_specs=[pl.BlockSpec(memory_space=pltpu.SMEM)] + [any_spec] * (2 * planes) + [
+            whole(ctrl.shape), whole(mem.shape), whole(mkl.shape), whole(take.shape),
+            pl.BlockSpec((1, width, hidden_size), lambda e: (e, 0, 0)),
+            pl.BlockSpec((1, hidden_size, width), lambda e: (e, 0, 0)),
+        ],
+        out_specs=(
+            whole(back_shape), whole(back_shape),
+            whole((experts, total, width)), whole((experts, total, width)),
+            pl.BlockSpec((1, total, hidden_size), lambda e: (e, 0, 0)),
+            pl.BlockSpec((1, total, hidden_size), lambda e: (e, 0, 0)),
+            whole((16, width)),
+        ),
+        scratch_shapes=[
+            pltpu.VMEM(back_shape, BF16),
+            pltpu.VMEM((quarters, nb, planes, piece, width), BF16),
+            pltpu.VMEM((micro, blocks // micro * 8, lanes), F32),
+            pltpu.VMEM((micro, blocks // micro * 8, lanes), F32),
+            pltpu.VMEM((blocks, experts * rows, lanes), BF16),
+            pltpu.VMEM((experts, total, width), BF16),
+            pltpu.VMEM((experts, total, width), BF16),
+            pltpu.SemaphoreType.DMA((2 * planes,)),
+        ],
+        compiler_params=pltpu.CompilerParams(vmem_limit_bytes=VMEM_LIMIT),
+        cost_estimate=pl.CostEstimate(flops=flops, bytes_accessed=50_000_000, transcendentals=experts * total * hidden_size),
+        name="mixture",
+    )(z, *x_parts, *g_parts, ctrl, mem, mkl, take, w1, w2)
+
+
+def ring(count):
+    return [(i, (i + 1) % count) for i in range(count)]
+
+
+def ring_gather(block, count):
+    parts = [block]
+    for _ in range(count - 1):
+        parts.append(lax.ppermute(parts[-1], "expert", ring(count)))
+    return parts
+
+
+def ring_scatter(parts, z, count):
+    def own(step):
+        return lax.dynamic_index_in_dim(parts, lax.rem(z - step + 2 * count, count), 0, keepdims=False)
+
+    held = own(1)
+    for step in range(1, count):
+        held = lax.ppermute(held, "expert", ring(count))
+        held = (held.astype(F32) + own(step + 1).astype(F32)).astype(BF16)
+    return held
+
+
+def body(
+    tokens,
+    cotangent,
+    query_key_value_weight,
+    output_weight,
+    controller_weight,
+    w_first,
+    w_second,
+    gain_one,
+    gain_two,
+    group_sizes,
+    live,
+):
+    micro, sl, local_len, width = tokens.shape
+    planes = lax.axis_size("expert")
+    nb = lax.axis_size("batch")
+    experts = w_first.shape[0]
+    seqs = live.shape[1]
+    z = lax.axis_index("expert")
+    piece = local_len // nb
+    if micro * sl != planes or piece % PB:
+        return body_by_position(
+            tokens, cotangent, query_key_value_weight, output_weight, controller_weight,
+            w_first, w_second, gain_one, gain_two, group_sizes, live)
+    g1, g2 = gain_one.reshape(1, width), gain_two.reshape(1, width)
+
+    sent = tokens.astype(BF16).reshape(planes, local_len, width)
+    x = lax.all_to_all(sent, "expert", split_axis=0, concat_axis=0, tiled=True)
+    x = x.reshape(planes * local_len, width)
+
+    cot = cotangent.astype(BF16).reshape(planes, nb, piece, width).transpose(1, 0, 2, 3)
+    cot = lax.all_to_all(cot, "batch", split_axis=0, concat_axis=0, tiled=True)
+    cot_parts = ring_gather(cot, planes)
+
+    qkv, lse, ctx, attn, mix = attention_forward(
+        x, query_key_value_weight, output_weight, g1, g2, nb, planes)
+
+    member, taking = jax.vmap(group_tables)(group_sizes, live)
+    groups = member.shape[2]
+    mem = member.reshape(micro, nb, sl, groups).transpose(0, 3, 2, 1).reshape(micro, groups, seqs)
+    mem = jnp.repeat(mem.astype(F32), PB, axis=2)
+    take = taking.reshape(micro, nb, sl).transpose(0, 2, 1).reshape(micro, 1, seqs)
+    take = jnp.repeat(take.astype(F32), PB, axis=2)
+    place = jnp.arange(seqs * PB, dtype=jnp.int32) % PB
+    same = (jnp.arange(PB, dtype=jnp.int32)[:, None] == place[None, :]).astype(F32)
+    mkl = (mem[:, :, None, :] * same).reshape(micro, groups * PB, seqs * PB)
+    ctrl = lax.dynamic_slice_in_dim(controller_weight, z * experts, experts, 1).T
+    ctrl = jnp.pad(ctrl, ((0, 16 - experts), (0, 0)))
+    z_arr = z.astype(jnp.int32).reshape(1)
+
+    quarters = planes // CHUNKS
+    spreads, backs, kept, dctrl = [], [], [], 0.0
+    for c in range(CHUNKS):
+        own = lax.all_to_all(
+            mix[:, c * quarters:(c + 1) * quarters], "batch", split_axis=0, concat_axis=0, tiled=True)
+        x_parts = ring_gather(own, planes)
+        spread, back, mixed, geo, hid, gpre, dc = moe(
+            c, z_arr, x_parts, cot_parts, ctrl, mem, mkl, take, w_first, w_second)
+        back = ring_scatter(back, z, planes)
+        backs.append(lax.all_to_all(back, "batch", split_axis=0, concat_axis=0, tiled=True))
+        spread = ring_scatter(spread, z, planes)
+        spreads.append(lax.all_to_all(spread, "batch", split_axis=0, concat_axis=0, tiled=True))
+        kept.append((mixed, geo, hid, gpre))
+        dctrl = dctrl + dc[:8] + dc[8:]
+    back = jnp.concatenate(backs, 1)
+    spread = jnp.concatenate(spreads, 1)
+
+    mixed, geo, hid, gpre = [jnp.concatenate(parts, 1) for parts in zip(*kept)]
+    sum_first = jnp.einsum("erd,erf->edf", mixed, gpre, preferred_element_type=F32).astype(BF16)
+    sum_second = jnp.einsum("erf,erd->efd", hid, geo, preferred_element_type=F32).astype(BF16)
+    grad_first = lax.psum_scatter(sum_first, "batch", scatter_dimension=2, tiled=True).astype(F32)
+    grad_second = lax.psum_scatter(sum_second, "batch", scatter_dimension=1, tiled=True).astype(F32)
+
+    cot_all = jnp.stack(cot_parts)
+    order = lax.rem(z - jnp.arange(planes) + planes, planes)
+    cot_own = lax.dynamic_index_in_dim(cot_all, z, 2, keepdims=False)
+    cot_own = jnp.take(cot_own, order, axis=0).transpose(1, 0, 2, 3)
+    cot_own = lax.all_to_all(cot_own, "batch", split_axis=0, concat_axis=0, tiled=True)
+
+    gin, dqkv, dwo, dg1, dg2 = attention_backward(
+        back, cot_own, x, attn, ctx, qkv, lse, query_key_value_weight, output_weight, g1, g2)
+
+    spread = spread.transpose(1, 0, 2, 3).reshape(planes, local_len, width)
+    out = (attn.reshape(planes, local_len, width) + spread.astype(F32)).astype(BF16)
+    out = lax.all_to_all(out, "expert", split_axis=0, concat_axis=0, tiled=True)
+    out = tokens + out.reshape(tokens.shape).astype(F32)
+    gin = lax.all_to_all(
+        gin.reshape(planes, local_len, width), "expert", split_axis=0, concat_axis=0, tiled=True)
+    grad_in = cotangent + gin.reshape(tokens.shape).astype(F32)
+
+    dctrl_all = jnp.zeros((planes, experts, width), F32)
+    dctrl_all = lax.dynamic_update_slice(dctrl_all, dctrl[None, :experts], (z, 0, 0))
+    dctrl_all = dctrl_all.reshape(planes * experts, width).T
+    axes = ("batch", "expert")
+    flat = jnp.concatenate([dqkv, dwo, dctrl_all, dg1.T, dg2.T], 1)
+    flat = lax.psum_scatter(flat, axes, scatter_dimension=0, tiled=True)
+    ends = [3 * width, 4 * width, 4 * width + planes * experts]
+    grad_qkv, grad_out, grad_ctrl = flat[:, :ends[0]], flat[:, ends[0]:ends[1]], flat[:, ends[1]:ends[2]]
+    return (out, grad_in, grad_qkv, grad_out, grad_ctrl, grad_first, grad_second,
+            flat[:, ends[2]], flat[:, ends[2] + 1])
+
+
 def solution(mesh):
     placed = (
         P(None, "batch", "expert", None),

time: 1490 us -> 791 us (0.53)
  waiting for transfers between devices: 808 us -> 440 us
  matrix products: 309 us -> 25.5 us
  Pallas kernels: 0 us -> 134 us
  local copies, waits for them, and re-layouts: 148 us -> 30 us
  other arithmetic: 80.6 us -> 41.3 us
  starting transfers between devices: 77.4 us -> 38.4 us
  blocking collectives: 40.1 us -> 57.4 us
    reduce_scatter x9 -> x3, waiting for transfers between devices: 481 us -> 78.2 us  [the longest x1 72.1 us: body(): lax.psum_scatter(sum_second, 'batch', scatter_dimension=1, tiled=True)]
    dot_general x54 -> x2, matrix products: 309 us -> 25.5 us  [the longest x1 12.8 us: body(): jnp.einsum('erd,erf->edf', mixed, gpre, preferred_element_type=F32)]
    ppermute x0 -> x21, waiting for transfers between devices: none -> 251 us  [the longest x12 171 us: ring_scatter(): held = lax.ppermute(held, 'expert', ring(count))]
    all_to_all x16 -> x8, waiting for transfers between devices: 255 us -> 111 us  [the longest x1 43.5 us: body(): x = lax.all_to_all(sent, 'expert', split_axis=0, concat_axis=0, tiled=True)]
    pallas_call x0 -> x4, Pallas kernels: none -> 134 us  [the longest x2 79.6 us: moe(): pl.pallas_call(functools.partial(moe_kernel, chunk), grid=(experts,), out...]
    all_gather x4 -> x0, waiting for transfers between devices: 70.9 us -> none  [the longest x2 38.1 us: body(): lax.all_gather(keys_here, 'expert', axis=1, tiled=True)]
    all_to_all x0 -> x3, blocking collectives: none -> 57.4 us  [the longest x1 28.3 us: body(): out = lax.all_to_all(out, 'expert', split_axis=0, concat_axis=0, tiled=True)]
    convert_element_type x29 -> x4, local copies, waits for them, and re-layouts: 52.5 us -> 0.48 us  [the longest x3 0.25 us: body(): take = jnp.repeat(take.astype(F32), PB, axis=2)]
  transfers between devices with their start and end apart: 29 -> 32, of which waited for: 20 -> 25; matrix products, arithmetic and copies ran while one was open for 29% -> 10% of each run, Pallas kernels for 0% -> 13%
where the time goes in v1:
time: 791 us; the launch traced here: 781 us
  waiting for transfers between devices  440 us (56%)
  Pallas kernels  134 us (17%)
  blocking collectives  57.4 us (7%)
  other arithmetic  41.3 us (5%)
  starting transfers between devices  38.4 us (5%)
  local copies, waits for them, and re-layouts  30 us (4%)
  matrix products  25.5 us (3%)
  between operations  14.6 us (2%)
    ppermute x12, waiting for transfers between devices, ring_scatter(): held = lax.ppermute(held, 'expert', ring(count))  171 us
    ppermute x9, waiting for transfers between devices, ring_gather(): parts.append(lax.ppermute(parts[-1], 'expert', ring(count)))  79.7 us
    pallas_call x2, Pallas kernels, moe(): pl.pallas_call(functools.partial(moe_kernel, chunk), grid=(experts,), out...  79.6 us
    reduce_scatter x1, waiting for transfers between devices, body(): lax.psum_scatter(sum_second, 'batch', scatter_dimension=1, tiled=True)  72.1 us
    all_to_all x1, waiting for transfers between devices, body(): x = lax.all_to_all(sent, 'expert', split_axis=0, concat_axis=0, tiled=True)  43.5 us
    pallas_call x1, Pallas kernels, attention_backward(): pl.pallas_call(attention_backward_kernel, out_shape=(jax.ShapeDtypeStruct...  28.8 us
    all_to_all x1, blocking collectives, body(): out = lax.all_to_all(out, 'expert', split_axis=0, concat_axis=0, tiled=True)  28.3 us
    pallas_call x1, Pallas kernels, attention_forward(): pl.pallas_call(attention_forward_kernel, out_shape=(jax.ShapeDtypeStruct(...  25.1 us
  transfers between devices with their start and end apart: 32, of which 25 were waited for; matrix products, arithmetic and copies ran while one was open for 10% of the time, Pallas kernels for 13%

profile of v1, /device:TPU:0, one launch (start us, length us, event | category | flops | bytes accessed | tf_op | source)
XLA Modules:
  0.0 780.9 jit_solution(11590407415207858946)
XLA Ops:
  7.2 1.9 convert_element_type.214
  10.1 5.2 all-to-all-start.2
  16.4 14.3 %all-to-all-done.2.refs_4_ = bf16[8,4,32,512]{3,2,1,0:T(8,128)(2,1)S(1)} async-done(((bf16[8,4,32,512]{3,2,1,0:T(8,128)(2,1)}), bf16[8,4,32,512]{3,2,1,0:T(8,128)(2,1)S(1)}, u32[]{:S(2)}, u32[]{:S(2)}) %all-to-all-start.2) | async-done | bytes 1048608 | tf_op jit(solution)/shard_map/all_to_all | solution.py:818
  30.7 4.9 all-to-all-start
  35.6 2.0 collective-permute-start.3
  37.6 43.5 %all-to-all-done = bf16[4,256,512]{2,1,0:T(8,128)(2,1)} async-done(((bf16[4,256,512]{2,1,0:T(8,128)(2,1)}), bf16[4,256,512]{2,1,0:T(8,128)(2,1)}, u32[]{:S(2)}, u32[]{:S(2)}) %all-to-all-start) | async-done | bytes 1048608 | tf_op jit(solution)/shard_map/all_to_all | solution.py:814
  81.1 25.1 %attention_forward.1 = (bf16[12,1024,128]{2,1,0:T(8,128)(2,1)}, f32[8,1,1024]{2,1,0:T(1,128)}, bf16[1024,512]{1,0:T(8,128)(2,1)}, f32[1024,512]{1,0:T(8,128)}, bf16[8,4,32,512]{3,2,1,0:T(8,128)(2,1)}) custom-call(bf16[1024,512]{1,0:T(8,128)(2,1)} %bitcast.1.x_ref, bf16[512,1536]{1,0:T(8,128)(2,1)} %wqkv_ref.3, bf16[512,512]{1,0:T(8,128)(2,1)} %wo_ref.3, ...), custom_call_target="tpu_custom_call" | custom-call | flops 15000000512 | bytes 12000000 | tf_op jit(solution)/shard_map/attention_forward/pallas_call | solution.py:422
  106.2 2.3 fusion.48
  108.5 4.8 all-to-all-start.4
  113.3 9.8 %all-to-all-done.4.refs_0_ = bf16[8,2,32,512]{3,2,1,0:T(8,128)(2,1)} async-done(((bf16[8,2,32,512]{3,2,1,0:T(8,128)(2,1)}), bf16[8,2,32,512]{3,2,1,0:T(8,128)(2,1)}, u32[]{:S(2)}, u32[]{:S(2)}) %all-to-all-start.4) | async-done | bytes 524320 | tf_op jit(solution)/shard_map/all_to_all | solution.py:840
  123.1 13.9 %all_to_all.55.refs_0_ = bf16[8,2,32,512]{3,2,1,0:T(8,128)(2,1)} all-to-all(bf16[8,2,32,512]{3,2,1,0:T(8,128)(2,1)} %get-tuple-element.59), channel_id=1, replica_groups=mesh['batch'=8,'expert'=4] {'batch'}, dimensions={0} | all-to-all | bytes 1048576 | tf_op jit(solution)/shard_map/all_to_all | solution.py:840
  137.1 15.5 %collective-permute-done.9.refs_1_ = bf16[8,2,32,512]{3,2,1,0:T(8,128)(2,1)} collective-permute-done((bf16[8,2,32,512]{3,2,1,0:T(8,128)(2,1)}, bf16[8,2,32,512]{3,2,1,0:T(8,128)(2,1)}, u32[]{:S(2)}, u32[]{:S(2)}) %collective-permute-start.9) | collective-permute-done | bytes 524320 | tf_op jit(solution)/shard_map/ppermute | solution.py:772
  153.4 10.5 %collective-permute-done.refs_1_ = bf16[8,2,32,512]{3,2,1,0:T(8,128)(2,1)} collective-permute-done((bf16[8,2,32,512]{3,2,1,0:T(8,128)(2,1)}, bf16[8,2,32,512]{3,2,1,0:T(8,128)(2,1)}, u32[]{:S(2)}, u32[]{:S(2)}) %collective-permute-start) | collective-permute-done | bytes 524320 | tf_op jit(solution)/shard_map/ppermute | solution.py:772
  163.9 11.2 %collective-permute-done.10.refs_2_ = bf16[8,2,32,512]{3,2,1,0:T(8,128)(2,1)} collective-permute-done((bf16[8,2,32,512]{3,2,1,0:T(8,128)(2,1)}, bf16[8,2,32,512]{3,2,1,0:T(8,128)(2,1)}, u32[]{:S(2)}, u32[]{:S(2)}) %collective-permute-start.10) | collective-permute-done | bytes 524320 | tf_op jit(solution)/shard_map/ppermute | solution.py:772
  177.6 31.2 %collective-permute-done.1.refs_2_ = bf16[8,2,32,512]{3,2,1,0:T(8,128)(2,1)} collective-permute-done((bf16[8,2,32,512]{3,2,1,0:T(8,128)(2,1)}, bf16[8,2,32,512]{3,2,1,0:T(8,128)(2,1)}, u32[]{:S(2)}, u32[]{:S(2)}) %collective-permute-start.1) | collective-permute-done | bytes 524320 | tf_op jit(solution)/shard_map/ppermute | solution.py:772
  208.8 11.2 %collective-permute-done.11.refs_3_ = bf16[8,2,32,512]{3,2,1,0:T(8,128)(2,1)} collective-permute-done((bf16[8,2,32,512]{3,2,1,0:T(8,128)(2,1)}, bf16[8,2,32,512]{3,2,1,0:T(8,128)(2,1)}, u32[]{:S(2)}, u32[]{:S(2)}) %collective-permute-start.11) | collective-permute-done | bytes 524320 | tf_op jit(solution)/shard_map/ppermute | solution.py:772
  220.1 39.8 %mixture.3 = (bf16[4,8,2,32,512]{4,3,2,1,0:T(8,128)(2,1)}, bf16[4,8,2,32,512]{4,3,2,1,0:T(8,128)(2,1)}, bf16[4,384,512]{2,1,0:T(8,128)(2,1)}, bf16[4,384,512]{2,...) custom-call(s32[1]{0:T(128)} %bitcast.5.z_ref, ...), custom_call_target="tpu_custom_call" | custom-call | flops 16884901888 | bytes 50000000 | tf_op jit(solution)/shard_map/mixture/pallas_call | solution.py:725
  259.9 1.9 dynamic-slice_bitcast_fusion
  262.8 39.8 %mixture.2 = (bf16[4,8,2,32,512]{4,3,2,1,0:T(8,128)(2,1)}, bf16[4,8,2,32,512]{4,3,2,1,0:T(8,128)(2,1)}, bf16[4,384,512]{2,1,0:T(8,128)(2,1)}, bf16[4,384,512]{2,...) custom-call(s32[1]{0:T(128)} %bitcast.5.z_ref, ...), custom_call_target="tpu_custom_call" | custom-call | flops 16884901888 | bytes 50000000 | tf_op jit(solution)/shard_map/mixture/pallas_call | solution.py:725
  302.6 1.9 dynamic-slice_bitcast_fusion.1
  304.5 2.0 fusion.27
  307.1 14.2 %collective-permute-done.15 = bf16[8,2,32,512]{3,2,1,0:T(8,128)(2,1)S(1)} collective-permute-done((bf16[8,2,32,512]{3,2,1,0:T(8,128)(2,1)}, bf16[8,2,32,512]{3,2,1,0:T(8,128)(2,1)S(1)}, u32[]{:S(2)}, u32[]{:S(2)}) %collective-permute-start.15) | collective-permute-done | bytes 524320 | tf_op jit(solution)/shard_map/ppermute | solution.py:782
  321.3 2.0 fusion.30
  323.3 9.2 %collective-permute-done.19 = bf16[8,2,32,512]{3,2,1,0:T(8,128)(2,1)S(1)} collective-permute-done((bf16[8,2,32,512]{3,2,1,0:T(8,128)(2,1)}, bf16[8,2,32,512]{3,2,1,0:T(8,128)(2,1)S(1)}, u32[]{:S(2)}, u32[]{:S(2)}) %collective-permute-start.19) | collective-permute-done | bytes 524320 | tf_op jit(solution)/shard_map/ppermute | solution.py:782
  332.6 2.0 fusion.26
  334.6 9.3 %collective-permute-done.16 = bf16[8,2,32,512]{3,2,1,0:T(8,128)(2,1)} collective-permute-done((bf16[8,2,32,512]{3,2,1,0:T(8,128)(2,1)}, bf16[8,2,32,512]{3,2,1,0:T(8,128)(2,1)}, u32[]{:S(2)}, u32[]{:S(2)}) %collective-permute-start.16) | collective-permute-done | bytes 524320 | tf_op jit(solution)/shard_map/ppermute | solution.py:782
  343.9 2.2 fusion.29
  346.1 9.1 %collective-permute-done.20 = bf16[8,2,32,512]{3,2,1,0:T(8,128)(2,1)} collective-permute-done((bf16[8,2,32,512]{3,2,1,0:T(8,128)(2,1)}, bf16[8,2,32,512]{3,2,1,0:T(8,128)(2,1)}, u32[]{:S(2)}, u32[]{:S(2)}) %collective-permute-start.20) | collective-permute-done | bytes 524320 | tf_op jit(solution)/shard_map/ppermute | solution.py:782
  355.2 2.2 fusion.25
  357.3 4.3 all-to-all-start.8
  361.6 3.0 collective-permute-done.17
  364.6 2.2 fusion.28
  366.7 4.7 all-to-all-done.8
  371.4 4.1 all-to-all-start.7
  375.6 2.2 fusion.24
  377.8 1.8 gather_fusion
  380.9 4.5 all-to-all-done.7
  385.3 3.6 all-to-all-start.9
  389.4 2.3 pad_maximum_fusion.gm_ref
  391.7 12.6 %all-to-all-done.9.cot_ref = bf16[8,4,32,512]{3,2,1,0:T(8,128)(2,1)S(1)} async-done(((bf16[8,4,32,512]{3,2,1,0:T(8,128)(2,1)}), bf16[8,4,32,512]{3,2,1,0:T(8,128)(2,1)S(1)}, u32[]{:S(2)}, u32[]{:S(2)}) %all-to-all-start.9) | async-done | bytes 1048608 | tf_op jit(solution)/shard_map/all_to_all | solution.py:864
  405.3 28.8 %attention_backward.1 = (bf16[1024,512]{1,0:T(8,128)(2,1)}, f32[512,1536]{1,0:T(8,128)}, f32[512,512]{1,0:T(8,128)}, f32[1,512]{1,0:T(1,128)}, f32[1,512]{1,0:T(1,128)}) custom-call(bf16[8,4,32,512]{3,2,1,0:T(8,128)(2,1)} %pad_maximum_fusion.gm_ref, bf16[8,4,32,512]{3,2,1,0:T(8,128)(2,1)} %copy-done.7, bf16[1024,512]{1,0:T(8,128)(2,1)} %bitcast.1.x_ref, ...), custom_call_target="tpu_custom_call" | custom-call | flops 35000000512 | bytes 20000000 | tf_op jit(solution)/shard_map/attention_backward/pallas_call | solution.py:525
  435.7 5.9 concatenate.23
  441.7 12.8 %fusion.11 = bf16[4,512,2048]{2,1,0:T(8,128)(2,1)} fusion(bf16[4,384,2048]{2,1,0:T(8,128)(2,1)} %get-tuple-element.52, bf16[4,384,2048]{2,1,0:T(8,128)(2,1)} %get-tuple-element.51, bf16[4,384,512]{2,1,0:T(8,128)(2,1)} %get-tuple-element.50, bf16[4,384,512]{2,1,0:T(8,128)(2,1)} %get-tuple-element.49), kind=kOutput, calls=%fused_computation.10 | convolution fusion | flops 6478102528 | bytes 24117248 | tf_op jit(solution)/shard_map/erd,erf->edf/dot_general | solution.py:855
  454.8 12.7 %fusion.8 = bf16[4,2048,512]{2,1,0:T(8,128)(2,1)} fusion(bf16[4,384,2048]{2,1,0:T(8,128)(2,1)} %get-tuple-element.54, bf16[4,384,2048]{2,1,0:T(8,128)(2,1)} %get-tuple-element.53, bf16[4,384,512]{2,1,0:T(8,128)(2,1)} %get-tuple-element.56, bf16[4,384,512]{2,1,0:T(8,128)(2,1)} %get-tuple-element.55), kind=kOutput, calls=%fused_computation.9 | convolution fusion | flops 6478102528 | bytes 24117248 | tf_op jit(solution)/shard_map/erf,erd->efd/dot_general | solution.py:856
  470.6 25.7 %collective-permute-done.12 = bf16[8,2,32,512]{3,2,1,0:T(8,128)(2,1)S(1)} collective-permute-done((bf16[8,2,32,512]{3,2,1,0:T(8,128)(2,1)S(1)}, bf16[8,2,32,512]{3,2,1,0:T(8,128)(2,1)S(1)}, u32[]{:S(2)}, u32[]{:S(2)}) %collective-permute-start.12) | collective-permute-done | bytes 524320 | tf_op jit(solution)/shard_map/ppermute | solution.py:782
  497.6 21.2 %collective-permute-done.6 = bf16[8,2,32,512]{3,2,1,0:T(8,128)(2,1)S(1)} collective-permute-done((bf16[8,2,32,512]{3,2,1,0:T(8,128)(2,1)S(1)}, bf16[8,2,32,512]{3,2,1,0:T(8,128)(2,1)S(1)}, u32[]{:S(2)}, u32[]{:S(2)}) %collective-permute-start.6) | collective-permute-done | bytes 524320 | tf_op jit(solution)/shard_map/ppermute | solution.py:782
  520.0 21.2 %collective-permute-done.13 = bf16[8,2,32,512]{3,2,1,0:T(8,128)(2,1)S(1)} collective-permute-done((bf16[8,2,32,512]{3,2,1,0:T(8,128)(2,1)S(1)}, bf16[8,2,32,512]{3,2,1,0:T(8,128)(2,1)S(1)}, u32[]{:S(2)}, u32[]{:S(2)}) %collective-permute-start.13) | collective-permute-done | bytes 524320 | tf_op jit(solution)/shard_map/ppermute | solution.py:782
  541.5 22.2 %collective-permute-done.7 = bf16[8,2,32,512]{3,2,1,0:T(8,128)(2,1)S(1)} collective-permute-done((bf16[8,2,32,512]{3,2,1,0:T(8,128)(2,1)S(1)}, bf16[8,2,32,512]{3,2,1,0:T(8,128)(2,1)S(1)}, u32[]{:S(2)}, u32[]{:S(2)}) %collective-permute-start.7) | collective-permute-done | bytes 524320 | tf_op jit(solution)/shard_map/ppermute | solution.py:782
  565.0 21.2 %collective-permute-done.14 = bf16[8,2,32,512]{3,2,1,0:T(8,128)(2,1)S(1)} collective-permute-done((bf16[8,2,32,512]{3,2,1,0:T(8,128)(2,1)S(1)}, bf16[8,2,32,512]{3,2,1,0:T(8,128)(2,1)S(1)}, u32[]{:S(2)}, u32[]{:S(2)}) %collective-permute-start.14) | collective-permute-done | bytes 524320 | tf_op jit(solution)/shard_map/ppermute | solution.py:782
  587.1 3.5 all-to-all-start.5
  590.6 14.7 %collective-permute-done.8 = bf16[8,2,32,512]{3,2,1,0:T(8,128)(2,1)} collective-permute-done((bf16[8,2,32,512]{3,2,1,0:T(8,128)(2,1)S(1)}, bf16[8,2,32,512]{3,2,1,0:T(8,128)(2,1)}, u32[]{:S(2)}, u32[]{:S(2)}) %collective-permute-start.8) | collective-permute-done | bytes 524320 | tf_op jit(solution)/shard_map/ppermute | solution.py:782
  606.7 15.2 %all_to_all.56 = bf16[8,2,32,512]{3,2,1,0:T(8,128)(2,1)S(1)} all-to-all(bf16[8,2,32,512]{3,2,1,0:T(8,128)(2,1)S(1)} %fusion.34), channel_id=1, replica_groups=mesh['batch'=8,'expert'=4] {'batch'}, dimensions={0} | all-to-all | bytes 1048576 | tf_op jit(solution)/shard_map/all_to_all | solution.py:848
  624.0 28.3 %all_to_all.57 = bf16[4,256,512]{2,1,0:T(8,128)(2,1)} all-to-all(bf16[4,256,512]{2,1,0:T(8,128)(2,1)S(1)} %fusion.20), channel_id=1, replica_groups=mesh['batch'=8,'expert'=4] {'expert'}, dimensions={0} | all-to-all | bytes 2097152 | tf_op jit(solution)/shard_map/all_to_all | solution.py:871
  652.3 3.5 all-to-all-start.10
  655.9 3.0 convert_add_fusion.1
  658.9 21.7 %all-to-all-done.10 = bf16[4,256,512]{2,1,0:T(8,128)(2,1)S(1)} async-done(((bf16[4,256,512]{2,1,0:T(8,128)(2,1)}), bf16[4,256,512]{2,1,0:T(8,128)(2,1)S(1)}, u32[]{:S(2)}, u32[]{:S(2)}) %all-to-all-start.10) | async-done | bytes 1048608 | tf_op jit(solution)/shard_map/all_to_all | solution.py:873
  680.6 3.9 convert_add_fusion
  684.5 1.5 slice.54
  686.0 1.4 slice.55
  688.7 1.5 slice_reduce_fusion
  690.2 6.2 reduce-scatter.6.cloned.1.call-done
  696.3 2.7 convert_element_type.278
  699.1 72.1 %reduce-scatter.8.cloned.1.call-done = bf16[4,256,512]{2,1,0:T(8,128)(2,1)} async-done(((bf16[4,2048,512]{2,1,0:T(8,128)(2,1)}), bf16[4,256,512]{2,1,0:T(8,128)(2,1)}) %reduce-scatter.8.cloned.1.call-update) | async-done | bytes 1048592 | tf_op jit(solution)/shard_map/reduce_scatter | solution.py:858
  771.1 2.8 convert_element_type.280
  (112 shorter events, 24.6 us)
Async XLA Ops:
  7.2 169.2 %copy-start = (bf16[512,16]{0,1:T(8,128)(2,1)S(1)}, bf16[512,16]{0,1:T(8,128)(2,1)}, u32[]{:S(2)}) copy-start(bf16[512,16]{0,1:T(8,128)(2,1)} %param.15) | copy-start | bytes 49156
  7.2 8.1 %copy-start.2 = (f32[2,2,256,512]{3,2,1,0:T(8,128)S(1)}, f32[2,2,256,512]{3,2,1,0:T(8,128)}, u32[]{:S(2)}) copy-start(f32[2,2,256,512]{3,2,1,0:T(8,128)} %param.11) | copy-start | bytes 6291460
  10.1 20.6 %all-to-all-start.2 = ((bf16[8,4,32,512]{3,2,1,0:T(8,128)(2,1)}), bf16[8,4,32,512]{3,2,1,0:T(8,128)(2,1)S(1)}, u32[]{:S(2)}, u32[]{:S(2)}) async-start(bf16[8,4,32,512]{3,2,1,0:T(8,128)(2,1)} %bitcast.91), calls=%async_computation.2 | async-start | bytes 2097152 | tf_op jit(solution)/shard_map/all_to_all | solution.py:818
  30.7 75.5 %copy-start.3 = (bf16[8,4,32,512]{3,2,1,0:T(8,128)(2,1)}, bf16[8,4,32,512]{3,2,1,0:T(8,128)(2,1)S(1)}, u32[]{:S(2)}) copy-start(bf16[8,4,32,512]{3,2,1,0:T(8,128)(2,1)S(1)} %all-to-all-done.2.refs_4_) | copy-start | bytes 3145732
  30.7 50.4 %all-to-all-start = ((bf16[4,256,512]{2,1,0:T(8,128)(2,1)}), bf16[4,256,512]{2,1,0:T(8,128)(2,1)}, u32[]{:S(2)}, u32[]{:S(2)}) async-start(bf16[4,256,512]{2,1,0:T(8,128)(2,1)} %bitcast), calls=%async_computation | async-start | bytes 2097152 | tf_op jit(solution)/shard_map/all_to_all | solution.py:814
  35.6 77.7 %collective-permute-start.3 = (bf16[8,4,32,512]{3,2,1,0:T(8,128)(2,1)S(1)}, bf16[8,4,32,512]{3,2,1,0:T(8,128)(2,1)}, u32[]{:S(2)}, u32[]{:S(2)}) collective-permute-start(bf16[8,4,32,512]{3,2,1,0:T(8,128)(2,1)S(1)} %all-to-all-done.2.refs_4_), channel_id=1, source_target_pairs={{0,1},{1,2},{2,3},{3,0},{4,5},{5,6},{6,7},{7,4},{8,9},{9,10},{10,1... | collective-permute-start | bytes 3145736 | tf_op jit(solution)/shard_map/ppermute | solution.py:772
  106.2 46.6 %copy-start.12 = (s32[2,3]{1,0:T(2,128)S(1)}, s32[2,3]{1,0:T(2,128)}, u32[]{:S(2)}) copy-start(s32[2,3]{1,0:T(2,128)} %param.20) | copy-start | bytes 76
  106.2 69.0 %copy-start.13 = (s32[2,16]{1,0:T(2,128)S(1)}, s32[2,16]{1,0:T(2,128)}, u32[]{:S(2)}) copy-start(s32[2,16]{1,0:T(2,128)} %param.21) | copy-start | bytes 388
  108.5 14.7 %all-to-all-start.4 = ((bf16[8,2,32,512]{3,2,1,0:T(8,128)(2,1)}), bf16[8,2,32,512]{3,2,1,0:T(8,128)(2,1)}, u32[]{:S(2)}, u32[]{:S(2)}) async-start(bf16[8,2,32,512]{3,2,1,0:T(8,128)(2,1)} %get-tuple-element.60), calls=%async_computation.4 | async-start | bytes 1048576 | tf_op jit(solution)/shard_map/all_to_all | solution.py:840
  113.3 39.4 %collective-permute-start.4 = (bf16[8,4,32,512]{3,2,1,0:T(8,128)(2,1)}, bf16[8,4,32,512]{3,2,1,0:T(8,128)(2,1)S(1)}, u32[]{:S(2)}, u32[]{:S(2)}) collective-permute-start(bf16[8,4,32,512]{3,2,1,0:T(8,128)(2,1)} %collective-permute-done.3.refs_5_), channel_id=1, source_target_pairs={{0,1},{1,2},{2,3},{3,0},{4,5},{5,6},{6,7},{7,4},{8,9},{9,10},{10,1... | collective-permute-start | bytes 3145736 | tf_op jit(solution)/shard_map/ppermute | solution.py:772
  123.1 29.5 %collective-permute-start.9 = (bf16[8,2,32,512]{3,2,1,0:T(8,128)(2,1)}, bf16[8,2,32,512]{3,2,1,0:T(8,128)(2,1)}, u32[]{:S(2)}, u32[]{:S(2)}) collective-permute-start(bf16[8,2,32,512]{3,2,1,0:T(8,128)(2,1)} %all-to-all-done.4.refs_0_), channel_id=1, source_target_pairs={{0,1},{1,2},{2,3},{3,0},{4,5},{5,6},{6,7},{7,4},{8,9},{9,10},{10,1... | collective-permute-start | bytes 1572872 | tf_op jit(solution)/shard_map/ppermute | solution.py:772
  137.0 26.9 %collective-permute-start = (bf16[8,2,32,512]{3,2,1,0:T(8,128)(2,1)}, bf16[8,2,32,512]{3,2,1,0:T(8,128)(2,1)}, u32[]{:S(2)}, u32[]{:S(2)}) collective-permute-start(bf16[8,2,32,512]{3,2,1,0:T(8,128)(2,1)} %all_to_all.55.refs_0_), channel_id=1, source_target_pairs={{0,1},{1,2},{2,3},{3,0},{4,5},{5,6},{6,7},{7,4},{8,9},{9,10},{10,1... | collective-permute-start | bytes 1572872 | tf_op jit(solution)/shard_map/ppermute | solution.py:772
  152.6 22.5 %collective-permute-start.10 = (bf16[8,2,32,512]{3,2,1,0:T(8,128)(2,1)}, bf16[8,2,32,512]{3,2,1,0:T(8,128)(2,1)}, u32[]{:S(2)}, u32[]{:S(2)}) collective-permute-start(bf16[8,2,32,512]{3,2,1,0:T(8,128)(2,1)} %collective-permute-done.9.refs_1_), channel_id=1, source_target_pairs={{0,1},{1,2},{2,3},{3,0},{4,5},{5,6},{6,7},{7,4},{8,9},{9,10},{10,1... | collective-permute-start | bytes 1572872 | tf_op jit(solution)/shard_map/ppermute | solution.py:772
  152.6 67.4 %copy-start.8 = (bf16[8,4,32,512]{3,2,1,0:T(8,128)(2,1)}, bf16[8,4,32,512]{3,2,1,0:T(8,128)(2,1)S(1)}, u32[]{:S(2)}) copy-start(bf16[8,4,32,512]{3,2,1,0:T(8,128)(2,1)S(1)} %collective-permute-done.4.refs_6_) | copy-start | bytes 3145732
  152.6 67.4 %collective-permute-start.5 = (bf16[8,4,32,512]{3,2,1,0:T(8,128)(2,1)S(1)}, bf16[8,4,32,512]{3,2,1,0:T(8,128)(2,1)}, u32[]{:S(2)}, u32[]{:S(2)}) collective-permute-start(bf16[8,4,32,512]{3,2,1,0:T(8,128)(2,1)S(1)} %collective-permute-done.4.refs_6_), channel_id=1, source_target_pairs={{0,1},{1,2},{2,3},{3,0},{4,5},{5,6},{6,7},{7,4},{8,9},{9,10},{10,1... | collective-permute-start | bytes 3145736 | tf_op jit(solution)/shard_map/ppermute | solution.py:772
  163.9 44.9 %collective-permute-start.1 = (bf16[8,2,32,512]{3,2,1,0:T(8,128)(2,1)}, bf16[8,2,32,512]{3,2,1,0:T(8,128)(2,1)}, u32[]{:S(2)}, u32[]{:S(2)}) collective-permute-start(bf16[8,2,32,512]{3,2,1,0:T(8,128)(2,1)} %collective-permute-done.refs_1_), channel_id=1, source_target_pairs={{0,1},{1,2},{2,3},{3,0},{4,5},{5,6},{6,7},{7,4},{8,9},{9,10},{10,1... | collective-permute-start | bytes 1572872 | tf_op jit(solution)/shard_map/ppermute | solution.py:772
  175.1 44.9 %collective-permute-start.11 = (bf16[8,2,32,512]{3,2,1,0:T(8,128)(2,1)}, bf16[8,2,32,512]{3,2,1,0:T(8,128)(2,1)}, u32[]{:S(2)}, u32[]{:S(2)}) collective-permute-start(bf16[8,2,32,512]{3,2,1,0:T(8,128)(2,1)} %collective-permute-done.10.refs_2_), channel_id=1, source_target_pairs={{0,1},{1,2},{2,3},{3,0},{4,5},{5,6},{6,7},{7,4},{8,9},{9,10},{10,1... | collective-permute-start | bytes 1572872 | tf_op jit(solution)/shard_map/ppermute | solution.py:772
  175.3 44.7 %copy-start.9 = (f32[2,3,256]{2,1,0:T(4,128)}, f32[2,3,256]{2,1,0:T(4,128)S(1)}, u32[]{:S(2)}) copy-start(f32[2,3,256]{2,1,0:T(4,128)S(1)} %copy.43.refs_9_) | copy-start | bytes 18436
  208.8 53.1 %collective-permute-start.2 = (bf16[8,2,32,512]{3,2,1,0:T(8,128)(2,1)}, bf16[8,2,32,512]{3,2,1,0:T(8,128)(2,1)S(1)}, u32[]{:S(2)}, u32[]{:S(2)}) collective-permute-start(bf16[8,2,32,512]{3,2,1,0:T(8,128)(2,1)} %collective-permute-done.1.refs_2_), channel_id=1, source_target_pairs={{0,1},{1,2},{2,3},{3,0},{4,5},{5,6},{6,7},{7,4},{8,9},{9,10},{10,1... | collective-permute-start | bytes 1572872 | tf_op jit(solution)/shard_map/ppermute | solution.py:772
  261.8 42.7 %collective-permute-start.18 = (bf16[8,2,32,512]{3,2,1,0:T(8,128)(2,1)}, bf16[8,2,32,512]{3,2,1,0:T(8,128)(2,1)S(1)}, u32[]{:S(2)}, u32[]{:S(2)}) collective-permute-start(bf16[8,2,32,512]{3,2,1,0:T(8,128)(2,1)} %dynamic-slice_bitcast_fusion), channel_id=1, source_target_pairs={{0,1},{1,2},{2,3},{3,0},{4,5},{5,6},{6,7},{7,4},{8,9},{9,10},{10,1... | collective-permute-start | bytes 1572872 | tf_op jit(solution)/shard_map/ppermute | solution.py:782
  262.0 0.8 copy-start.14
  304.5 16.9 %collective-permute-start.15 = (bf16[8,2,32,512]{3,2,1,0:T(8,128)(2,1)}, bf16[8,2,32,512]{3,2,1,0:T(8,128)(2,1)S(1)}, u32[]{:S(2)}, u32[]{:S(2)}) collective-permute-start(bf16[8,2,32,512]{3,2,1,0:T(8,128)(2,1)} %dynamic-slice_bitcast_fusion.1), channel_id=1, source_target_pairs={{0,1},{1,2},{2,3},{3,0},{4,5},{5,6},{6,7},{7,4},{8,9},{9,10},{10,1... | collective-permute-start | bytes 1572872 | tf_op jit(solution)/shard_map/ppermute | solution.py:782
  306.5 26.1 %collective-permute-start.19 = (bf16[8,2,32,512]{3,2,1,0:T(8,128)(2,1)}, bf16[8,2,32,512]{3,2,1,0:T(8,128)(2,1)S(1)}, u32[]{:S(2)}, u32[]{:S(2)}) collective-permute-start(bf16[8,2,32,512]{3,2,1,0:T(8,128)(2,1)} %fusion.27), channel_id=1, source_target_pairs={{0,1},{1,2},{2,3},{3,0},{4,5},{5,6},{6,7},{7,4},{8,9},{9,10},{10,1... | collective-permute-start | bytes 1572872 | tf_op jit(solution)/shard_map/ppermute | solution.py:782
  323.3 20.6 %collective-permute-start.16 = (bf16[8,2,32,512]{3,2,1,0:T(8,128)(2,1)}, bf16[8,2,32,512]{3,2,1,0:T(8,128)(2,1)}, u32[]{:S(2)}, u32[]{:S(2)}) collective-permute-start(bf16[8,2,32,512]{3,2,1,0:T(8,128)(2,1)} %fusion.30), channel_id=1, source_target_pairs={{0,1},{1,2},{2,3},{3,0},{4,5},{5,6},{6,7},{7,4},{8,9},{9,10},{10,1... | collective-permute-start | bytes 1572872 | tf_op jit(solution)/shard_map/ppermute | solution.py:782
  334.6 41.0 %copy-start.4 = (bf16[8,4,32,512]{3,2,1,0:T(8,128)(2,1)S(1)}, bf16[8,4,32,512]{3,2,1,0:T(8,128)(2,1)}, u32[]{:S(2)}) copy-start(bf16[8,4,32,512]{3,2,1,0:T(8,128)(2,1)} %copy-done.3) | copy-start | bytes 3145732
  334.6 20.6 %collective-permute-start.20 = (bf16[8,2,32,512]{3,2,1,0:T(8,128)(2,1)}, bf16[8,2,32,512]{3,2,1,0:T(8,128)(2,1)}, u32[]{:S(2)}, u32[]{:S(2)}) collective-permute-start(bf16[8,2,32,512]{3,2,1,0:T(8,128)(2,1)} %fusion.26), channel_id=1, source_target_pairs={{0,1},{1,2},{2,3},{3,0},{4,5},{5,6},{6,7},{7,4},{8,9},{9,10},{10,1... | collective-permute-start | bytes 1572872 | tf_op jit(solution)/shard_map/ppermute | solution.py:782
  346.1 18.5 %collective-permute-start.17 = (bf16[8,2,32,512]{3,2,1,0:T(8,128)(2,1)}, bf16[8,2,32,512]{3,2,1,0:T(8,128)(2,1)}, u32[]{:S(2)}, u32[]{:S(2)}) collective-permute-start(bf16[8,2,32,512]{3,2,1,0:T(8,128)(2,1)} %fusion.29), channel_id=1, source_target_pairs={{0,1},{1,2},{2,3},{3,0},{4,5},{5,6},{6,7},{7,4},{8,9},{9,10},{10,1... | collective-permute-start | bytes 1572872 | tf_op jit(solution)/shard_map/ppermute | solution.py:782
  357.3 14.1 %all-to-all-start.8 = ((bf16[8,2,32,512]{3,2,1,0:T(8,128)(2,1)}), bf16[8,2,32,512]{3,2,1,0:T(8,128)(2,1)}, u32[]{:S(2)}, u32[]{:S(2)}) async-start(bf16[8,2,32,512]{3,2,1,0:T(8,128)(2,1)} %fusion.25), calls=%async_computation.8 | async-start | bytes 1048576 | tf_op jit(solution)/shard_map/all_to_all | solution.py:846
  371.4 13.9 %all-to-all-start.7 = ((bf16[8,2,32,512]{3,2,1,0:T(8,128)(2,1)}), bf16[8,2,32,512]{3,2,1,0:T(8,128)(2,1)}, u32[]{:S(2)}, u32[]{:S(2)}) async-start(bf16[8,2,32,512]{3,2,1,0:T(8,128)(2,1)} %fusion.28), calls=%async_computation.7 | async-start | bytes 1048576 | tf_op jit(solution)/shard_map/all_to_all | solution.py:846
  377.8 11.3 %copy-start.10 = (f32[16,512]{1,0:T(8,128)S(1)}, f32[16,512]{1,0:T(8,128)}, u32[]{:S(2)}) copy-start(f32[16,512]{1,0:T(8,128)} %get-tuple-element.46) | copy-start | bytes 98308
  377.8 11.3 %copy-start.11 = (f32[16,512]{1,0:T(8,128)S(1)}, f32[16,512]{1,0:T(8,128)}, u32[]{:S(2)}) copy-start(f32[16,512]{1,0:T(8,128)} %get-tuple-element.45) | copy-start | bytes 98308
  385.3 18.9 %all-to-all-start.9 = ((bf16[8,4,32,512]{3,2,1,0:T(8,128)(2,1)}), bf16[8,4,32,512]{3,2,1,0:T(8,128)(2,1)S(1)}, u32[]{:S(2)}, u32[]{:S(2)}) async-start(bf16[8,4,32,512]{3,2,1,0:T(8,128)(2,1)} %fusion.37), calls=%async_computation.9 | async-start | bytes 2097152 | tf_op jit(solution)/shard_map/all_to_all | solution.py:864
  388.9 295.6 %reduce-scatter.4.cloned.1.call-start = ((), (), s32[]{:S(2)}) async-start(), calls=%async_computation.14 | async-start | bytes 4595712 | tf_op jit(solution)/shard_map/reduce_scatter | solution.py:882
  404.2 1.0 copy-start.7
  441.6 254.7 %reduce-scatter.6.cloned.1.call-start = ((), (), s32[]{:S(2)}) async-start(), calls=%async_computation.15 | async-start | bytes 9437184 | tf_op jit(solution)/shard_map/reduce_scatter | solution.py:857
  454.5 316.6 %reduce-scatter.8.cloned.1.call-start = ((), (), s32[]{:S(2)}) async-start(), calls=%async_computation.16 | async-start | bytes 9437184 | tf_op jit(solution)/shard_map/reduce_scatter | solution.py:858
  467.5 73.7 %copy-start.6 = (bf16[4,8,2,32,512]{4,3,2,1,0:T(8,128)(2,1)S(1)}, bf16[4,8,2,32,512]{4,3,2,1,0:T(8,128)(2,1)}, u32[]{:S(2)}) copy-start(bf16[4,8,2,32,512]{4,3,2,1,0:T(8,128)(2,1)} %get-tuple-element.36) | copy-start | bytes 6291460
  468.8 27.5 %collective-permute-start.12 = (bf16[8,2,32,512]{3,2,1,0:T(8,128)(2,1)S(1)}, bf16[8,2,32,512]{3,2,1,0:T(8,128)(2,1)S(1)}, u32[]{:S(2)}, u32[]{:S(2)}) collective-permute-start(bf16[8,2,32,512]{3,2,1,0:T(8,128)(2,1)S(1)} %dynamic-slice_bitcast_fusion.2), channel_id=1, source_target_pairs={{0,1},{1,2},{2,3},{3,0},{4,5},{5,6},{6,7},{7,4},{8,9},{9,10},{10,1... | collective-permute-start | bytes 1572872 | tf_op jit(solution)/shard_map/ppermute | solution.py:782
  469.9 48.8 %collective-permute-start.6 = (bf16[8,2,32,512]{3,2,1,0:T(8,128)(2,1)S(1)}, bf16[8,2,32,512]{3,2,1,0:T(8,128)(2,1)S(1)}, u32[]{:S(2)}, u32[]{:S(2)}) collective-permute-start(bf16[8,2,32,512]{3,2,1,0:T(8,128)(2,1)S(1)} %dynamic-slice_bitcast_fusion.3), channel_id=1, source_target_pairs={{0,1},{1,2},{2,3},{3,0},{4,5},{5,6},{6,7},{7,4},{8,9},{9,10},{10,1... | collective-permute-start | bytes 1572872 | tf_op jit(solution)/shard_map/ppermute | solution.py:782
  497.5 43.7 %collective-permute-start.13 = (bf16[8,2,32,512]{3,2,1,0:T(8,128)(2,1)S(1)}, bf16[8,2,32,512]{3,2,1,0:T(8,128)(2,1)S(1)}, u32[]{:S(2)}, u32[]{:S(2)}) collective-permute-start(bf16[8,2,32,512]{3,2,1,0:T(8,128)(2,1)S(1)} %fusion.33), channel_id=1, source_target_pairs={{0,1},{1,2},{2,3},{3,0},{4,5},{5,6},{6,7},{7,4},{8,9},{9,10},{10,1... | collective-permute-start | bytes 1572872 | tf_op jit(solution)/shard_map/ppermute | solution.py:782
  520.0 43.7 %collective-permute-start.7 = (bf16[8,2,32,512]{3,2,1,0:T(8,128)(2,1)S(1)}, bf16[8,2,32,512]{3,2,1,0:T(8,128)(2,1)S(1)}, u32[]{:S(2)}, u32[]{:S(2)}) collective-permute-start(bf16[8,2,32,512]{3,2,1,0:T(8,128)(2,1)S(1)} %fusion.36), channel_id=1, source_target_pairs={{0,1},{1,2},{2,3},{3,0},{4,5},{5,6},{6,7},{7,4},{8,9},{9,10},{10,1... | collective-permute-start | bytes 1572872 | tf_op jit(solution)/shard_map/ppermute | solution.py:782
  541.4 44.8 %collective-permute-start.14 = (bf16[8,2,32,512]{3,2,1,0:T(8,128)(2,1)S(1)}, bf16[8,2,32,512]{3,2,1,0:T(8,128)(2,1)S(1)}, u32[]{:S(2)}, u32[]{:S(2)}) collective-permute-start(bf16[8,2,32,512]{3,2,1,0:T(8,128)(2,1)S(1)} %fusion.32), channel_id=1, source_target_pairs={{0,1},{1,2},{2,3},{3,0},{4,5},{5,6},{6,7},{7,4},{8,9},{9,10},{10,1... | collective-permute-start | bytes 1572872 | tf_op jit(solution)/shard_map/ppermute | solution.py:782
  564.9 40.4 %collective-permute-start.8 = (bf16[8,2,32,512]{3,2,1,0:T(8,128)(2,1)S(1)}, bf16[8,2,32,512]{3,2,1,0:T(8,128)(2,1)}, u32[]{:S(2)}, u32[]{:S(2)}) collective-permute-start(bf16[8,2,32,512]{3,2,1,0:T(8,128)(2,1)S(1)} %fusion.35), channel_id=1, source_target_pairs={{0,1},{1,2},{2,3},{3,0},{4,5},{5,6},{6,7},{7,4},{8,9},{9,10},{10,1... | collective-permute-start | bytes 1572872 | tf_op jit(solution)/shard_map/ppermute | solution.py:782
  587.1 19.5 %all-to-all-start.5 = ((bf16[8,2,32,512]{3,2,1,0:T(8,128)(2,1)}), bf16[8,2,32,512]{3,2,1,0:T(8,128)(2,1)S(1)}, u32[]{:S(2)}, u32[]{:S(2)}) async-start(bf16[8,2,32,512]{3,2,1,0:T(8,128)(2,1)} %fusion.31), calls=%async_computation.5 | async-start | bytes 1048576 | tf_op jit(solution)/shard_map/all_to_all | solution.py:848
  621.9 1.6 copy-start.5
  652.3 28.3 %all-to-all-start.10 = ((bf16[4,256,512]{2,1,0:T(8,128)(2,1)}), bf16[4,256,512]{2,1,0:T(8,128)(2,1)S(1)}, u32[]{:S(2)}, u32[]{:S(2)}) async-start(bf16[4,256,512]{2,1,0:T(8,128)(2,1)} %bitcast.98), calls=%async_computation.10 | async-start | bytes 2097152 | tf_op jit(solution)/shard_map/all_to_all | solution.py:873
  688.7 85.3 %copy-start.1 = (bf16[512,16]{0,1:T(8,128)(2,1)S(1)}, bf16[512,16]{0,1:T(8,128)(2,1)}, u32[]{:S(2)}) copy-start(bf16[512,16]{0,1:T(8,128)(2,1)} %param.15) | copy-start | bytes 49156
Sparse Core Ops, SparseCore 0:
  441.8 180.5 reduce-scatter.3
  626.2 70.1 reduce-scatter.5
  699.8 71.2 reduce-scatter.7

commit v2 on v1

--- a/solution.py
+++ b/solution.py
@@ -316,6 +316,8 @@
 PB = 16
 CHUNKS = 2
 VMEM_LIMIT = 60 * 1024 * 1024
+KERNEL_COST = pl.CostEstimate(flops=30_000_000_000, bytes_accessed=100_000, transcendentals=0)
+SMALL_COST = pl.CostEstimate(flops=1_000_000, bytes_accessed=100_000, transcendentals=0)
 
 
 def dot_nn(a, b):
@@ -356,15 +358,26 @@
     return key <= query
 
 
-def attention_forward_kernel(x_ref, wqkv_ref, wo_ref, g1_ref, g2_ref,
-                             qkv_ref, lse_ref, ctx_ref, attn_ref, mix_ref, ctx_pairs):
+def attention_forward_kernel(z_ref, *refs):
+    quarters = 4
+    parts = refs[:quarters]
+    (wqkv_ref, wo_ref, g1_ref, g2_ref, x_ref, qkv_ref, lse_ref, ctx_ref, attn_ref, mix_ref, more_ref) = refs[quarters:-2]
+    ctx_pairs, sems = refs[-2:]
     length, width = x_ref.shape
     pairs = HEADS // 2
     lanes = width // pairs
     half = lanes // 2
-    nb, quarters, piece, _ = mix_ref.shape
+    nb = mix_ref.shape[0]
     tile = length // quarters
     factor = half ** (-0.5)
+    copies = []
+    for k in range(quarters):
+        source = lax.rem(z_ref[0] - k + quarters, quarters)
+        rows = pl.ds(pl.multiple_of(source * tile, tile), tile)
+        copies.append(pltpu.make_async_copy(parts[k], x_ref.at[rows, :], sems.at[k]))
+        copies[-1].start()
+    for copy in copies:
+        copy.wait()
 
     def project(i, carry):
         rows = pl.ds(pl.multiple_of(i * tile, tile), tile)
@@ -376,7 +389,7 @@
                 qkv_ref[part * pairs + p, rows, :] = out[:, p * lanes:(p + 1) * lanes]
         return carry
 
-    lax.fori_loop(0, quarters, project, 0)
+    lax.fori_loop(0, quarters, project, 0, unroll=True)
 
     def attend(p, carry):
         values_t = qkv_ref[2 * pairs + p].T
@@ -408,42 +421,61 @@
         attn_ref[rows, :] = attn
         normed, _ = row_norm(x_ref[rows, :].astype(F32) + attn)
         mix = (normed * g2_ref[...]).astype(BF16)
+        low = attn.astype(BF16)
         for b in range(nb):
-            mix_ref[b, i, :, :] = mix[b * piece:(b + 1) * piece]
+            at = b * CHUNKS * PB
+            mix_ref[b, i] = mix[at:at + PB]
+            more_ref[b, 0, i] = mix[at + PB:at + 2 * PB]
+            more_ref[b, 1, i] = low[at:at + PB]
+            more_ref[b, 2, i] = low[at + PB:at + 2 * PB]
         return carry
 
-    lax.fori_loop(0, quarters, finish, 0)
-
-
-def attention_forward(x, wqkv, wo, g1, g2, nb, quarters):
-    length, width = x.shape
+    lax.fori_loop(0, quarters, finish, 0, unroll=True)
+
+
+def attention_forward(z, parts, wqkv, wo, g1, g2, nb):
+    quarters = len(parts)
+    tile, width = parts[0].shape
+    length = quarters * tile
     pairs = HEADS // 2
     lanes = width // pairs
+    vmem = pl.BlockSpec(memory_space=pltpu.VMEM)
     return pl.pallas_call(
         attention_forward_kernel,
+        in_specs=[pl.BlockSpec(memory_space=pltpu.SMEM)]
+        + [pl.BlockSpec(memory_space=pl.ANY)] * quarters + [vmem] * 4,
         out_shape=(
+            jax.ShapeDtypeStruct((length, width), BF16),
             jax.ShapeDtypeStruct((3 * pairs, length, lanes), BF16),
             jax.ShapeDtypeStruct((HEADS, 1, length), F32),
             jax.ShapeDtypeStruct((length, width), BF16),
             jax.ShapeDtypeStruct((length, width), F32),
-            jax.ShapeDtypeStruct((nb, quarters, length // quarters // nb, width), BF16),
+            jax.ShapeDtypeStruct((nb, quarters, PB, width), BF16),
+            jax.ShapeDtypeStruct((nb, 3, quarters, PB, width), BF16),
         ),
-        scratch_shapes=[pltpu.VMEM((pairs, length, lanes), BF16)],
+        scratch_shapes=[
+            pltpu.VMEM((pairs, length, lanes), BF16),
+            pltpu.SemaphoreType.DMA((quarters,)),
+        ],
         compiler_params=pltpu.CompilerParams(vmem_limit_bytes=VMEM_LIMIT),
-        cost_estimate=pl.CostEstimate(flops=15_000_000_000, bytes_accessed=12_000_000, transcendentals=5_000_000),
+        cost_estimate=KERNEL_COST,
         name="attention_forward",
-    )(x, wqkv, wo, g1, g2)
-
-
-def attention_backward_kernel(gm_ref, cot_ref, x_ref, attn_ref, ctx_ref, qkv_ref, lse_ref,
+    )(z, *parts, wqkv, wo, g1, g2)
+
+
+def attention_backward_kernel(count, *refs):
+    attention_backward_body(*refs[:11], *refs[11 + count:])
+
+
+def attention_backward_body(gm_ref, cot_ref, x_ref, attn_ref, ctx_ref, qkv_ref, lse_ref,
                               wqkv_ref, wo_ref, g1_ref, g2_ref,
-                              gin_ref, dqkv_ref, dwo_ref, dg1_ref, dg2_ref,
+                              gin_ref, dw_ref, dg1_ref, dg2_ref,
                               delta, ga_rows, dctx, gqkv, attn_in, dk_sum, dv_sum):
     length, width = x_ref.shape
     pairs = HEADS // 2
     lanes = width // pairs
     half = lanes // 2
-    nb, quarters, piece, _ = gm_ref.shape
+    nb, _, quarters, _, _ = gm_ref.shape
     tile = length // quarters
     factor = half ** (-0.5)
     dg2_ref[...] = jnp.zeros_like(dg2_ref)
@@ -452,7 +484,7 @@
     def first(i, carry):
         rows = pl.ds(pl.multiple_of(i * tile, tile), tile)
         normed, inverse = row_norm(x_ref[rows, :].astype(F32) + attn_ref[rows, :])
-        grad = jnp.concatenate([gm_ref[b, i] for b in range(nb)], 0).astype(F32)
+        grad = jnp.concatenate([gm_ref[b, c, i] for b in range(nb) for c in range(CHUNKS)], 0).astype(F32)
         dg2_ref[...] += jnp.sum(grad * normed, 0, keepdims=True)
         back = row_norm_back(grad, normed, inverse, g2_ref[...])
         delta[rows, :] = back
@@ -464,9 +496,9 @@
             dctx[p, rows, :] = grad_ctx[:, p * lanes:(p + 1) * lanes]
         return carry
 
-    lax.fori_loop(0, quarters, first, 0)
-
-    dwo_ref[...] = dot_tn(ctx_ref[...], ga_rows[...])
+    lax.fori_loop(0, quarters, first, 0, unroll=True)
+
+    dw_ref[:, 3 * width:] = dot_tn(ctx_ref[...], ga_rows[...]).astype(BF16)
 
     def attend(p, carry):
         lane0 = pl.multiple_of(p * lanes, lanes)
@@ -511,23 +543,23 @@
         gin_ref[rows, :] = (delta[rows, :] + row_norm_back(grad, normed, inverse, g1_ref[...])).astype(BF16)
         return carry
 
-    lax.fori_loop(0, quarters, last, 0)
+    lax.fori_loop(0, quarters, last, 0, unroll=True)
 
     for c in range(3):
         grads = jnp.concatenate([gqkv[c * pairs + p] for p in range(pairs)], -1)
-        dqkv_ref[:, c * width:(c + 1) * width] = dot_tn(attn_in[...], grads)
-
-
-def attention_backward(gm, cot, x, attn, ctx, qkv, lse, wqkv, wo, g1, g2):
+        dw_ref[:, c * width:(c + 1) * width] = dot_tn(attn_in[...], grads).astype(BF16)
+
+
+def attention_backward(gm, cot, x, attn, ctx, qkv, lse, wqkv, wo, g1, g2, waits=()):
     length, width = x.shape
     pairs = HEADS // 2
     lanes = width // pairs
     return pl.pallas_call(
-        attention_backward_kernel,
+        functools.partial(attention_backward_kernel, len(waits)),
+        in_specs=[pl.BlockSpec(memory_space=pltpu.VMEM)] * 11 + [pl.BlockSpec(memory_space=pl.ANY)] * len(waits),
         out_shape=(
             jax.ShapeDtypeStruct((length, width), BF16),
-            jax.ShapeDtypeStruct((width, 3 * width), F32),
-            jax.ShapeDtypeStruct((width, width), F32),
+            jax.ShapeDtypeStruct((width, 4 * width), BF16),
             jax.ShapeDtypeStruct((1, width), F32),
             jax.ShapeDtypeStruct((1, width), F32),
         ),
@@ -541,9 +573,9 @@
             pltpu.VMEM((length, lanes), F32),
         ],
         compiler_params=pltpu.CompilerParams(vmem_limit_bytes=VMEM_LIMIT),
-        cost_estimate=pl.CostEstimate(flops=35_000_000_000, bytes_accessed=20_000_000, transcendentals=5_000_000),
+        cost_estimate=SMALL_COST,
         name="attention_backward",
-    )(gm, cot, x, attn, ctx, qkv, lse, wqkv, wo, g1, g2)
+    )(gm, cot, x, attn, ctx, qkv, lse, wqkv, wo, g1, g2, *waits)
 
 
 def group_reduce(rows, mem, op, fill):
@@ -567,221 +599,389 @@
     return v * half, slope
 
 
-def moe_kernel(chunk, z_ref, *refs):
-    n = 4
-    xs_in, gs_in = refs[:n], refs[n:2 * n]
-    (ctrl_ref, mem_ref, mkl_ref, take_ref, w1_ref, w2_ref,
-     spread_ref, gm_ref, mixed_ref, geo_ref, hid_ref, gpre_ref, dctrl_ref,
-     xs, gs, logits, gates, weights, eo, gmx, sems) = refs[2 * n:]
+def start(copy):
+    copy.start()
+
+
+def wait(copy):
+    copy.wait()
+
+
+def arrivals(z, sources, sems, base, act, place):
+    n = (len(sources) + 1) // 2
+    act(pltpu.make_async_copy(*place(sources[0], z), sems.at[base]))
+    for k in range(1, n):
+        @pl.when(z >= k)
+        def _():
+            act(pltpu.make_async_copy(*place(sources[k], z - k), sems.at[base + k]))
+
+        @pl.when(z + k < n)
+        def _():
+            act(pltpu.make_async_copy(*place(sources[n - 1 + k], z + k), sems.at[base + n - 1 + k]))
+
+
+def x_rows(xs, m, q, sl):
+    planes, nb, quarters, piece, width = xs.shape
+    return jnp.concatenate([xs[m * sl + s, :, q].reshape(nb * piece, width) for s in range(sl)], 0)
+
+
+def g_rows(gs, m, q, sl):
+    quarters, nb, planes, piece, width = gs.shape
+    return jnp.concatenate([gs[q, :, m * sl + s].reshape(nb * piece, width) for s in range(sl)], 0)
+
+
+def mixture_forward_kernel(chunk, parts, waits, z_ref, *refs):
+    x_in, refs = refs[:parts], refs[parts + waits:]
+    (a_in, ctrl_ref, mem_ref, mkl_ref, take_ref, w1_ref, w2_ref,
+     spread_ref, mixed_ref, hid_ref, slope_ref, eo_ref, weights_ref, gates_ref,
+     xs, attn, logits, sems) = refs
     planes, nb, quarters, piece, width = xs.shape
     micro = mem_ref.shape[0]
     sl = planes // micro
-    lanes = mem_ref.shape[2]
     experts = mixed_ref.shape[0]
     rows = mkl_ref.shape[1]
-    halves = piece // PB
-    per_micro = quarters * halves
     e = pl.program_id(0)
-
-    def x_block(m, q, h):
-        at = pl.ds(pl.multiple_of(h * PB, PB), PB)
-        return jnp.concatenate(
-            [xs[m * sl + s, :, q, at, :].reshape(nb * PB, width) for s in range(sl)], 0)
-
-    def g_block(m, q, h):
-        at = pl.ds(pl.multiple_of(h * PB, PB), PB)
-        return jnp.concatenate(
-            [gs[q, :, m * sl + s, at, :].reshape(nb * PB, width) for s in range(sl)], 0)
-
-    def store_block(ref, m, q, h, value):
-        at = pl.ds(pl.multiple_of(h * PB, PB), PB)
-        for s in range(sl):
-            part = value[s * nb * PB:(s + 1) * nb * PB].reshape(nb, PB, width)
-            ref[m * sl + s, :, q, at, :] = part
+    z = z_ref[0]
+    x_place = lambda ref, plane: (ref, xs.at[plane])
+    a_copy = pltpu.make_async_copy(a_in.at[:, 1 + chunk], attn, sems.at[parts])
 
     @pl.when(e == 0)
     def _():
-        z = z_ref[0]
-        for k in range(n):
-            source = lax.rem(z - k + n, n)
-            pltpu.make_async_copy(xs_in[k], xs.at[source], sems.at[k]).start()
-        for k in range(n):
-            source = lax.rem(z - k + n, n)
-
-            @pl.when(source // quarters == chunk)
-            def _():
-                slot = gs.at[lax.rem(source, quarters)]
-                pltpu.make_async_copy(gs_in[k], slot, sems.at[n + k]).start()
-
-        for k in range(n):
-            source = lax.rem(z - k + n, n)
-            pltpu.make_async_copy(xs_in[k], xs.at[source], sems.at[k]).wait()
-
+        arrivals(z, x_in, sems, 0, start, x_place)
+        a_copy.start()
+        arrivals(z, x_in, sems, 0, wait, x_place)
         for m in range(micro):
-            def score(i, carry):
-                block = x_block(m, i // halves, lax.rem(i, halves))
-                at = pl.ds(pl.multiple_of(i * 8, 8), 8)
-                logits[m, at, :] = dot_nt(ctrl_ref[...], block)[:8]
-                return carry
-
-            lax.fori_loop(0, per_micro, score, 0)
+            for q in range(quarters):
+                logits[m, q * 8:(q + 1) * 8, :] = dot_nt(ctrl_ref[...], x_rows(xs, m, q, sl))[:8]
             mem = mem_ref[m]
             taking = take_ref[m] > 0
             values = logits[m]
             high = group_reduce(jnp.where(taking, values, NEG_FILL), mem, jnp.maximum, NEG_FILL)
             scaled = jnp.where(taking, jnp.exp(values - high), 0.0)
-            gates[m] = scaled / group_reduce(scaled, mem, jnp.add, 0.0)
-
-        for k in range(n):
-            source = lax.rem(z - k + n, n)
-
-            @pl.when(source // quarters == chunk)
-            def _():
-                slot = gs.at[lax.rem(source, quarters)]
-                pltpu.make_async_copy(gs_in[k], slot, sems.at[n + k]).wait()
-
+            gates_ref[m] = scaled / group_reduce(scaled, mem, jnp.add, 0.0)
         for m in range(micro):
-            def blend(i, carry):
-                q, h = i // halves, lax.rem(i, halves)
-                block = m * per_micro + i
-                own = gates[m, pl.ds(pl.multiple_of(i * 8, 8), 8), :]
+            for q in range(quarters):
+                block = m * quarters + q
+                own = gates_ref[m, q * 8:(q + 1) * 8, :]
                 w = jnp.concatenate(
                     [(mkl_ref[m] * own[j:j + 1, :]).astype(BF16) for j in range(experts)], 0)
-                weights[block] = w
-                blended = dot_nn(w, x_block(m, q, h)).astype(BF16)
-                grads = dot_nn(w, g_block(m, q, h)).astype(BF16)
-                at = pl.ds(pl.multiple_of(block * rows, rows), rows)
+                weights_ref[block] = w
+                blended = dot_nn(w, x_rows(xs, m, q, sl)).astype(BF16)
                 for j in range(experts):
-                    mixed_ref[j, at, :] = blended[j * rows:(j + 1) * rows]
-                    geo_ref[j, at, :] = grads[j * rows:(j + 1) * rows]
-                return carry
-
-            lax.fori_loop(0, per_micro, blend, 0)
-
-    hidden_size = w1_ref.shape[2]
-    step = 512
-    blended, grads = mixed_ref[e], geo_ref[e]
-    out_sum = jnp.zeros(blended.shape, F32)
-    back_sum = jnp.zeros(blended.shape, F32)
-    for f in range(0, hidden_size, step):
-        first, second = w1_ref[0, :, f:f + step], w2_ref[0, f:f + step, :]
-        value, slope = gelu_both(dot_nn(blended, first))
-        hidden = value.astype(BF16)
-        hid_ref[0, :, f:f + step] = hidden
-        out_sum += dot_nn(hidden, second)
-        grad_pre = (dot_nt(grads, second) * slope).astype(BF16)
-        gpre_ref[0, :, f:f + step] = grad_pre
-        back_sum += dot_nt(grad_pre, first)
-    eo[e] = out_sum.astype(BF16)
-    gmx[e] = back_sum.astype(BF16)
+                    mixed_ref[j, block * rows:(block + 1) * rows, :] = blended[j * rows:(j + 1) * rows]
+
+    value, slope = gelu_both(dot_nn(mixed_ref[e], w1_ref[0]))
+    hidden = value.astype(BF16)
+    hid_ref[0] = hidden
+    slope_ref[0] = slope.astype(BF16)
+    eo_ref[e] = dot_nn(hidden, w2_ref[0]).astype(BF16)
 
     @pl.when(e == experts - 1)
     def _():
-        dctrl_ref[...] = jnp.zeros_like(dctrl_ref)
-        ctrl8 = ctrl_ref[:8, :]
-        ctrl_twice = jnp.concatenate([ctrl8.astype(F32), ctrl8.astype(F32)], 0).astype(BF16)
         for m in range(micro):
-            def spread_out(i, carry):
-                q, h = i // halves, lax.rem(i, halves)
-                block = m * per_micro + i
-                at = pl.ds(pl.multiple_of(block * rows, rows), rows)
-                outs = jnp.concatenate([eo[j, at, :] for j in range(experts)], 0)
+            for q in range(quarters):
+                block = m * quarters + q
+                outs = jnp.concatenate(
+                    [eo_ref[j, block * rows:(block + 1) * rows, :] for j in range(experts)], 0)
+                spread = dot_tn(weights_ref[block], outs).astype(BF16)
+                for s in range(sl):
+                    at = slice(s * nb * PB, (s + 1) * nb * PB)
+                    spread_ref[q, :, m * sl + s] = spread[at].reshape(nb, PB, width)
+        a_copy.wait()
+        for q in range(quarters):
+            spread_ref[q, :, z] = (spread_ref[q, :, z].astype(F32) + attn[:, q].astype(F32)).astype(BF16)
+
+
+def mixture_backward_kernel(chunk, parts, waits, z_ref, *refs):
+    x_in, g_in, refs = refs[:parts], refs[parts:2 * parts], refs[2 * parts + waits:]
+    (ctrl_ref, mem_ref, mkl_ref, weights_ref, gates_ref, eo_ref, slope_ref, w1_ref, w2_ref,
+     gm_ref, geo_ref, gpre_ref, dctrl_ref, xs, gs, gmx, sems) = refs
+    planes, nb, quarters, piece, width = xs.shape
+    micro, _, lanes = mem_ref.shape
+    sl = planes // micro
+    experts = geo_ref.shape[0]
+    rows = mkl_ref.shape[1]
+    e = pl.program_id(0)
+    z = z_ref[0]
+    mine = pl.ds(chunk * PB, PB)
+    x_place = lambda ref, plane: (ref, xs.at[plane])
+    g_place = lambda ref, plane: (ref.at[:, :, mine, :], gs.at[plane])
+
+    @pl.when(e == 0)
+    def _():
+        arrivals(z, g_in, sems, 0, start, g_place)
+        arrivals(z, x_in, sems, parts, start, x_place)
+        arrivals(z, g_in, sems, 0, wait, g_place)
+        for m in range(micro):
+            for q in range(quarters):
+                block = m * quarters + q
+                grads = dot_nn(weights_ref[block], g_rows(gs, m, q, sl)).astype(BF16)
+                for j in range(experts):
+                    geo_ref[j, block * rows:(block + 1) * rows, :] = grads[j * rows:(j + 1) * rows]
+        arrivals(z, x_in, sems, parts, wait, x_place)
+
+    grad_pre = (dot_nt(geo_ref[e], w2_ref[0]) * slope_ref[0].astype(F32)).astype(BF16)
+    gpre_ref[0] = grad_pre
+    gmx[e] = dot_nt(grad_pre, w1_ref[0]).astype(BF16)
+
+    @pl.when(e == experts - 1)
+    def _():
+        dctrl = jnp.zeros(dctrl_ref.shape, F32)
+        ctrl8 = ctrl_ref[:8, :].astype(F32)
+        ctrl_twice = jnp.concatenate([ctrl8, ctrl8], 0).astype(BF16)
+        for m in range(micro):
+            for q in range(quarters):
+                block = m * quarters + q
+                at = slice(block * rows, (block + 1) * rows)
+                outs = jnp.concatenate([eo_ref[j, at, :] for j in range(experts)], 0)
                 backs = jnp.concatenate([gmx[j, at, :] for j in range(experts)], 0)
-                w = weights[block]
-                x_rows, g_rows = x_block(m, q, h), g_block(m, q, h)
-                store_block(spread_ref, m, q, h, dot_tn(w, outs).astype(BF16))
-                dots = dot_nt(outs, g_rows) + dot_nt(backs, x_rows)
+                w = weights_ref[block]
+                inputs = x_rows(xs, m, q, sl)
+                dots = dot_nt(outs, g_rows(gs, m, q, sl)) + dot_nt(backs, inputs)
                 grad_gates = [
                     jnp.sum(dots[j * rows:(j + 1) * rows] * mkl_ref[m], 0, keepdims=True)
                     for j in range(experts)]
                 if experts < 8:
                     grad_gates.append(jnp.zeros((8 - experts, lanes), F32))
                 grad_gates = jnp.concatenate(grad_gates, 0)
-                own = gates[m, pl.ds(pl.multiple_of(i * 8, 8), 8), :]
+                own = gates_ref[m, q * 8:(q + 1) * 8, :]
                 inner = group_reduce(own * grad_gates, mem_ref[m], jnp.add, 0.0)
                 grad_logits = own * (grad_gates - inner)
                 upper = grad_logits.astype(BF16).astype(F32)
                 both = jnp.concatenate([upper, grad_logits - upper], 0).astype(BF16)
-                grad_mix = dot_tn(w, backs) + dot_tn(both, ctrl_twice)
-                store_block(gm_ref, m, q, h, grad_mix.astype(BF16))
-                dctrl_ref[...] += dot_nn(both, x_rows)
-                return carry
-
-            lax.fori_loop(0, per_micro, spread_out, 0)
-
-
-def moe(chunk, z, x_parts, g_parts, ctrl, mem, mkl, take, w1, w2):
-    planes = len(x_parts)
+                grad_mix = (dot_tn(w, backs) + dot_tn(both, ctrl_twice)).astype(BF16)
+                for s in range(sl):
+                    part = slice(s * nb * PB, (s + 1) * nb * PB)
+                    gm_ref[m * sl + s, :, q] = grad_mix[part].reshape(nb, PB, width)
+                dctrl += dot_nn(both, inputs)
+        dctrl_ref[...] = dctrl
+
+
+def whole(shape):
+    return pl.BlockSpec(shape, lambda e: (0,) * len(shape))
+
+
+def by_expert(shape):
+    return pl.BlockSpec((1,) + shape[1:], lambda e: (e, 0, 0))
+
+
+def mixture_sizes(x_parts, mem, mkl, w1):
     nb, quarters, piece, width = x_parts[0].shape
-    micro, groups, lanes = mem.shape
+    planes = quarters
     experts, _, hidden_size = w1.shape
-    rows = mkl.shape[1]
-    blocks = micro * quarters * (piece // PB)
-    total = blocks * rows
-    whole = lambda shape: pl.BlockSpec(shape, lambda e: (0,) * len(shape))
-    back_shape = (planes, nb, quarters, piece, width)
+    total = mem.shape[0] * quarters * mkl.shape[1]
+    back = (planes, nb, quarters, piece, width)
+    return back, (experts, total, width), (experts, total, hidden_size)
+
+
+def mixture_forward(chunk, z, x_parts, a_all, ctrl, mem, mkl, take, w1, w2, waits=()):
+    back, narrow, wide = mixture_sizes(x_parts, mem, mkl, w1)
+    micro, _, lanes = mem.shape
+    quarters = back[2]
+    weights = (micro * quarters, narrow[0] * mkl.shape[1], lanes)
+    gates = (micro, quarters * 8, lanes)
     any_spec = pl.BlockSpec(memory_space=pl.ANY)
-    flops = experts * total * width * hidden_size * 8 + 4_000_000_000
     return pl.pallas_call(
-        functools.partial(moe_kernel, chunk),
-        grid=(experts,),
+        functools.partial(mixture_forward_kernel, chunk, len(x_parts), len(waits)),
+        grid=(narrow[0],),
         out_shape=(
-            jax.ShapeDtypeStruct(back_shape, BF16),
-            jax.ShapeDtypeStruct(back_shape, BF16),
-            jax.ShapeDtypeStruct((experts, total, width), BF16),
-            jax.ShapeDtypeStruct((experts, total, width), BF16),
-            jax.ShapeDtypeStruct((experts, total, hidden_size), BF16),
-            jax.ShapeDtypeStruct((experts, total, hidden_size), BF16),
-            jax.ShapeDtypeStruct((16, width), F32),
+            jax.ShapeDtypeStruct(back, BF16),
+            jax.ShapeDtypeStruct(narrow, BF16),
+            jax.ShapeDtypeStruct(wide, BF16),
+            jax.ShapeDtypeStruct(wide, BF16),
+            jax.ShapeDtypeStruct(narrow, BF16),
+            jax.ShapeDtypeStruct(weights, BF16),
+            jax.ShapeDtypeStruct(gates, F32),
         ),
-        in_specs=[pl.BlockSpec(memory_space=pltpu.SMEM)] + [any_spec] * (2 * planes) + [
-            whole(ctrl.shape), whole(mem.shape), whole(mkl.shape), whole(take.shape),
-            pl.BlockSpec((1, width, hidden_size), lambda e: (e, 0, 0)),
-            pl.BlockSpec((1, hidden_size, width), lambda e: (e, 0, 0)),
-        ],
-        out_specs=(
-            whole(back_shape), whole(back_shape),
-            whole((experts, total, width)), whole((experts, total, width)),
-            pl.BlockSpec((1, total, hidden_size), lambda e: (e, 0, 0)),
-            pl.BlockSpec((1, total, hidden_size), lambda e: (e, 0, 0)),
-            whole((16, width)),
-        ),
+        in_specs=[pl.BlockSpec(memory_space=pltpu.SMEM)]
+        + [any_spec] * (len(x_parts) + len(waits) + 1)
+        + [whole(ctrl.shape), whole(mem.shape), whole(mkl.shape), whole(take.shape),
+           by_expert(w1.shape), by_expert(w2.shape)],
+        out_specs=(whole(back), whole(narrow), by_expert(wide), by_expert(wide),
+                   whole(narrow), whole(weights), whole(gates)),
         scratch_shapes=[
-            pltpu.VMEM(back_shape, BF16),
-            pltpu.VMEM((quarters, nb, planes, piece, width), BF16),
-            pltpu.VMEM((micro, blocks // micro * 8, lanes), F32),
-            pltpu.VMEM((micro, blocks // micro * 8, lanes), F32),
-            pltpu.VMEM((blocks, experts * rows, lanes), BF16),
-            pltpu.VMEM((experts, total, width), BF16),
-            pltpu.VMEM((experts, total, width), BF16),
-            pltpu.SemaphoreType.DMA((2 * planes,)),
+            pltpu.VMEM(back, BF16),
+            pltpu.VMEM(back[1:], BF16),
+            pltpu.VMEM(gates, F32),
+            pltpu.SemaphoreType.DMA((len(x_parts) + 1,)),
         ],
         compiler_params=pltpu.CompilerParams(vmem_limit_bytes=VMEM_LIMIT),
-        cost_estimate=pl.CostEstimate(flops=flops, bytes_accessed=50_000_000, transcendentals=experts * total * hidden_size),
-        name="mixture",
-    )(z, *x_parts, *g_parts, ctrl, mem, mkl, take, w1, w2)
-
-
-def ring(count):
-    return [(i, (i + 1) % count) for i in range(count)]
-
-
-def ring_gather(block, count):
-    parts = [block]
-    for _ in range(count - 1):
-        parts.append(lax.ppermute(parts[-1], "expert", ring(count)))
-    return parts
-
-
-def ring_scatter(parts, z, count):
-    def own(step):
-        return lax.dynamic_index_in_dim(parts, lax.rem(z - step + 2 * count, count), 0, keepdims=False)
-
-    held = own(1)
+        cost_estimate=KERNEL_COST,
+        name="mixture_forward",
+    )(z, *x_parts, *waits, a_all, ctrl, mem, mkl, take, w1, w2)
+
+
+def mixture_backward(chunk, z, x_parts, g_parts, ctrl, mem, mkl, weights, gates, eo, slope, w1, w2, waits=()):
+    back, narrow, wide = mixture_sizes(x_parts, mem, mkl, w1)
+    parts = len(x_parts)
+    any_spec = pl.BlockSpec(memory_space=pl.ANY)
+    return pl.pallas_call(
+        functools.partial(mixture_backward_kernel, chunk, parts, len(waits)),
+        grid=(narrow[0],),
+        out_shape=(
+            jax.ShapeDtypeStruct(back, BF16),
+            jax.ShapeDtypeStruct(narrow, BF16),
+            jax.ShapeDtypeStruct(wide, BF16),
+            jax.ShapeDtypeStruct((16, back[4]), F32),
+        ),
+        in_specs=[pl.BlockSpec(memory_space=pltpu.SMEM)]
+        + [any_spec] * (2 * parts + len(waits))
+        + [whole(ctrl.shape), whole(mem.shape), whole(mkl.shape), whole(weights.shape),
+           whole(gates.shape), whole(narrow), by_expert(wide), by_expert(w1.shape), by_expert(w2.shape)],
+        out_specs=(whole(back), whole(narrow), by_expert(wide), whole((16, back[4]))),
+        scratch_shapes=[
+            pltpu.VMEM(back, BF16),
+            pltpu.VMEM(back, BF16),
+            pltpu.VMEM(narrow, BF16),
+            pltpu.SemaphoreType.DMA((2 * parts,)),
+        ],
+        compiler_params=pltpu.CompilerParams(vmem_limit_bytes=VMEM_LIMIT),
+        cost_estimate=KERNEL_COST,
+        name="mixture_backward",
+    )(z, *x_parts, *g_parts, *waits, ctrl, mem, mkl, weights, gates, eo, slope, w1, w2)
+
+
+def own_cotangent_kernel(parts, z_ref, *refs):
+    g_in, (cot_ref, sems) = refs[:parts], refs[-2:]
+    z = z_ref[0]
+    place = lambda ref, plane: (ref.at[:, z], cot_ref.at[:, plane])
+    arrivals(z, g_in, sems, 0, start, place)
+    arrivals(z, g_in, sems, 0, wait, place)
+
+
+def own_cotangent(z, g_parts, waits=()):
+    nb, planes, piece, width = g_parts[0].shape
+    any_spec = pl.BlockSpec(memory_space=pl.ANY)
+    return pl.pallas_call(
+        functools.partial(own_cotangent_kernel, len(g_parts)),
+        out_shape=jax.ShapeDtypeStruct((nb, planes, piece, width), BF16),
+        in_specs=[pl.BlockSpec(memory_space=pltpu.SMEM)] + [any_spec] * (len(g_parts) + len(waits)),
+        scratch_shapes=[pltpu.SemaphoreType.DMA((len(g_parts),))],
+        cost_estimate=SMALL_COST,
+        compiler_params=pltpu.CompilerParams(vmem_limit_bytes=VMEM_LIMIT),
+        name="own_cotangent",
+    )(z, *g_parts, *waits)
+
+
+def weight_grads_kernel(z_ref, m0, m1, p0, p1, h0, h1, o0, o1, *refs):
+    keep_ref, send_ref = refs[-2:]
+    width, step = keep_ref.shape[-2:]
+    crossed = pl.program_id(0) >= pl.num_programs(0) // 2
+    core = lax.rem(z_ref[1], 2)
+    left1 = m0[0].T, m1[0].T
+    left2 = o0[0].T, o1[0].T
+    for t in range(p0.shape[2] // step // 2):
+        x, y = t % 2, t // 2
+        hop1, hop2 = jnp.where(crossed, y, x), jnp.where(crossed, x, y)
+        for ref, part in ((keep_ref, core), (send_ref, 1 - core)):
+            at = pl.ds(pl.multiple_of((2 * t + part) * step, step), step)
+            first = dot_nn(left1[0], p0[0, :, at]) + dot_nn(left1[1], p1[0, :, at])
+            ref[0, 0, hop1, hop2, 0] = first.astype(BF16)
+            second = dot_nn(left2[0], h0[0, :, at]) + dot_nn(left2[1], h1[0, :, at])
+            ref[0, 0, hop1, hop2, 1] = second.astype(BF16)
+
+
+def weight_grads(z, mixed, gpre, hid, geo, nb, waits=()):
+    experts, total, width = mixed[0].shape
+    hidden_size = gpre[0].shape[2]
+    step = hidden_size // nb
+    half = experts // 2
+    row = pl.BlockSpec((1, total, width), lambda e: (e, 0, 0))
+    wide = pl.BlockSpec((1, total, hidden_size), lambda e: (e, 0, 0))
+    out = pl.BlockSpec((1, 1, 2, 2, 2, width, step), lambda e: (e // half, e % half, 0, 0, 0, 0, 0))
+    return pl.pallas_call(
+        weight_grads_kernel,
+        grid=(experts,),
+        in_specs=[pl.BlockSpec(memory_space=pltpu.SMEM)]
+        + [row] * 2 + [wide] * 4 + [row] * 2 + [pl.BlockSpec(memory_space=pl.ANY)] * len(waits),
+        out_shape=(jax.ShapeDtypeStruct((2, half, 2, 2, 2, width, step), BF16),) * 2,
+        out_specs=(out, out),
+        compiler_params=pltpu.CompilerParams(vmem_limit_bytes=VMEM_LIMIT),
+        cost_estimate=SMALL_COST,
+        name="weight_grads",
+    )(z, *mixed, *gpre, *hid, *geo, *waits)
+
+
+def pick(parts, index):
+    return lax.dynamic_index_in_dim(parts, index, 0, keepdims=False)
+
+
+def pass_on(*refs):
+    pass
+
+
+def after(value, *others):
+    spec = pl.BlockSpec(memory_space=pl.ANY)
+    return pl.pallas_call(
+        pass_on,
+        out_shape=jax.ShapeDtypeStruct(value.shape, value.dtype),
+        in_specs=[spec] * (1 + len(others)),
+        out_specs=spec,
+        input_output_aliases={0: 0},
+        name="after",
+        cost_estimate=SMALL_COST,
+    )(value, *others)
+
+
+def line_step(ups, downs, count):
+    up = [(i, i + 1) for i in range(count - 1)]
+    down = [(i + 1, i) for i in range(count - 1)]
+    return (ups + [lax.ppermute(ups[-1], "expert", up)],
+            downs + [lax.ppermute(downs[-1], "expert", down)])
+
+
+def line_scatter(parts, z, count):
+    up = [(i, i + 1) for i in range(count - 1)]
+    down = [(i + 1, i) for i in range(count - 1)]
+
+    def own(index):
+        return pick(parts, jnp.clip(index, 0, count - 1)).astype(F32)
+
+    rising, falling = own(z + count - 1).astype(BF16), own(z - count + 1).astype(BF16)
     for step in range(1, count):
-        held = lax.ppermute(held, "expert", ring(count))
-        held = (held.astype(F32) + own(step + 1).astype(F32)).astype(BF16)
-    return held
+        rising = lax.ppermute(rising, "expert", up).astype(F32)
+        falling = lax.ppermute(falling, "expert", down).astype(F32)
+        if step < count - 1:
+            rising = (rising + own(z + count - 1 - step)).astype(BF16)
+            falling = (falling + own(z - count + 1 + step)).astype(BF16)
+    return (rising + falling + own(z)).astype(BF16)
+
+
+def to_planes(parts, z, count):
+    got = [pick(parts, z)]
+    for k in range(1, count):
+        part = pick(parts, lax.rem(z + k, count))
+        got.append(lax.ppermute(part, "expert", [(i, (i + k) % count) for i in range(count)]))
+    return got
+
+
+def swap_halves(blocks, bit, count):
+    mine = lax.rem(lax.axis_index("batch") >> bit, 2)
+    other = lax.ppermute(pick(blocks, 1 - mine), "batch", [(i, i ^ (1 << bit)) for i in range(count)])
+    return (pick(blocks, mine).astype(F32) + other.astype(F32)).astype(BF16)
+
+
+def first_halves(keep, came):
+    own = lax.axis_index("batch")
+    mine = [lax.rem(own >> bit, 2) for bit in (1, 2)]
+
+    def part(half, expert, index):
+        return (pick(keep[half, expert], index).astype(F32) + pick(came[half, expert], index).astype(F32)).astype(BF16)
+
+    experts = range(keep.shape[1])
+    return ([[part(i, e, mine[i]) for e in experts] for i in range(2)],
+            [[part(i, e, 1 - mine[i]) for e in experts] for i in range(2)])
+
+
+def hop(keep, send, bit):
+    came = lax.ppermute(send, "batch", [(j, j ^ (1 << bit)) for j in range(8)])
+    return (keep.astype(F32) + came.astype(F32)).astype(BF16)
+
+
+def second_hop(held):
+    both = [swap_halves(part, 2 - i, 8) for i in range(2) for part in held[i]]
+    both = jnp.stack(both).astype(F32)
+    return both[:, 0], both[:, 1].transpose(0, 2, 1)
 
 
 def body(
@@ -804,22 +1004,29 @@
     seqs = live.shape[1]
     z = lax.axis_index("expert")
     piece = local_len // nb
-    if micro * sl != planes or piece % PB:
+    if micro * sl != planes or piece != CHUNKS * PB or nb != 8:
         return body_by_position(
             tokens, cotangent, query_key_value_weight, output_weight, controller_weight,
             w_first, w_second, gain_one, gain_two, group_sizes, live)
     g1, g2 = gain_one.reshape(1, width), gain_two.reshape(1, width)
 
-    sent = tokens.astype(BF16).reshape(planes, local_len, width)
-    x = lax.all_to_all(sent, "expert", split_axis=0, concat_axis=0, tiled=True)
-    x = x.reshape(planes * local_len, width)
-
-    cot = cotangent.astype(BF16).reshape(planes, nb, piece, width).transpose(1, 0, 2, 3)
-    cot = lax.all_to_all(cot, "batch", split_axis=0, concat_axis=0, tiled=True)
-    cot_parts = ring_gather(cot, planes)
-
-    qkv, lse, ctx, attn, mix = attention_forward(
-        x, query_key_value_weight, output_weight, g1, g2, nb, planes)
+    own = lax.axis_index("batch")
+    z_arr = jnp.stack([z, own]).astype(jnp.int32)
+    x_parts = to_planes(tokens.reshape(planes, local_len, width).astype(BF16), z, planes)
+
+    cot = cotangent.reshape(planes, nb, piece, width)
+    pieces = []
+    for k in range(nb):
+        part = lax.dynamic_index_in_dim(cot, own ^ k, 1, keepdims=False).astype(BF16)
+        if k:
+            part = lax.ppermute(part, "batch", [(i, i ^ k) for i in range(nb)])
+        pieces.append(part)
+    pieces[1] = after(pieces[1], *x_parts[1:])
+    cot = jnp.take(jnp.stack(pieces), own ^ jnp.arange(nb), axis=0)
+    g_up, g_down = line_step([cot], [cot], planes)
+
+    x, qkv, lse, ctx, attn, mix, more = attention_forward(
+        z_arr, x_parts, query_key_value_weight, output_weight, g1, g2, nb)
 
     member, taking = jax.vmap(group_tables)(group_sizes, live)
     groups = member.shape[2]
@@ -832,54 +1039,85 @@
     mkl = (mem[:, :, None, :] * same).reshape(micro, groups * PB, seqs * PB)
     ctrl = lax.dynamic_slice_in_dim(controller_weight, z * experts, experts, 1).T
     ctrl = jnp.pad(ctrl, ((0, 16 - experts), (0, 0)))
-    z_arr = z.astype(jnp.int32).reshape(1)
-
-    quarters = planes // CHUNKS
-    spreads, backs, kept, dctrl = [], [], [], 0.0
-    for c in range(CHUNKS):
-        own = lax.all_to_all(
-            mix[:, c * quarters:(c + 1) * quarters], "batch", split_axis=0, concat_axis=0, tiled=True)
-        x_parts = ring_gather(own, planes)
-        spread, back, mixed, geo, hid, gpre, dc = moe(
-            c, z_arr, x_parts, cot_parts, ctrl, mem, mkl, take, w_first, w_second)
-        back = ring_scatter(back, z, planes)
-        backs.append(lax.all_to_all(back, "batch", split_axis=0, concat_axis=0, tiled=True))
-        spread = ring_scatter(spread, z, planes)
-        spreads.append(lax.all_to_all(spread, "batch", split_axis=0, concat_axis=0, tiled=True))
-        kept.append((mixed, geo, hid, gpre))
-        dctrl = dctrl + dc[:8] + dc[8:]
-    back = jnp.concatenate(backs, 1)
-    spread = jnp.concatenate(spreads, 1)
-
-    mixed, geo, hid, gpre = [jnp.concatenate(parts, 1) for parts in zip(*kept)]
-    sum_first = jnp.einsum("erd,erf->edf", mixed, gpre, preferred_element_type=F32).astype(BF16)
-    sum_second = jnp.einsum("erf,erd->efd", hid, geo, preferred_element_type=F32).astype(BF16)
-    grad_first = lax.psum_scatter(sum_first, "batch", scatter_dimension=2, tiled=True).astype(F32)
-    grad_second = lax.psum_scatter(sum_second, "batch", scatter_dimension=1, tiled=True).astype(F32)
-
-    cot_all = jnp.stack(cot_parts)
-    order = lax.rem(z - jnp.arange(planes) + planes, planes)
-    cot_own = lax.dynamic_index_in_dim(cot_all, z, 2, keepdims=False)
-    cot_own = jnp.take(cot_own, order, axis=0).transpose(1, 0, 2, 3)
-    cot_own = lax.all_to_all(cot_own, "batch", split_axis=0, concat_axis=0, tiled=True)
-
-    gin, dqkv, dwo, dg1, dg2 = attention_backward(
-        back, cot_own, x, attn, ctx, qkv, lse, query_key_value_weight, output_weight, g1, g2)
-
-    spread = spread.transpose(1, 0, 2, 3).reshape(planes, local_len, width)
-    out = (attn.reshape(planes, local_len, width) + spread.astype(F32)).astype(BF16)
-    out = lax.all_to_all(out, "expert", split_axis=0, concat_axis=0, tiled=True)
-    out = tokens + out.reshape(tokens.shape).astype(F32)
-    gin = lax.all_to_all(
-        gin.reshape(planes, local_len, width), "expert", split_axis=0, concat_axis=0, tiled=True)
+
+    def over_batch(block):
+        return lax.all_to_all(block, "batch", split_axis=0, concat_axis=0, tiled=True)
+
+    def over_expert(blocks):
+        return lax.all_to_all(blocks, "expert", split_axis=0, concat_axis=0, tiled=True)
+
+    own0 = over_batch(after(mix, g_up[1], g_down[1]))
+    g_up, g_down = line_step(g_up, g_down, planes)
+    up0, down0 = line_step([own0], [own0], planes)
+    more = over_batch(after(more, own0))
+    own1 = more[:, 0]
+    up1, down1 = line_step([own1], [own1], planes)
+    up0, down0 = line_step(up0, down0, planes)
+    up0[-1] = after(up0[-1], up1[-1], down1[-1])
+    g_up[-1] = after(g_up[-1], up0[-2], down0[-2])
+    g_up, g_down = line_step(g_up, g_down, planes)
+    up0, down0 = line_step(up0, down0, planes)
+    up1, down1 = line_step(up1, down1, planes)
+    second = up1[-1], down1[-1]
+    up1, down1 = line_step(up1, down1, planes)
+    g_parts = g_up + g_down[1:]
+    x0, x1 = up0 + down0[1:], up1 + down1[1:]
+
+    spread0, mixed0, hid0, slope0, eo0, weights0, gates0 = mixture_forward(
+        0, z_arr, x0, more, ctrl, mem, mkl, take, w_first, w_second)
+    cot_picked = own_cotangent(z_arr, g_parts, waits=(eo0,) + second)
+    spread0 = lax.psum_scatter(after(spread0, cot_picked), "expert", scatter_dimension=0, tiled=False)
+    cot_own = over_batch(cot_picked)
+    back0, geo0, gpre0, dctrl0 = mixture_backward(
+        0, z_arr, x0, g_parts, ctrl, mem, mkl, weights0, gates0, eo0, slope0, w_first, w_second,
+        waits=(cot_picked,))
+    back0 = over_expert(after(back0, cot_own, up1[-1], down1[-1]))
+    spread1, mixed1, hid1, slope1, eo1, weights1, gates1 = mixture_forward(
+        1, z_arr, x1, more, ctrl, mem, mkl, take, w_first, w_second, waits=(dctrl0, spread0))
+    back1, geo1, gpre1, dctrl1 = mixture_backward(
+        1, z_arr, x1, g_parts, ctrl, mem, mkl, weights1, gates1, eo1, slope1, w_first, w_second)
+    back0 = after(back0, dctrl1)
+    back1 = after(back1, back0)
+    dctrl = dctrl0[:8] + dctrl0[8:] + dctrl1[:8] + dctrl1[8:]
+    keep, send = weight_grads(
+        z_arr, (mixed0, mixed1), (gpre0, gpre1), (hid0, hid1), (geo0, geo1), nb, waits=(back1,))
+    back1 = after(over_expert(back1), send)
+    spread1 = lax.psum_scatter(after(spread1, back1), "expert", scatter_dimension=0, tiled=False)
+    back = jnp.stack([back0, back1], 2)
+    back = jnp.sum(back.astype(F32), 0).astype(BF16)
+    back = over_batch(back)
+    came = lax.ppermute(after(send, back1), "batch", [(i, i ^ 1) for i in range(nb)])
+    keeps, sends = first_halves(keep, came)
+
+    gin, dw, dg1, dg2 = attention_backward(
+        back, cot_own, x, attn, ctx, qkv, lse, query_key_value_weight, output_weight, g1, g2,
+        waits=tuple(sends[0] + sends[1]))
+    held = [[hop(keeps[i][e], sends[i][e], 1 + i) for e in range(len(sends[i]))] for i in range(2)]
+    gin = after(gin, held[0][0], held[1][0])
+    dw = after(dw, held[0][0], held[1][0])
+    grad_first, grad_second = second_hop(held)
+
+    got = jnp.stack(to_planes(gin.reshape(planes, local_len, width), z, planes))
+    gin = jnp.take(got, lax.rem(z - jnp.arange(planes) + planes, planes), axis=0)
     grad_in = cotangent + gin.reshape(tokens.shape).astype(F32)
 
     dctrl_all = jnp.zeros((planes, experts, width), F32)
     dctrl_all = lax.dynamic_update_slice(dctrl_all, dctrl[None, :experts], (z, 0, 0))
     dctrl_all = dctrl_all.reshape(planes * experts, width).T
-    axes = ("batch", "expert")
-    flat = jnp.concatenate([dqkv, dwo, dctrl_all, dg1.T, dg2.T], 1)
-    flat = lax.psum_scatter(flat, axes, scatter_dimension=0, tiled=True)
+    extra = jnp.concatenate([dctrl_all, dg1.T, dg2.T], 1)
+    extra = jnp.pad(extra, ((0, 0), (0, 128 - extra.shape[1]))).astype(BF16)
+    flat = jnp.concatenate([dw, extra], 1)
+    flat = flat.reshape(nb // 2, 2, -1, flat.shape[1]).transpose(1, 0, 2, 3)
+    flat = swap_halves(flat, 0, nb)
+    chips = [[c + 2 * i for i in range(nb // 2)] for c in range(2)]
+    flat = lax.all_to_all(flat, "batch", split_axis=0, concat_axis=0, tiled=True, axis_index_groups=chips)
+    flat = jnp.sum(flat.astype(F32), 0).astype(BF16)
+    spread = jnp.stack([after(spread0, flat), spread1], 1)
+    spread = over_batch(spread)
+    out = tokens + spread.transpose(2, 0, 1, 3, 4).reshape(tokens.shape).astype(F32)
+    flat = flat.reshape(planes, -1, flat.shape[1])
+    flat = lax.all_to_all(flat, "expert", split_axis=0, concat_axis=0, tiled=True)
+    flat = jnp.sum(flat.astype(F32), 0)
     ends = [3 * width, 4 * width, 4 * width + planes * experts]
     grad_qkv, grad_out, grad_ctrl = flat[:, :ends[0]], flat[:, ends[0]:ends[1]], flat[:, ends[1]:ends[2]]
     return (out, grad_in, grad_qkv, grad_out, grad_ctrl, grad_first, grad_second,

time: 791 us -> 542 us (0.69)
  waiting for transfers between devices: 440 us -> 118 us
  starting transfers between devices: 38.4 us -> 118 us
  blocking collectives: 57.4 us -> 13.9 us
  Pallas kernels: 134 us -> 168 us
  matrix products: 25.5 us -> 0 us
  local copies, waits for them, and re-layouts: 30 us -> 49 us
  other arithmetic: 41.3 us -> 49.8 us
    ppermute x21 -> x41, waiting for transfers between devices: 251 us -> 79.4 us  [the longest x9 31.9 us: line_step(): lax.ppermute(downs[-1], 'expert', down)]
    ppermute x21 -> x41, starting transfers between devices: 4.03 us -> 84.1 us  [the longest x9 42.1 us: line_step(): lax.ppermute(ups[-1], 'expert', up)]
    all_to_all x8, waiting for transfers between devices: 111 us -> 34.6 us  [the longest x2 24.9 us: over_expert(): lax.all_to_all(blocks, 'expert', split_axis=0, concat_axis=0, tiled=True)]
    reduce_scatter x3 -> x2, waiting for transfers between devices: 78.2 us -> 3.68 us  [the longest x1 3.68 us: body(): lax.psum_scatter(after(spread0, cot_picked), 'expert', scatter_dimension=...]
    all_to_all x3 -> x1, blocking collectives: 57.4 us -> 13.9 us  [over_batch(): lax.all_to_all(block, 'batch', split_axis=0, concat_axis=0, tiled=True)]
    pallas_call x4 -> x23, Pallas kernels: 134 us -> 168 us  [the longest x2 46.7 us: mixture_backward(): pl.pallas_call(functools.partial(mixture_backward_kernel, chunk, parts, l...]
    dot_general x2 -> x0, matrix products: 25.5 us -> none  [the longest x1 12.8 us: body(): jnp.einsum('erd,erf->edf', mixed, gpre, preferred_element_type=F32)]
    unnamed x30 -> x116, local copies, waits for them, and re-layouts: 3.09 us -> 15.1 us
  transfers between devices with their start and end apart: 32 -> 51, of which waited for: 25 -> 19; matrix products, arithmetic and copies ran while one was open for 10% -> 15% of each run, Pallas kernels for 13% -> 31%
where the time goes in v2:
time: 542 us; the launch traced here: 532 us
  Pallas kernels  168 us (31%)
  starting transfers between devices  118 us (22%)
  waiting for transfers between devices  118 us (22%)
  other arithmetic  49.8 us (9%)
  local copies, waits for them, and re-layouts  49 us (9%)
  between operations  15.5 us (3%)
  blocking collectives  13.9 us (3%)
    pallas_call x2, Pallas kernels, mixture_backward(): pl.pallas_call(functools.partial(mixture_backward_kernel, chunk, parts, l...  46.7 us
    pallas_call x2, Pallas kernels, mixture_forward(): pl.pallas_call(functools.partial(mixture_forward_kernel, chunk, len(x_par...  44.7 us
    ppermute x9, starting transfers between devices, line_step(): lax.ppermute(ups[-1], 'expert', up)  42.1 us
    ppermute x9, waiting for transfers between devices, line_step(): lax.ppermute(downs[-1], 'expert', down)  31.9 us
    ppermute x9, waiting for transfers between devices, line_step(): lax.ppermute(ups[-1], 'expert', up)  28.1 us
    pallas_call x1, Pallas kernels, attention_backward(): pl.pallas_call(functools.partial(attention_backward_kernel, len(waits)),...  26.7 us
    all_to_all x2, waiting for transfers between devices, over_expert(): lax.all_to_all(blocks, 'expert', split_axis=0, concat_axis=0, tiled=True)  24.9 us
    pallas_call x1, Pallas kernels, attention_forward(): pl.pallas_call(attention_forward_kernel, in_specs=[pl.BlockSpec(memory_sp...  23.7 us
  transfers between devices with their start and end apart: 51, of which 19 were waited for; matrix products, arithmetic and copies ran while one was open for 15% of the time, Pallas kernels for 31%

profile of v2, /device:TPU:0, one launch (start us, length us, event | category | flops | bytes accessed | tf_op | source)
XLA Modules:
  0.0 532.5 jit_solution(10636179714453091531)
XLA Ops:
  10.0 3.0 collective-permute-start
  13.0 2.6 collective-permute-start.1
  24.4 8.6 %collective-permute-done.1.refs_2_ = bf16[256,512]{1,0:T(8,128)(2,1)} collective-permute-done((bf16[256,512]{1,0:T(8,128)(2,1)}, bf16[256,512]{1,0:T(8,128)(2,1)}, u32[]{:S(2)}, u32[]{:S(2)}) %collective-permute-start.1) | collective-permute-done | bytes 262176 | tf_op jit(solution)/shard_map/ppermute | solution.py:954
  38.9 5.6 %collective-permute-done.7 = bf16[4,32,512]{2,1,0:T(8,128)(2,1)S(1)} collective-permute-done((bf16[4,32,512]{2,1,0:T(8,128)(2,1)}, bf16[4,32,512]{2,1,0:T(8,128)(2,1)S(1)}, u32[]{:S(2)}, u32[]{:S(2)}) %collective-permute-start.7) | collective-permute-done | bytes 131104 | tf_op jit(solution)/shard_map/ppermute | solution.py:1022
  46.5 6.7 %collective-permute-start.10 = (bf16[8,4,32,512]{3,2,1,0:T(8,128)(2,1)}, bf16[8,4,32,512]{3,2,1,0:T(8,128)(2,1)S(1)}, u32[]{:S(2)}, u32[]{:S(2)}) collective-permute-start(bf16[8,4,32,512]{3,2,1,0:T(8,128)(2,1)} %broadcast_select_fusion.refs_0_.refs_7_), channel_id=1, source_target_pairs={{0,1},{1,2},{2,3},{4,5},{5,6},{6,7},{8,9},{9,10},{10,11},{12,13},{... | collective-permute-start | bytes 3145736 | tf_op jit(solution)/shard_map/ppermute | solution.py:929
  54.6 23.7 %attention_forward.1 = (bf16[1024,512]{1,0:T(8,128)(2,1)}, bf16[12,1024,128]{2,1,0:T(8,128)(2,1)}, f32[8,1,1024]{2,1,0:T(1,128)}, bf16[1024,512]{1,0:T(8,128)(2,...) custom-call(s32[2]{0:T(128)} %pad_add_fusion.z_ref, ...), custom_call_target="tpu_custom_call" | custom-call | flops 30000001024 | bytes 100000 | tf_op jit(solution)/shard_map/attention_forward/pallas_call | solution.py:443
  81.2 13.9 %all_to_all.45.refs_1_.refs_0_ = bf16[8,4,16,512]{3,2,1,0:T(8,128)(2,1)} all-to-all(bf16[8,4,16,512]{3,2,1,0:T(8,128)(2,1)} %after.16), channel_id=1, replica_groups=mesh['batch'=8,'expert'=4] {'batch'}, dimensions={0} | all-to-all | bytes 1048576 | tf_op jit(solution)/shard_map/all_to_all | solution.py:1044
  95.1 4.6 all-to-all-start.1
  99.7 4.5 collective-permute-start.12
  105.5 9.5 %collective-permute-done.12.refs_1_ = bf16[8,4,16,512]{3,2,1,0:T(8,128)(2,1)} collective-permute-done((bf16[8,4,16,512]{3,2,1,0:T(8,128)(2,1)S(1)}, bf16[8,4,16,512]{3,2,1,0:T(8,128)(2,1)}, u32[]{:S(2)}, u32[]{:S(2)}) %collective-permute-start.12) | collective-permute-done | bytes 524320 | tf_op jit(solution)/shard_map/ppermute | solution.py:929
  115.1 5.3 collective-permute-start.13
  123.6 5.4 %collective-permute-start.14 = (bf16[8,4,16,512]{3,2,1,0:T(8,128)(2,1)}, bf16[8,4,16,512]{3,2,1,0:T(8,128)(2,1)}, u32[]{:S(2)}, u32[]{:S(2)}) collective-permute-start(bf16[8,4,16,512]{3,2,1,0:T(8,128)(2,1)} %slice_bitcast_fusion.2.refs_0_), channel_id=1, source_target_pairs={{0,1},{1,2},{2,3},{4,5},{5,6},{6,7},{8,9},{9,10},{10,11},{12,13},{... | collective-permute-start | bytes 1572872 | tf_op jit(solution)/shard_map/ppermute | solution.py:929
  130.2 4.6 collective-permute-start.20
  138.7 4.7 collective-permute-done.14.refs_1_
  143.4 5.2 collective-permute-done.15.refs_2_.refs_4_
  148.7 3.7 collective-permute-start.16
  154.8 11.0 %collective-permute-done.20.refs_0_ = bf16[8,4,32,512]{3,2,1,0:T(8,128)(2,1)S(1)} collective-permute-done((bf16[8,4,32,512]{3,2,1,0:T(8,128)(2,1)S(1)}, bf16[8,4,32,512]{3,2,1,0:T(8,128)(2,1)S(1)}, u32[]{:S(2)}, u32[]{:S(2)}) %collective-permute-start.20) | collective-permute-done | bytes 1048608 | tf_op jit(solution)/shard_map/ppermute | solution.py:929
  166.8 4.4 collective-permute-start.21
  172.5 4.6 collective-permute-start.24
  177.1 5.2 collective-permute-done.19.refs_6_
  184.1 22.3 %mixture_forward.2 = (bf16[4,8,4,16,512]{4,3,2,1,0:T(8,128)(2,1)}, bf16[4,384,512]{2,1,0:T(8,128)(2,1)}, bf16[4,384,2048]{2,1,0:T(8,128)(2,1)}, bf16[4,384,2048]...) custom-call(s32[2]{0:T(128)} %pad_add_fusion.z_ref, ...), custom_call_target="tpu_custom_call" | custom-call | flops 30000001024 | bytes 100000 | tf_op jit(solution)/shard_map/mixture_forward/pallas_call | solution.py:784
  206.5 2.8 collective-permute-done.24.refs_8_.refs_2_
  209.3 4.8 collective-permute-done.25.refs_9_.refs_5_
  215.0 3.0 own_cotangent.1.refs_1_.refs_14_
  218.0 3.8 all-to-all-start.2
  221.9 2.9 collective-permute-start.26
  226.0 23.4 %mixture_backward.2 = (bf16[4,8,4,16,512]{4,3,2,1,0:T(8,128)(2,1)}, bf16[4,384,512]{2,1,0:T(8,128)(2,1)}, bf16[4,384,2048]{2,1,0:T(8,128)(2,1)}, f32[16,512]{1,0:T(8,128)}) custom-call(s32[2]{0:T(128)} %pad_add_fusion.z_ref, bf16[8,4,16,512]{3,2,1,0:T(8,128)(2,1)} %all_to_all.45.refs_1_.refs_0_, bf16[8,4,16,512]{3,2,1,0:T(8,128)(2,1)} %collective-permute-done.12.refs_1_, ...), custom_call_target="tpu_custom_call" | custom-call | flops 30000001024 | bytes 100000 | tf_op jit(solution)/shard_map/mixture_backward/pallas_call | solution.py:818
  249.5 14.1 %collective-permute-done.27.refs_3_.refs_6_ = bf16[8,4,16,512]{3,2,1,0:T(8,128)(2,1)S(1)} collective-permute-done((bf16[8,4,16,512]{3,2,1,0:T(8,128)(2,1)S(1)}, bf16[8,4,16,512]{3,2,1,0:T(8,128)(2,1)S(1)}, u32[]{:S(2)}, u32[]{:S(2)}) %collective-permute-start.27) | collective-permute-done | bytes 524320 | tf_op jit(solution)/shard_map/ppermute | solution.py:930
  264.7 3.8 all-to-all-start.3
  268.5 3.7 reduce-scatter.3.cloned.1.call-done
  272.2 22.4 %mixture_forward.3 = (bf16[4,8,4,16,512]{4,3,2,1,0:T(8,128)(2,1)}, bf16[4,384,512]{2,1,0:T(8,128)(2,1)}, bf16[4,384,2048]{2,1,0:T(8,128)(2,1)}, bf16[4,384,2048]...) custom-call(s32[2]{0:T(128)} %pad_add_fusion.z_ref, ...), custom_call_target="tpu_custom_call" | custom-call | flops 30000001024 | bytes 100000 | tf_op jit(solution)/shard_map/mixture_forward/pallas_call | solution.py:784
  294.6 23.3 %mixture_backward.3 = (bf16[4,8,4,16,512]{4,3,2,1,0:T(8,128)(2,1)}, bf16[4,384,512]{2,1,0:T(8,128)(2,1)}, bf16[4,384,2048]{2,1,0:T(8,128)(2,1)}, f32[16,512]{1,0:T(8,128)}) custom-call(s32[2]{0:T(128)} %pad_add_fusion.z_ref, bf16[8,4,16,512]{3,2,1,0:T(8,128)(2,1)} %slice_bitcast_fusion.2.refs_0_, bf16[8,4,16,512]{3,2,1,0:T(8,128)(2,1)} %collective-permute-done.14.refs_1_, ...), custom_call_target="tpu_custom_call" | custom-call | flops 30000001024 | bytes 100000 | tf_op jit(solution)/shard_map/mixture_backward/pallas_call | solution.py:818
  319.2 3.8 all-to-all-start.4
  323.1 23.4 %weight_grads.1 = (bf16[2,2,2,2,2,512,256]{6,5,4,3,2,1,0:T(8,128)(2,1)}, bf16[2,2,2,2,2,512,256]{6,5,4,3,2,1,0:T(8,128)(2,1)}) custom-call(s32[2]{0:T(128)} %pad_add_fusion.z_ref, bf16[4,384,512]{2,1,0:T(8,128)(2,1)} %get-tuple-element.59.m0, bf16[4,384,512]{2,1,0:T(8,128)(2,1)} %get-tuple-element.60.m1, bf16[4,384,2048]{2,1,0:T(8,128)(2,1)} %get-tuple-element.61.p0, ...), custom_call_target="tpu_custom_call" | custom-call | flops 1000000 | bytes 100000 | tf_op jit(solution)/shard_map/weight_grads/pallas_call | solution.py:892
  346.4 24.9 %all-to-all-done.4.refs_0_ = bf16[4,8,4,16,512]{4,3,2,1,0:T(8,128)(2,1)S(1)} async-done(((bf16[4,8,4,16,512]{4,3,2,1,0:T(8,128)(2,1)}), bf16[4,8,4,16,512]{4,3,2,1,0:T(8,128)(2,1)S(1)}, u32[]{:S(2)}, u32[]{:S(2)}) %all-to-all-start.4) | async-done | bytes 2097184 | tf_op jit(solution)/shard_map/all_to_all | solution.py:1047
  373.4 5.8 %fusion.40 = (bf16[1,1,2,2,2,512,256]{6,5,4,3,2,1,0:T(8,128)(2,1)S(1)}, bf16[1,1,2,2,2,512,256]{6,5,4,3,2,1,0:T(8,128)(2,1)}, bf16[1,1,2,2,2,512,256]{6,5,4,3,2,...) fusion(bf16[2,2,2,2,2,512,256]{6,5,4,3,2,1,0:T(8,128)(2,1)} %get-tuple-element.73), kind=kLoop, calls=%fused_computation.129 | loop fusion | bytes 16777216 | tf_op jit(solution)/shard_map/slice | solution.py:969
  380.3 2.0 maximum_reduce_fusion
  383.4 3.6 all-to-all-start.5
  387.3 5.3 %fusion.41 = (bf16[1,1,2,2,2,512,256]{6,5,4,3,2,1,0:T(8,128)(2,1)}, bf16[1,1,2,2,2,512,256]{6,5,4,3,2,1,0:T(8,128)(2,1)S(1)}, bf16[1,1,2,2,2,512,256]{6,5,4,3,2,...) fusion(bf16[2,2,2,2,2,512,256]{6,5,4,3,2,1,0:T(8,128)(2,1)} %collective-permute-done.28), kind=kLoop, calls=%fused_computation.130 | loop fusion | bytes 16777216 | tf_op jit(solution)/shard_map/slice | solution.py:969
  393.9 2.0 collective-permute-start.29
  399.1 2.9 fusion.8.refs_12_
  406.3 26.7 %attention_backward.1 = (bf16[1024,512]{1,0:T(8,128)(2,1)}, bf16[512,2048]{1,0:T(8,128)(2,1)}, f32[1,512]{1,0:T(1,128)}, f32[1,512]{1,0:T(1,128)}) custom-call(bf16[8,2,4,16,512]{4,3,2,1,0:T(8,128)(2,1)} %copy-done.29, bf16[8,4,32,512]{3,2,1,0:T(8,128)(2,1)} %copy-done.9, bf16[1024,512]{1,0:T(8,128)(2,1)} %get-tuple-element.68.refs_2_, ...), custom_call_target="tpu_custom_call" | custom-call | flops 1000000 | bytes 100000 | tf_op jit(solution)/shard_map/attention_backward/pallas_call | solution.py:557
  433.9 3.4 fusion.6.refs_1_
  437.3 2.7 fusion.5.refs_2_
  440.0 2.0 fusion.1
  450.9 2.2 constant_dynamic-slice_fusion
  454.0 2.0 collective-permute-start.33
  456.0 2.7 fusion.3
  458.7 2.0 collective-permute-start.34
  460.7 2.5 fusion.2
  463.2 4.3 all-to-all-start.6
  468.4 2.0 collective-permute-start.38
  470.3 3.8 collective-permute-done.33
  475.5 2.4 pad_maximum_fusion.1
  477.8 2.8 gather_fusion.1
  480.6 3.1 convert_add_fusion.5
  483.7 2.1 fusion.19
  485.8 2.2 reduce_sum.34.refs_1_
  488.0 6.6 %all-to-all-start.8 = ((bf16[4,16,2176]{2,1,0:T(8,128)(2,1)}), bf16[4,16,2176]{2,1,0:T(8,128)(2,1)S(1)}, u32[]{:S(2)}, u32[]{:S(2)}) async-start(bf16[4,16,2176]{2,1,0:T(8,128)(2,1)} %bitcast.60), calls=%async_computation.10 | async-start | bytes 557056 | tf_op jit(solution)/shard_map/all_to_all | solution.py:1119
  494.6 2.0 fusion.20
  496.6 2.0 fusion.21
  501.0 3.1 all-to-all-done.8
  504.1 3.6 all-to-all-start.7
  516.5 6.6 %all-to-all-done.7 = bf16[8,2,4,16,512]{4,3,2,1,0:T(8,128)(2,1)S(1)} async-done(((bf16[8,2,4,16,512]{4,3,2,1,0:T(8,128)(2,1)}), bf16[8,2,4,16,512]{4,3,2,1,0:T(8,128)(2,1)S(1)}, u32[]{:S(2)}, u32[]{:S(2)}) %all-to-all-start.7) | async-done | bytes 1048608 | tf_op jit(solution)/shard_map/all_to_all | solution.py:1044
  (264 shorter events, 83.5 us)
Async XLA Ops:
  7.2 146.3 %copy-start = (bf16[512,16]{0,1:T(8,128)(2,1)S(1)}, bf16[512,16]{0,1:T(8,128)(2,1)}, u32[]{:S(2)}) copy-start(bf16[512,16]{0,1:T(8,128)(2,1)} %param.15) | copy-start | bytes 49156
  7.2 9.8 %copy-start.23 = (f32[2,2,256,512]{3,2,1,0:T(8,128)S(1)}, f32[2,2,256,512]{3,2,1,0:T(8,128)}, u32[]{:S(2)}) copy-start(f32[2,2,256,512]{3,2,1,0:T(8,128)} %param.12) | copy-start | bytes 6291460
  10.0 12.6 %collective-permute-start = (bf16[256,512]{1,0:T(8,128)(2,1)}, bf16[256,512]{1,0:T(8,128)(2,1)}, u32[]{:S(2)}, u32[]{:S(2)}) collective-permute-start(bf16[256,512]{1,0:T(8,128)(2,1)} %get-tuple-element.140), channel_id=1, source_target_pairs={{0,1},{1,2},{2,3},{3,0},{4,5},{5,6},{6,7},{7,4},{8,9},{9,10},{10,1... | collective-permute-start | bytes 786440 | tf_op jit(solution)/shard_map/ppermute | solution.py:954
  13.0 20.0 %collective-permute-start.1 = (bf16[256,512]{1,0:T(8,128)(2,1)}, bf16[256,512]{1,0:T(8,128)(2,1)}, u32[]{:S(2)}, u32[]{:S(2)}) collective-permute-start(bf16[256,512]{1,0:T(8,128)(2,1)} %get-tuple-element.139), channel_id=1, source_target_pairs={{0,2},{1,3},{2,0},{3,1},{4,6},{5,7},{6,4},{7,5},{8,10},{9,11},{10,... | collective-permute-start | bytes 786440 | tf_op jit(solution)/shard_map/ppermute | solution.py:954
  15.6 18.5 %collective-permute-start.2 = (bf16[256,512]{1,0:T(8,128)(2,1)S(1)}, bf16[256,512]{1,0:T(8,128)(2,1)}, u32[]{:S(2)}, u32[]{:S(2)}) collective-permute-start(bf16[256,512]{1,0:T(8,128)(2,1)S(1)} %get-tuple-element.138), channel_id=1, source_target_pairs={{0,3},{1,0},{2,1},{3,2},{4,7},{5,4},{6,5},{7,6},{8,11},{9,8},{10,9... | collective-permute-start | bytes 786440 | tf_op jit(solution)/shard_map/ppermute | solution.py:954
  17.9 3.3 collective-permute-start.3
  17.9 18.6 %collective-permute-start.4 = (bf16[4,32,512]{2,1,0:T(8,128)(2,1)}, bf16[4,32,512]{2,1,0:T(8,128)(2,1)}, u32[]{:S(2)}, u32[]{:S(2)}) collective-permute-start(bf16[4,32,512]{2,1,0:T(8,128)(2,1)} %get-tuple-element.132), channel_id=1, source_target_pairs={{0,8},{4,12},{8,0},{12,4},{16,24},{20,28},{24,16},{28,20},{1,9},{5... | collective-permute-start | bytes 393224 | tf_op jit(solution)/shard_map/ppermute | solution.py:1022
  21.2 14.4 %copy-start.46 = (bf16[4,32,512]{2,1,0:T(8,128)(2,1)}, bf16[4,32,512]{2,1,0:T(8,128)(2,1)S(1)}, u32[]{:S(2)}) copy-start(bf16[4,32,512]{2,1,0:T(8,128)(2,1)S(1)} %collective-permute-done.3.refs_0_) | copy-start | bytes 393220
  21.2 17.7 %collective-permute-start.5 = (bf16[4,32,512]{2,1,0:T(8,128)(2,1)}, bf16[4,32,512]{2,1,0:T(8,128)(2,1)S(1)}, u32[]{:S(2)}, u32[]{:S(2)}) collective-permute-start(bf16[4,32,512]{2,1,0:T(8,128)(2,1)} %get-tuple-element.131), channel_id=1, source_target_pairs={{0,12},{4,8},{8,4},{12,0},{16,28},{20,24},{24,20},{28,16},{1,13},{... | collective-permute-start | bytes 393224 | tf_op jit(solution)/shard_map/ppermute | solution.py:1022
  22.7 16.2 %collective-permute-start.6 = (bf16[4,32,512]{2,1,0:T(8,128)(2,1)}, bf16[4,32,512]{2,1,0:T(8,128)(2,1)S(1)}, u32[]{:S(2)}, u32[]{:S(2)}) collective-permute-start(bf16[4,32,512]{2,1,0:T(8,128)(2,1)} %get-tuple-element.130), channel_id=1, source_target_pairs={{0,16},{4,20},{8,24},{12,28},{16,0},{20,4},{24,8},{28,12},{1,17},{... | collective-permute-start | bytes 393224 | tf_op jit(solution)/shard_map/ppermute | solution.py:1022
  33.1 11.5 %collective-permute-start.7 = (bf16[4,32,512]{2,1,0:T(8,128)(2,1)}, bf16[4,32,512]{2,1,0:T(8,128)(2,1)S(1)}, u32[]{:S(2)}, u32[]{:S(2)}) collective-permute-start(bf16[4,32,512]{2,1,0:T(8,128)(2,1)} %get-tuple-element.129), channel_id=1, source_target_pairs={{0,20},{4,16},{8,28},{12,24},{16,4},{20,0},{24,12},{28,8},{1,21},{... | collective-permute-start | bytes 393224 | tf_op jit(solution)/shard_map/ppermute | solution.py:1022
  34.1 10.5 %collective-permute-start.8 = (bf16[4,32,512]{2,1,0:T(8,128)(2,1)}, bf16[4,32,512]{2,1,0:T(8,128)(2,1)S(1)}, u32[]{:S(2)}, u32[]{:S(2)}) collective-permute-start(bf16[4,32,512]{2,1,0:T(8,128)(2,1)} %get-tuple-element.128), channel_id=1, source_target_pairs={{0,24},{4,28},{8,16},{12,20},{16,8},{20,12},{24,0},{28,4},{1,25},{... | collective-permute-start | bytes 393224 | tf_op jit(solution)/shard_map/ppermute | solution.py:1022
  35.6 9.9 %copy-start.53 = (pred[8]{0:T(512)(128)(4,1)S(1)}, pred[8]{0:T(512)(128)(4,1)}, u32[]{:S(2)}) copy-start(pred[8]{0:T(512)(128)(4,1)} %compare_and_fusion.1) | copy-start | bytes 28
  36.5 8.1 %collective-permute-start.9 = (bf16[4,32,512]{2,1,0:T(8,128)(2,1)}, bf16[4,32,512]{2,1,0:T(8,128)(2,1)S(1)}, u32[]{:S(2)}, u32[]{:S(2)}) collective-permute-start(bf16[4,32,512]{2,1,0:T(8,128)(2,1)} %get-tuple-element.127), channel_id=1, source_target_pairs={{0,28},{4,24},{8,20},{12,16},{16,12},{20,8},{24,4},{28,0},{1,29},{... | collective-permute-start | bytes 393224 | tf_op jit(solution)/shard_map/ppermute | solution.py:1022
  46.5 31.7 %collective-permute-start.10 = (bf16[8,4,32,512]{3,2,1,0:T(8,128)(2,1)}, bf16[8,4,32,512]{3,2,1,0:T(8,128)(2,1)S(1)}, u32[]{:S(2)}, u32[]{:S(2)}) collective-permute-start(bf16[8,4,32,512]{3,2,1,0:T(8,128)(2,1)} %broadcast_select_fusion.refs_0_.refs_7_), channel_id=1, source_target_pairs={{0,1},{1,2},{2,3},{4,5},{5,6},{6,7},{8,9},{9,10},{10,11},{12,13},{... | collective-permute-start | bytes 3145736 | tf_op jit(solution)/shard_map/ppermute | solution.py:929
  53.3 26.9 %collective-permute-start.11 = (bf16[8,4,32,512]{3,2,1,0:T(8,128)(2,1)}, bf16[8,4,32,512]{3,2,1,0:T(8,128)(2,1)S(1)}, u32[]{:S(2)}, u32[]{:S(2)}) collective-permute-start(bf16[8,4,32,512]{3,2,1,0:T(8,128)(2,1)} %broadcast_select_fusion.refs_0_.refs_7_), channel_id=1, source_target_pairs={{1,0},{2,1},{3,2},{5,4},{6,5},{7,6},{9,8},{10,9},{11,10},{13,12},{... | collective-permute-start | bytes 3145736 | tf_op jit(solution)/shard_map/ppermute | solution.py:930
  95.1 35.2 %copy-start.31 = (bf16[8,4,32,512]{3,2,1,0:T(8,128)(2,1)S(1)}, bf16[8,4,32,512]{3,2,1,0:T(8,128)(2,1)}, u32[]{:S(2)}) copy-start(bf16[8,4,32,512]{3,2,1,0:T(8,128)(2,1)} %copy-done.30) | copy-start | bytes 3145732
  95.1 39.8 %copy-start.33 = (bf16[8,4,32,512]{3,2,1,0:T(8,128)(2,1)S(1)}, bf16[8,4,32,512]{3,2,1,0:T(8,128)(2,1)}, u32[]{:S(2)}) copy-start(bf16[8,4,32,512]{3,2,1,0:T(8,128)(2,1)} %copy-done.32) | copy-start | bytes 3145732
  95.1 41.1 %copy-start.51 = (s32[2,3]{1,0:T(2,128)S(1)}, s32[2,3]{1,0:T(2,128)}, u32[]{:S(2)}) copy-start(s32[2,3]{1,0:T(2,128)} %param.20) | copy-start | bytes 76
  95.1 26.6 %all-to-all-start.1 = ((bf16[8,3,4,16,512]{4,3,2,1,0:T(8,128)(2,1)}), bf16[8,3,4,16,512]{4,3,2,1,0:T(8,128)(2,1)}, u32[]{:S(2)}, u32[]{:S(2)}) async-start(bf16[8,3,4,16,512]{4,3,2,1,0:T(8,128)(2,1)} %after.17), calls=%async_computation.1 | async-start | bytes 3145728 | tf_op jit(solution)/shard_map/all_to_all | solution.py:1044
  99.7 52.7 %copy-start.52 = (s32[2,16]{1,0:T(2,128)S(1)}, s32[2,16]{1,0:T(2,128)}, u32[]{:S(2)}) copy-start(s32[2,16]{1,0:T(2,128)} %param.21) | copy-start | bytes 388
  99.7 172.5 %reduce-scatter.3.cloned.1.call-start = ((), (), s32[]{:S(2)}) async-start(), calls=%async_computation.11 | async-start | bytes 2621440 | tf_op jit(solution)/shard_map/reduce_scatter | solution.py:1069
  99.7 15.3 %collective-permute-start.12 = (bf16[8,4,16,512]{3,2,1,0:T(8,128)(2,1)S(1)}, bf16[8,4,16,512]{3,2,1,0:T(8,128)(2,1)}, u32[]{:S(2)}, u32[]{:S(2)}) collective-permute-start(bf16[8,4,16,512]{3,2,1,0:T(8,128)(2,1)S(1)} %copy-done.35), channel_id=1, source_target_pairs={{0,1},{1,2},{2,3},{4,5},{5,6},{6,7},{8,9},{9,10},{10,11},{12,13},{... | collective-permute-start | bytes 1572872 | tf_op jit(solution)/shard_map/ppermute | solution.py:929
  104.2 16.1 %collective-permute-start.17 = (bf16[8,4,16,512]{3,2,1,0:T(8,128)(2,1)S(1)}, bf16[8,4,16,512]{3,2,1,0:T(8,128)(2,1)}, u32[]{:S(2)}, u32[]{:S(2)}) collective-permute-start(bf16[8,4,16,512]{3,2,1,0:T(8,128)(2,1)S(1)} %copy-done.35), channel_id=1, source_target_pairs={{1,0},{2,1},{3,2},{5,4},{6,5},{7,6},{9,8},{10,9},{11,10},{13,12},{... | collective-permute-start | bytes 1572872 | tf_op jit(solution)/shard_map/ppermute | solution.py:930
  115.1 19.8 %collective-permute-start.13 = (bf16[8,4,16,512]{3,2,1,0:T(8,128)(2,1)}, bf16[8,4,16,512]{3,2,1,0:T(8,128)(2,1)}, u32[]{:S(2)}, u32[]{:S(2)}) collective-permute-start(bf16[8,4,16,512]{3,2,1,0:T(8,128)(2,1)} %collective-permute-done.12.refs_1_), channel_id=1, source_target_pairs={{0,1},{1,2},{2,3},{4,5},{5,6},{6,7},{8,9},{9,10},{10,11},{12,13},{... | collective-permute-start | bytes 1572872 | tf_op jit(solution)/shard_map/ppermute | solution.py:929
  120.4 17.1 %collective-permute-start.18 = (bf16[8,4,16,512]{3,2,1,0:T(8,128)(2,1)}, bf16[8,4,16,512]{3,2,1,0:T(8,128)(2,1)}, u32[]{:S(2)}, u32[]{:S(2)}) collective-permute-start(bf16[8,4,16,512]{3,2,1,0:T(8,128)(2,1)} %collective-permute-done.17.refs_4_.refs_2_), channel_id=1, source_target_pairs={{1,0},{2,1},{3,2},{5,4},{6,5},{7,6},{9,8},{10,9},{11,10},{13,12},{... | collective-permute-start | bytes 1572872 | tf_op jit(solution)/shard_map/ppermute | solution.py:930
  123.6 19.9 %collective-permute-start.14 = (bf16[8,4,16,512]{3,2,1,0:T(8,128)(2,1)}, bf16[8,4,16,512]{3,2,1,0:T(8,128)(2,1)}, u32[]{:S(2)}, u32[]{:S(2)}) collective-permute-start(bf16[8,4,16,512]{3,2,1,0:T(8,128)(2,1)} %slice_bitcast_fusion.2.refs_0_), channel_id=1, source_target_pairs={{0,1},{1,2},{2,3},{4,5},{5,6},{6,7},{8,9},{9,10},{10,11},{12,13},{... | collective-permute-start | bytes 1572872 | tf_op jit(solution)/shard_map/ppermute | solution.py:929
  128.9 19.7 %collective-permute-start.15 = (bf16[8,4,16,512]{3,2,1,0:T(8,128)(2,1)}, bf16[8,4,16,512]{3,2,1,0:T(8,128)(2,1)}, u32[]{:S(2)}, u32[]{:S(2)}) collective-permute-start(bf16[8,4,16,512]{3,2,1,0:T(8,128)(2,1)} %slice_bitcast_fusion.2.refs_0_), channel_id=1, source_target_pairs={{1,0},{2,1},{3,2},{5,4},{6,5},{7,6},{9,8},{10,9},{11,10},{13,12},{... | collective-permute-start | bytes 1572872 | tf_op jit(solution)/shard_map/ppermute | solution.py:930
  130.2 35.6 %collective-permute-start.20 = (bf16[8,4,32,512]{3,2,1,0:T(8,128)(2,1)S(1)}, bf16[8,4,32,512]{3,2,1,0:T(8,128)(2,1)S(1)}, u32[]{:S(2)}, u32[]{:S(2)}) collective-permute-start(bf16[8,4,32,512]{3,2,1,0:T(8,128)(2,1)S(1)} %copy-done.31), channel_id=1, source_target_pairs={{0,1},{1,2},{2,3},{4,5},{5,6},{6,7},{8,9},{9,10},{10,11},{12,13},{... | collective-permute-start | bytes 3145736 | tf_op jit(solution)/shard_map/ppermute | solution.py:929
  134.9 36.4 %collective-permute-start.22 = (bf16[8,4,32,512]{3,2,1,0:T(8,128)(2,1)S(1)}, bf16[8,4,32,512]{3,2,1,0:T(8,128)(2,1)}, u32[]{:S(2)}, u32[]{:S(2)}) collective-permute-start(bf16[8,4,32,512]{3,2,1,0:T(8,128)(2,1)S(1)} %copy-done.33), channel_id=1, source_target_pairs={{1,0},{2,1},{3,2},{5,4},{6,5},{7,6},{9,8},{10,9},{11,10},{13,12},{... | collective-permute-start | bytes 3145736 | tf_op jit(solution)/shard_map/ppermute | solution.py:930
  137.4 44.9 %collective-permute-start.19 = (bf16[8,4,16,512]{3,2,1,0:T(8,128)(2,1)}, bf16[8,4,16,512]{3,2,1,0:T(8,128)(2,1)}, u32[]{:S(2)}, u32[]{:S(2)}) collective-permute-start(bf16[8,4,16,512]{3,2,1,0:T(8,128)(2,1)} %collective-permute-done.18.refs_5_), channel_id=1, source_target_pairs={{1,0},{2,1},{3,2},{5,4},{6,5},{7,6},{9,8},{10,9},{11,10},{13,12},{... | collective-permute-start | bytes 1572872 | tf_op jit(solution)/shard_map/ppermute | solution.py:930
  148.7 35.5 %collective-permute-start.16 = (bf16[8,4,16,512]{3,2,1,0:T(8,128)(2,1)}, bf16[8,4,16,512]{3,2,1,0:T(8,128)(2,1)}, u32[]{:S(2)}, u32[]{:S(2)}) collective-permute-start(bf16[8,4,16,512]{3,2,1,0:T(8,128)(2,1)} %after.18.refs_2_), channel_id=1, source_target_pairs={{0,1},{1,2},{2,3},{4,5},{5,6},{6,7},{8,9},{9,10},{10,11},{12,13},{... | collective-permute-start | bytes 1572872 | tf_op jit(solution)/shard_map/ppermute | solution.py:929
  152.5 31.6 %copy-start.49 = (f32[2,3,256]{2,1,0:T(4,128)}, f32[2,3,256]{2,1,0:T(4,128)S(1)}, u32[]{:S(2)}) copy-start(f32[2,3,256]{2,1,0:T(4,128)S(1)} %copy.100.refs_9_.refs_16_.refs_11_.refs_15_) | copy-start | bytes 18436
  166.8 39.7 %collective-permute-start.21 = (bf16[8,4,32,512]{3,2,1,0:T(8,128)(2,1)}, bf16[8,4,32,512]{3,2,1,0:T(8,128)(2,1)S(1)}, u32[]{:S(2)}, u32[]{:S(2)}) collective-permute-start(bf16[8,4,32,512]{3,2,1,0:T(8,128)(2,1)} %after.19.refs_2_.refs_9_), channel_id=1, source_target_pairs={{0,1},{1,2},{2,3},{4,5},{5,6},{6,7},{8,9},{9,10},{10,11},{12,13},{... | collective-permute-start | bytes 3145736 | tf_op jit(solution)/shard_map/ppermute | solution.py:929
  171.2 35.3 %collective-permute-start.23 = (bf16[8,4,32,512]{3,2,1,0:T(8,128)(2,1)}, bf16[8,4,32,512]{3,2,1,0:T(8,128)(2,1)S(1)}, u32[]{:S(2)}, u32[]{:S(2)}) collective-permute-start(bf16[8,4,32,512]{3,2,1,0:T(8,128)(2,1)} %collective-permute-done.22.refs_5_.refs_12_), channel_id=1, source_target_pairs={{1,0},{2,1},{3,2},{5,4},{6,5},{7,6},{9,8},{10,9},{11,10},{13,12},{... | collective-permute-start | bytes 3145736 | tf_op jit(solution)/shard_map/ppermute | solution.py:930
  172.5 36.8 %collective-permute-start.24 = (bf16[8,4,16,512]{3,2,1,0:T(8,128)(2,1)}, bf16[8,4,16,512]{3,2,1,0:T(8,128)(2,1)S(1)}, u32[]{:S(2)}, u32[]{:S(2)}) collective-permute-start(bf16[8,4,16,512]{3,2,1,0:T(8,128)(2,1)} %collective-permute-done.14.refs_1_), channel_id=1, source_target_pairs={{0,1},{1,2},{2,3},{4,5},{5,6},{6,7},{8,9},{9,10},{10,11},{12,13},{... | collective-permute-start | bytes 1572872 | tf_op jit(solution)/shard_map/ppermute | solution.py:929
  182.4 31.8 %collective-permute-start.25 = (bf16[8,4,16,512]{3,2,1,0:T(8,128)(2,1)}, bf16[8,4,16,512]{3,2,1,0:T(8,128)(2,1)S(1)}, u32[]{:S(2)}, u32[]{:S(2)}) collective-permute-start(bf16[8,4,16,512]{3,2,1,0:T(8,128)(2,1)} %collective-permute-done.15.refs_2_.refs_4_), channel_id=1, source_target_pairs={{1,0},{2,1},{3,2},{5,4},{6,5},{7,6},{9,8},{10,9},{11,10},{13,12},{... | collective-permute-start | bytes 1572872 | tf_op jit(solution)/shard_map/ppermute | solution.py:930
  218.0 45.5 %all-to-all-start.2 = ((bf16[8,4,32,512]{3,2,1,0:T(8,128)(2,1)}), bf16[8,4,32,512]{3,2,1,0:T(8,128)(2,1)S(1)}, u32[]{:S(2)}, u32[]{:S(2)}) async-start(bf16[8,4,32,512]{3,2,1,0:T(8,128)(2,1)} %own_cotangent.1.refs_1_.refs_14_), calls=%async_computation.3 | async-start | bytes 2097152 | tf_op jit(solution)/shard_map/all_to_all | solution.py:1044
  221.9 27.6 %collective-permute-start.26 = (bf16[8,4,16,512]{3,2,1,0:T(8,128)(2,1)S(1)}, bf16[8,4,16,512]{3,2,1,0:T(8,128)(2,1)S(1)}, u32[]{:S(2)}, u32[]{:S(2)}) collective-permute-start(bf16[8,4,16,512]{3,2,1,0:T(8,128)(2,1)S(1)} %copy-done.41), channel_id=1, source_target_pairs={{0,1},{1,2},{2,3},{4,5},{5,6},{6,7},{8,9},{9,10},{10,11},{12,13},{... | collective-permute-start | bytes 1572872 | tf_op jit(solution)/shard_map/ppermute | solution.py:929
  224.7 38.8 %collective-permute-start.27 = (bf16[8,4,16,512]{3,2,1,0:T(8,128)(2,1)S(1)}, bf16[8,4,16,512]{3,2,1,0:T(8,128)(2,1)S(1)}, u32[]{:S(2)}, u32[]{:S(2)}) collective-permute-start(bf16[8,4,16,512]{3,2,1,0:T(8,128)(2,1)S(1)} %copy-done.43), channel_id=1, source_target_pairs={{1,0},{2,1},{3,2},{5,4},{6,5},{7,6},{9,8},{10,9},{11,10},{13,12},{... | collective-permute-start | bytes 1572872 | tf_op jit(solution)/shard_map/ppermute | solution.py:930
  249.4 14.1 %copy-start.44 = (bf16[8,4,16,512]{3,2,1,0:T(8,128)(2,1)}, bf16[8,4,16,512]{3,2,1,0:T(8,128)(2,1)S(1)}, u32[]{:S(2)}) copy-start(bf16[8,4,16,512]{3,2,1,0:T(8,128)(2,1)S(1)} %collective-permute-done.26.refs_2_.refs_3_) | copy-start | bytes 1572868
  264.7 53.2 %all-to-all-start.3 = ((bf16[4,8,4,16,512]{4,3,2,1,0:T(8,128)(2,1)}), bf16[4,8,4,16,512]{4,3,2,1,0:T(8,128)(2,1)S(1)}, u32[]{:S(2)}, u32[]{:S(2)}) async-start(bf16[4,8,4,16,512]{4,3,2,1,0:T(8,128)(2,1)} %after.21), calls=%async_computation.4 | async-start | bytes 4194304 | tf_op jit(solution)/shard_map/all_to_all | solution.py:1047
  319.2 52.1 %all-to-all-start.4 = ((bf16[4,8,4,16,512]{4,3,2,1,0:T(8,128)(2,1)}), bf16[4,8,4,16,512]{4,3,2,1,0:T(8,128)(2,1)S(1)}, u32[]{:S(2)}, u32[]{:S(2)}) async-start(bf16[4,8,4,16,512]{4,3,2,1,0:T(8,128)(2,1)} %after.23.refs_0_), calls=%async_computation.5 | async-start | bytes 4194304 | tf_op jit(solution)/shard_map/all_to_all | solution.py:1047
  372.6 14.7 %collective-permute-start.28 = (bf16[2,2,2,2,2,512,256]{6,5,4,3,2,1,0:T(8,128)(2,1)}, bf16[2,2,2,2,2,512,256]{6,5,4,3,2,1,0:T(8,128)(2,1)}, u32[]{:S(2)}, u32[]{:S(2)}) collective-permute-start(bf16[2,2,2,2,2,512,256]{6,5,4,3,2,1,0:T(8,128)(2,1)} %after.25), channel_id=1, source_target_pairs={{0,4},{4,0},{8,12},{12,8},{16,20},{20,16},{24,28},{28,24},{1,5},{5... | collective-permute-start | bytes 25165832 | tf_op jit(solution)/shard_map/ppermute | solution.py:1089
  383.4 22.0 %all-to-all-start.5 = ((bf16[8,2,4,16,512]{4,3,2,1,0:T(8,128)(2,1)}), bf16[8,2,4,16,512]{4,3,2,1,0:T(8,128)(2,1)S(1)}, u32[]{:S(2)}, u32[]{:S(2)}) async-start(bf16[8,2,4,16,512]{4,3,2,1,0:T(8,128)(2,1)} %copy.104), calls=%async_computation.6 | async-start | bytes 2097152 | tf_op jit(solution)/shard_map/all_to_all | solution.py:1044
  387.0 111.6 %reduce-scatter.5.cloned.1.call-start = ((), (), s32[]{:S(2)}) async-start(), calls=%async_computation.12 | async-start | bytes 2621440 | tf_op jit(solution)/shard_map/reduce_scatter | solution.py:1085
  393.9 40.0 %collective-permute-start.29 = (bf16[2,2,512,256]{3,2,1,0:T(8,128)(2,1)}, bf16[2,2,512,256]{3,2,1,0:T(8,128)(2,1)}, u32[]{:S(2)}, u32[]{:S(2)}) collective-permute-start(bf16[2,2,512,256]{3,2,1,0:T(8,128)(2,1)} %fusion.7.refs_11_), channel_id=1, source_target_pairs={{0,8},{4,12},{8,0},{12,4},{16,24},{20,28},{24,16},{28,20},{1,9},{5... | collective-permute-start | bytes 3145736 | tf_op jit(solution)/shard_map/ppermute | solution.py:977
  397.1 40.1 %collective-permute-start.30 = (bf16[2,2,512,256]{3,2,1,0:T(8,128)(2,1)}, bf16[2,2,512,256]{3,2,1,0:T(8,128)(2,1)}, u32[]{:S(2)}, u32[]{:S(2)}) collective-permute-start(bf16[2,2,512,256]{3,2,1,0:T(8,128)(2,1)} %fusion.9.refs_13_), channel_id=1, source_target_pairs={{0,16},{4,20},{8,24},{12,28},{16,0},{20,4},{24,8},{28,12},{1,17},{... | collective-permute-start | bytes 3145736 | tf_op jit(solution)/shard_map/ppermute | solution.py:977
  402.0 44.5 %collective-permute-start.36 = (bf16[2,2,512,256]{3,2,1,0:T(8,128)(2,1)}, bf16[2,2,512,256]{3,2,1,0:T(8,128)(2,1)}, u32[]{:S(2)}, u32[]{:S(2)}) collective-permute-start(bf16[2,2,512,256]{3,2,1,0:T(8,128)(2,1)} %fusion.8.refs_12_), channel_id=1, source_target_pairs={{0,8},{4,12},{8,0},{12,4},{16,24},{20,28},{24,16},{28,20},{1,9},{5... | collective-permute-start | bytes 3145736 | tf_op jit(solution)/shard_map/ppermute | solution.py:977
  404.8 49.2 %collective-permute-start.39 = (bf16[2,2,512,256]{3,2,1,0:T(8,128)(2,1)}, bf16[2,2,512,256]{3,2,1,0:T(8,128)(2,1)}, u32[]{:S(2)}, u32[]{:S(2)}) collective-permute-start(bf16[2,2,512,256]{3,2,1,0:T(8,128)(2,1)} %fusion.10.refs_14_), channel_id=1, source_target_pairs={{0,16},{4,20},{8,24},{12,28},{16,0},{20,4},{24,8},{28,12},{1,17},{... | collective-permute-start | bytes 3145736 | tf_op jit(solution)/shard_map/ppermute | solution.py:977
  443.1 15.6 %collective-permute-start.31 = (bf16[4,64,2176]{2,1,0:T(8,128)(2,1)}, bf16[4,64,2176]{2,1,0:T(8,128)(2,1)}, u32[]{:S(2)}, u32[]{:S(2)}) collective-permute-start(bf16[4,64,2176]{2,1,0:T(8,128)(2,1)} %dynamic-slice_bitcast_fusion), channel_id=1, source_target_pairs={{0,4},{4,0},{8,12},{12,8},{16,20},{20,16},{24,28},{28,24},{1,5},{5... | collective-permute-start | bytes 3342344 | tf_op jit(solution)/shard_map/ppermute | solution.py:960
  444.8 38.9 %collective-permute-start.35 = (bf16[2,512,256]{2,1,0:T(8,128)(2,1)}, bf16[2,512,256]{2,1,0:T(8,128)(2,1)}, u32[]{:S(2)}, u32[]{:S(2)}) collective-permute-start(bf16[2,512,256]{2,1,0:T(8,128)(2,1)} %dynamic-slice_bitcast_fusion.4), channel_id=1, source_target_pairs={{0,16},{4,20},{8,24},{12,28},{16,0},{20,4},{24,8},{28,12},{1,17},{... | collective-permute-start | bytes 1572872 | tf_op jit(solution)/shard_map/ppermute | solution.py:960
  449.4 45.2 %collective-permute-start.37 = (bf16[2,512,256]{2,1,0:T(8,128)(2,1)}, bf16[2,512,256]{2,1,0:T(8,128)(2,1)}, u32[]{:S(2)}, u32[]{:S(2)}) collective-permute-start(bf16[2,512,256]{2,1,0:T(8,128)(2,1)} %dynamic-slice_bitcast_fusion.3), channel_id=1, source_target_pairs={{0,16},{4,20},{8,24},{12,28},{16,0},{20,4},{24,8},{28,12},{1,17},{... | collective-permute-start | bytes 1572872 | tf_op jit(solution)/shard_map/ppermute | solution.py:960
  453.1 15.2 %collective-permute-start.32 = (bf16[256,512]{1,0:T(8,128)(2,1)}, bf16[256,512]{1,0:T(8,128)(2,1)}, u32[]{:S(2)}, u32[]{:S(2)}) collective-permute-start(bf16[256,512]{1,0:T(8,128)(2,1)} %get-tuple-element.137), channel_id=1, source_target_pairs={{0,1},{1,2},{2,3},{3,0},{4,5},{5,6},{6,7},{7,4},{8,9},{9,10},{10,1... | collective-permute-start | bytes 786440 | tf_op jit(solution)/shard_map/ppermute | solution.py:954
  454.0 20.2 %collective-permute-start.33 = (bf16[256,512]{1,0:T(8,128)(2,1)}, bf16[256,512]{1,0:T(8,128)(2,1)}, u32[]{:S(2)}, u32[]{:S(2)}) collective-permute-start(bf16[256,512]{1,0:T(8,128)(2,1)} %get-tuple-element.136), channel_id=1, source_target_pairs={{0,2},{1,3},{2,0},{3,1},{4,6},{5,7},{6,4},{7,5},{8,10},{9,11},{10,... | collective-permute-start | bytes 786440 | tf_op jit(solution)/shard_map/ppermute | solution.py:954
  458.7 8.8 %copy-start.27 = (bf16[2,2,512,256]{3,2,1,0:T(8,128)(2,1)S(1)}, bf16[2,2,512,256]{3,2,1,0:T(8,128)(2,1)}, u32[]{:S(2)}) copy-start(bf16[2,2,512,256]{3,2,1,0:T(8,128)(2,1)} %fusion.3) | copy-start | bytes 3145732
  458.7 16.1 %collective-permute-start.34 = (bf16[256,512]{1,0:T(8,128)(2,1)}, bf16[256,512]{1,0:T(8,128)(2,1)S(1)}, u32[]{:S(2)}, u32[]{:S(2)}) collective-permute-start(bf16[256,512]{1,0:T(8,128)(2,1)} %get-tuple-element.135), channel_id=1, source_target_pairs={{0,3},{1,0},{2,1},{3,2},{4,7},{5,4},{6,5},{7,6},{8,11},{9,8},{10,9... | collective-permute-start | bytes 786440 | tf_op jit(solution)/shard_map/ppermute | solution.py:954
  463.2 22.6 %all-to-all-start.6 = ((bf16[4,64,2176]{2,1,0:T(8,128)(2,1)}), bf16[4,64,2176]{2,1,0:T(8,128)(2,1)}, u32[]{:S(2)}, u32[]{:S(2)}) async-start(bf16[4,64,2176]{2,1,0:T(8,128)(2,1)} %fusion.2), calls=%async_computation.7 | async-start | bytes 2228224 | tf_op jit(solution)/shard_map/all_to_all | solution.py:1113
  468.4 28.3 %collective-permute-start.38 = (bf16[2,512,256]{2,1,0:T(8,128)(2,1)}, bf16[2,512,256]{2,1,0:T(8,128)(2,1)}, u32[]{:S(2)}, u32[]{:S(2)}) collective-permute-start(bf16[2,512,256]{2,1,0:T(8,128)(2,1)} %dynamic-slice_bitcast_fusion.2), channel_id=1, source_target_pairs={{0,8},{4,12},{8,0},{12,4},{16,24},{20,28},{24,16},{28,20},{1,9},{5... | collective-permute-start | bytes 1572872 | tf_op jit(solution)/shard_map/ppermute | solution.py:960
  474.2 33.5 %collective-permute-start.40 = (bf16[2,512,256]{2,1,0:T(8,128)(2,1)}, bf16[2,512,256]{2,1,0:T(8,128)(2,1)}, u32[]{:S(2)}, u32[]{:S(2)}) collective-permute-start(bf16[2,512,256]{2,1,0:T(8,128)(2,1)} %dynamic-slice_bitcast_fusion.1), channel_id=1, source_target_pairs={{0,8},{4,12},{8,0},{12,4},{16,24},{20,28},{24,16},{28,20},{1,9},{5... | collective-permute-start | bytes 1572872 | tf_op jit(solution)/shard_map/ppermute | solution.py:960
  483.7 10.9 %copy-start.26 = (bf16[2,2,512,256]{3,2,1,0:T(8,128)(2,1)S(1)}, bf16[2,2,512,256]{3,2,1,0:T(8,128)(2,1)}, u32[]{:S(2)}) copy-start(bf16[2,2,512,256]{3,2,1,0:T(8,128)(2,1)} %copy-done.25) | copy-start | bytes 3145732
  488.0 16.1 %all-to-all-start.8 = ((bf16[4,16,2176]{2,1,0:T(8,128)(2,1)}), bf16[4,16,2176]{2,1,0:T(8,128)(2,1)S(1)}, u32[]{:S(2)}, u32[]{:S(2)}) async-start(bf16[4,16,2176]{2,1,0:T(8,128)(2,1)} %bitcast.60), calls=%async_computation.10 | async-start | bytes 557056 | tf_op jit(solution)/shard_map/all_to_all | solution.py:1119
  504.1 18.9 %all-to-all-start.7 = ((bf16[8,2,4,16,512]{4,3,2,1,0:T(8,128)(2,1)}), bf16[8,2,4,16,512]{4,3,2,1,0:T(8,128)(2,1)S(1)}, u32[]{:S(2)}, u32[]{:S(2)}) async-start(bf16[8,2,4,16,512]{4,3,2,1,0:T(8,128)(2,1)} %copy.106), calls=%async_computation.9 | async-start | bytes 2097152 | tf_op jit(solution)/shard_map/all_to_all | solution.py:1044
  513.9 9.5 %copy-start.12 = (f32[2,2,256,512]{3,2,1,0:T(8,128)S(1)}, f32[2,2,256,512]{3,2,1,0:T(8,128)}, u32[]{:S(2)}) copy-start(f32[2,2,256,512]{3,2,1,0:T(8,128)} %param.11) | copy-start | bytes 6291460
  (41 other events, 160.4 us)
Sparse Core Ops, SparseCore 0:
  218.1 53.9 reduce-scatter.2
  399.2 41.9 reduce-scatter.4

commit v3 on v2

--- a/solution.py
+++ b/solution.py
@@ -358,9 +358,9 @@
     return key <= query
 
 
-def attention_forward_kernel(z_ref, *refs):
+def attention_forward_kernel(waits, z_ref, *refs):
     quarters = 4
-    parts = refs[:quarters]
+    parts, refs = refs[:quarters], refs[:quarters] + refs[quarters + waits:]
     (wqkv_ref, wo_ref, g1_ref, g2_ref, x_ref, qkv_ref, lse_ref, ctx_ref, attn_ref, mix_ref, more_ref) = refs[quarters:-2]
     ctx_pairs, sems = refs[-2:]
     length, width = x_ref.shape
@@ -433,7 +433,7 @@
     lax.fori_loop(0, quarters, finish, 0, unroll=True)
 
 
-def attention_forward(z, parts, wqkv, wo, g1, g2, nb):
+def attention_forward(z, parts, wqkv, wo, g1, g2, nb, waits=()):
     quarters = len(parts)
     tile, width = parts[0].shape
     length = quarters * tile
@@ -441,9 +441,9 @@
     lanes = width // pairs
     vmem = pl.BlockSpec(memory_space=pltpu.VMEM)
     return pl.pallas_call(
-        attention_forward_kernel,
+        functools.partial(attention_forward_kernel, len(waits)),
         in_specs=[pl.BlockSpec(memory_space=pltpu.SMEM)]
-        + [pl.BlockSpec(memory_space=pl.ANY)] * quarters + [vmem] * 4,
+        + [pl.BlockSpec(memory_space=pl.ANY)] * (quarters + len(waits)) + [vmem] * 4,
         out_shape=(
             jax.ShapeDtypeStruct((length, width), BF16),
             jax.ShapeDtypeStruct((3 * pairs, length, lanes), BF16),
@@ -458,16 +458,16 @@
             pltpu.SemaphoreType.DMA((quarters,)),
         ],
         compiler_params=pltpu.CompilerParams(vmem_limit_bytes=VMEM_LIMIT),
-        cost_estimate=KERNEL_COST,
+        cost_estimate=SMALL_COST,
         name="attention_forward",
-    )(z, *parts, wqkv, wo, g1, g2)
+    )(z, *parts, *waits, wqkv, wo, g1, g2)
 
 
 def attention_backward_kernel(count, *refs):
-    attention_backward_body(*refs[:11], *refs[11 + count:])
-
-
-def attention_backward_body(gm_ref, cot_ref, x_ref, attn_ref, ctx_ref, qkv_ref, lse_ref,
+    attention_backward_body(*refs[:12], *refs[12 + count:])
+
+
+def attention_backward_body(gm0_ref, gm1_ref, cot_ref, x_ref, attn_ref, ctx_ref, qkv_ref, lse_ref,
                               wqkv_ref, wo_ref, g1_ref, g2_ref,
                               gin_ref, dw_ref, dg1_ref, dg2_ref,
                               delta, ga_rows, dctx, gqkv, attn_in, dk_sum, dv_sum):
@@ -475,7 +475,7 @@
     pairs = HEADS // 2
     lanes = width // pairs
     half = lanes // 2
-    nb, _, quarters, _, _ = gm_ref.shape
+    nb, quarters, _, _ = gm0_ref.shape
     tile = length // quarters
     factor = half ** (-0.5)
     dg2_ref[...] = jnp.zeros_like(dg2_ref)
@@ -484,7 +484,7 @@
     def first(i, carry):
         rows = pl.ds(pl.multiple_of(i * tile, tile), tile)
         normed, inverse = row_norm(x_ref[rows, :].astype(F32) + attn_ref[rows, :])
-        grad = jnp.concatenate([gm_ref[b, c, i] for b in range(nb) for c in range(CHUNKS)], 0).astype(F32)
+        grad = jnp.concatenate([r[b, i] for b in range(nb) for r in (gm0_ref, gm1_ref)], 0).astype(F32)
         dg2_ref[...] += jnp.sum(grad * normed, 0, keepdims=True)
         back = row_norm_back(grad, normed, inverse, g2_ref[...])
         delta[rows, :] = back
@@ -550,13 +550,13 @@
         dw_ref[:, c * width:(c + 1) * width] = dot_tn(attn_in[...], grads).astype(BF16)
 
 
-def attention_backward(gm, cot, x, attn, ctx, qkv, lse, wqkv, wo, g1, g2, waits=()):
+def attention_backward(gm0, gm1, cot, x, attn, ctx, qkv, lse, wqkv, wo, g1, g2, waits=()):
     length, width = x.shape
     pairs = HEADS // 2
     lanes = width // pairs
     return pl.pallas_call(
         functools.partial(attention_backward_kernel, len(waits)),
-        in_specs=[pl.BlockSpec(memory_space=pltpu.VMEM)] * 11 + [pl.BlockSpec(memory_space=pl.ANY)] * len(waits),
+        in_specs=[pl.BlockSpec(memory_space=pltpu.VMEM)] * 12 + [pl.BlockSpec(memory_space=pl.ANY)] * len(waits),
         out_shape=(
             jax.ShapeDtypeStruct((length, width), BF16),
             jax.ShapeDtypeStruct((width, 4 * width), BF16),
@@ -575,7 +575,7 @@
         compiler_params=pltpu.CompilerParams(vmem_limit_bytes=VMEM_LIMIT),
         cost_estimate=SMALL_COST,
         name="attention_backward",
-    )(gm, cot, x, attn, ctx, qkv, lse, wqkv, wo, g1, g2, *waits)
+    )(gm0, gm1, cot, x, attn, ctx, qkv, lse, wqkv, wo, g1, g2, *waits)
 
 
 def group_reduce(rows, mem, op, fill):
@@ -608,6 +608,9 @@
 
 
 def arrivals(z, sources, sems, base, act, place):
+    if len(sources) == 1:
+        act(pltpu.make_async_copy(*place(sources[0], None), sems.at[base]))
+        return
     n = (len(sources) + 1) // 2
     act(pltpu.make_async_copy(*place(sources[0], z), sems.at[base]))
     for k in range(1, n):
@@ -642,7 +645,7 @@
     rows = mkl_ref.shape[1]
     e = pl.program_id(0)
     z = z_ref[0]
-    x_place = lambda ref, plane: (ref, xs.at[plane])
+    x_place = lambda ref, plane: (ref, xs if plane is None else xs.at[plane])
     a_copy = pltpu.make_async_copy(a_in.at[:, 1 + chunk], attn, sems.at[parts])
 
     @pl.when(e == 0)
@@ -686,10 +689,11 @@
                 spread = dot_tn(weights_ref[block], outs).astype(BF16)
                 for s in range(sl):
                     at = slice(s * nb * PB, (s + 1) * nb * PB)
-                    spread_ref[q, :, m * sl + s] = spread[at].reshape(nb, PB, width)
+                    spread_ref[q, :, 0, m * sl + s] = spread[at].reshape(nb, PB, width)
         a_copy.wait()
         for q in range(quarters):
-            spread_ref[q, :, z] = (spread_ref[q, :, z].astype(F32) + attn[:, q].astype(F32)).astype(BF16)
+            mine = spread_ref[q, :, 0, z].astype(F32) + attn[:, q].astype(F32)
+            spread_ref[q, :, 0, z] = mine.astype(BF16)
 
 
 def mixture_backward_kernel(chunk, parts, waits, z_ref, *refs):
@@ -704,8 +708,8 @@
     e = pl.program_id(0)
     z = z_ref[0]
     mine = pl.ds(chunk * PB, PB)
-    x_place = lambda ref, plane: (ref, xs.at[plane])
-    g_place = lambda ref, plane: (ref.at[:, :, mine, :], gs.at[plane])
+    x_place = lambda ref, plane: (ref, xs if plane is None else xs.at[plane])
+    g_place = lambda ref, plane: (ref.at[..., mine, :], gs if plane is None else gs.at[plane])
 
     @pl.when(e == 0)
     def _():
@@ -766,7 +770,7 @@
 
 
 def mixture_sizes(x_parts, mem, mkl, w1):
-    nb, quarters, piece, width = x_parts[0].shape
+    nb, quarters, piece, width = x_parts[0].shape[-4:]
     planes = quarters
     experts, _, hidden_size = w1.shape
     total = mem.shape[0] * quarters * mkl.shape[1]
@@ -784,8 +788,9 @@
     return pl.pallas_call(
         functools.partial(mixture_forward_kernel, chunk, len(x_parts), len(waits)),
         grid=(narrow[0],),
+        input_output_aliases={1 + len(x_parts): 0} if chunk else {},
         out_shape=(
-            jax.ShapeDtypeStruct(back, BF16),
+            jax.ShapeDtypeStruct(back[:2] + (CHUNKS,) + back[2:], BF16),
             jax.ShapeDtypeStruct(narrow, BF16),
             jax.ShapeDtypeStruct(wide, BF16),
             jax.ShapeDtypeStruct(wide, BF16),
@@ -797,7 +802,7 @@
         + [any_spec] * (len(x_parts) + len(waits) + 1)
         + [whole(ctrl.shape), whole(mem.shape), whole(mkl.shape), whole(take.shape),
            by_expert(w1.shape), by_expert(w2.shape)],
-        out_specs=(whole(back), whole(narrow), by_expert(wide), by_expert(wide),
+        out_specs=(pl.BlockSpec(back[:2] + (1,) + back[2:], lambda e: (0, 0, chunk, 0, 0, 0)), whole(narrow), by_expert(wide), by_expert(wide),
                    whole(narrow), whole(weights), whole(gates)),
         scratch_shapes=[
             pltpu.VMEM(back, BF16),
@@ -806,7 +811,7 @@
             pltpu.SemaphoreType.DMA((len(x_parts) + 1,)),
         ],
         compiler_params=pltpu.CompilerParams(vmem_limit_bytes=VMEM_LIMIT),
-        cost_estimate=KERNEL_COST,
+        cost_estimate=SMALL_COST,
         name="mixture_forward",
     )(z, *x_parts, *waits, a_all, ctrl, mem, mkl, take, w1, w2)
 
@@ -836,31 +841,9 @@
             pltpu.SemaphoreType.DMA((2 * parts,)),
         ],
         compiler_params=pltpu.CompilerParams(vmem_limit_bytes=VMEM_LIMIT),
-        cost_estimate=KERNEL_COST,
+        cost_estimate=SMALL_COST,
         name="mixture_backward",
     )(z, *x_parts, *g_parts, *waits, ctrl, mem, mkl, weights, gates, eo, slope, w1, w2)
-
-
-def own_cotangent_kernel(parts, z_ref, *refs):
-    g_in, (cot_ref, sems) = refs[:parts], refs[-2:]
-    z = z_ref[0]
-    place = lambda ref, plane: (ref.at[:, z], cot_ref.at[:, plane])
-    arrivals(z, g_in, sems, 0, start, place)
-    arrivals(z, g_in, sems, 0, wait, place)
-
-
-def own_cotangent(z, g_parts, waits=()):
-    nb, planes, piece, width = g_parts[0].shape
-    any_spec = pl.BlockSpec(memory_space=pl.ANY)
-    return pl.pallas_call(
-        functools.partial(own_cotangent_kernel, len(g_parts)),
-        out_shape=jax.ShapeDtypeStruct((nb, planes, piece, width), BF16),
-        in_specs=[pl.BlockSpec(memory_space=pltpu.SMEM)] + [any_spec] * (len(g_parts) + len(waits)),
-        scratch_shapes=[pltpu.SemaphoreType.DMA((len(g_parts),))],
-        cost_estimate=SMALL_COST,
-        compiler_params=pltpu.CompilerParams(vmem_limit_bytes=VMEM_LIMIT),
-        name="own_cotangent",
-    )(z, *g_parts, *waits)
 
 
 def weight_grads_kernel(z_ref, m0, m1, p0, p1, h0, h1, o0, o1, *refs):
@@ -1023,10 +1006,10 @@
         pieces.append(part)
     pieces[1] = after(pieces[1], *x_parts[1:])
     cot = jnp.take(jnp.stack(pieces), own ^ jnp.arange(nb), axis=0)
-    g_up, g_down = line_step([cot], [cot], planes)
+    g_all = lax.all_gather(cot, "expert", axis=0, tiled=False)
 
     x, qkv, lse, ctx, attn, mix, more = attention_forward(
-        z_arr, x_parts, query_key_value_weight, output_weight, g1, g2, nb)
+        z_arr, x_parts, query_key_value_weight, output_weight, g1, g2, nb, waits=(cot,))
 
     member, taking = jax.vmap(group_tables)(group_sizes, live)
     groups = member.shape[2]
@@ -1046,52 +1029,39 @@
     def over_expert(blocks):
         return lax.all_to_all(blocks, "expert", split_axis=0, concat_axis=0, tiled=True)
 
-    own0 = over_batch(after(mix, g_up[1], g_down[1]))
-    g_up, g_down = line_step(g_up, g_down, planes)
-    up0, down0 = line_step([own0], [own0], planes)
+    own0 = over_batch(mix)
+    x0 = [lax.all_gather(own0, "expert", axis=0, tiled=False)]
     more = over_batch(after(more, own0))
-    own1 = more[:, 0]
-    up1, down1 = line_step([own1], [own1], planes)
-    up0, down0 = line_step(up0, down0, planes)
-    up0[-1] = after(up0[-1], up1[-1], down1[-1])
-    g_up[-1] = after(g_up[-1], up0[-2], down0[-2])
-    g_up, g_down = line_step(g_up, g_down, planes)
-    up0, down0 = line_step(up0, down0, planes)
-    up1, down1 = line_step(up1, down1, planes)
-    second = up1[-1], down1[-1]
-    up1, down1 = line_step(up1, down1, planes)
-    g_parts = g_up + g_down[1:]
-    x0, x1 = up0 + down0[1:], up1 + down1[1:]
-
+    x1 = [lax.all_gather(more[:, 0], "expert", axis=0, tiled=False)]
+    g_parts = [g_all]
+
+    cot_own = lax.dynamic_index_in_dim(g_all, z, 2, keepdims=False).transpose(1, 0, 2, 3)
+    cot_own = over_batch(cot_own)
     spread0, mixed0, hid0, slope0, eo0, weights0, gates0 = mixture_forward(
-        0, z_arr, x0, more, ctrl, mem, mkl, take, w_first, w_second)
-    cot_picked = own_cotangent(z_arr, g_parts, waits=(eo0,) + second)
-    spread0 = lax.psum_scatter(after(spread0, cot_picked), "expert", scatter_dimension=0, tiled=False)
-    cot_own = over_batch(cot_picked)
+        0, z_arr, x0, more, ctrl, mem, mkl, take, w_first, w_second, waits=(cot_own,))
     back0, geo0, gpre0, dctrl0 = mixture_backward(
         0, z_arr, x0, g_parts, ctrl, mem, mkl, weights0, gates0, eo0, slope0, w_first, w_second,
-        waits=(cot_picked,))
-    back0 = over_expert(after(back0, cot_own, up1[-1], down1[-1]))
-    spread1, mixed1, hid1, slope1, eo1, weights1, gates1 = mixture_forward(
-        1, z_arr, x1, more, ctrl, mem, mkl, take, w_first, w_second, waits=(dctrl0, spread0))
+        waits=())
+    back0 = lax.psum_scatter(after(back0, x1[0]), "expert", scatter_dimension=0, tiled=False)
+    spread, mixed1, hid1, slope1, eo1, weights1, gates1 = mixture_forward(
+        1, z_arr, x1, more, ctrl, mem, mkl, take, w_first, w_second, waits=(spread0, dctrl0))
     back1, geo1, gpre1, dctrl1 = mixture_backward(
         1, z_arr, x1, g_parts, ctrl, mem, mkl, weights1, gates1, eo1, slope1, w_first, w_second)
-    back0 = after(back0, dctrl1)
-    back1 = after(back1, back0)
     dctrl = dctrl0[:8] + dctrl0[8:] + dctrl1[:8] + dctrl1[8:]
+    back1 = lax.psum_scatter(after(back1, back0), "expert", scatter_dimension=0, tiled=False)
+    back0 = over_batch(back0)
     keep, send = weight_grads(
-        z_arr, (mixed0, mixed1), (gpre0, gpre1), (hid0, hid1), (geo0, geo1), nb, waits=(back1,))
-    back1 = after(over_expert(back1), send)
-    spread1 = lax.psum_scatter(after(spread1, back1), "expert", scatter_dimension=0, tiled=False)
-    back = jnp.stack([back0, back1], 2)
-    back = jnp.sum(back.astype(F32), 0).astype(BF16)
-    back = over_batch(back)
-    came = lax.ppermute(after(send, back1), "batch", [(i, i ^ 1) for i in range(nb)])
+        z_arr, (mixed0, mixed1), (gpre0, gpre1), (hid0, hid1), (geo0, geo1), nb, waits=(back0,))
+    spread = lax.psum_scatter(after(spread, back1), "expert", scatter_dimension=0, tiled=False)
+    send = after(send, back1)
+    back1 = over_batch(back1)
+    came = lax.ppermute(send, "batch", [(i, i ^ 1) for i in range(nb)])
     keeps, sends = first_halves(keep, came)
 
     gin, dw, dg1, dg2 = attention_backward(
-        back, cot_own, x, attn, ctx, qkv, lse, query_key_value_weight, output_weight, g1, g2,
-        waits=tuple(sends[0] + sends[1]))
+        back0, back1, cot_own, x, attn, ctx, qkv, lse, query_key_value_weight, output_weight, g1, g2,
+        waits=(sends[0][0], sends[1][0]))
+    sends = [[part if e == 0 else after(part, dg1) for e, part in enumerate(parts)] for parts in sends]
     held = [[hop(keeps[i][e], sends[i][e], 1 + i) for e in range(len(sends[i]))] for i in range(2)]
     gin = after(gin, held[0][0], held[1][0])
     dw = after(dw, held[0][0], held[1][0])
@@ -1112,8 +1082,7 @@
     chips = [[c + 2 * i for i in range(nb // 2)] for c in range(2)]
     flat = lax.all_to_all(flat, "batch", split_axis=0, concat_axis=0, tiled=True, axis_index_groups=chips)
     flat = jnp.sum(flat.astype(F32), 0).astype(BF16)
-    spread = jnp.stack([after(spread0, flat), spread1], 1)
-    spread = over_batch(spread)
+    spread = over_batch(after(spread, flat))
     out = tokens + spread.transpose(2, 0, 1, 3, 4).reshape(tokens.shape).astype(F32)
     flat = flat.reshape(planes, -1, flat.shape[1])
     flat = lax.all_to_all(flat, "expert", split_axis=0, concat_axis=0, tiled=True)

time: 542 us -> 486 us (0.90)
  starting transfers between devices: 118 us -> 47.7 us
  blocking collectives: 13.9 us -> 51.9 us
  waiting for transfers between devices: 118 us -> 107 us
    ppermute x19 -> x1, waiting for transfers between devices: 60 us -> 2.79 us  [body(): came = lax.ppermute(send, 'batch', [(i, i ^ 1) for i in range(nb)])]
    all_gather x0 -> x3, waiting for transfers between devices: none -> 56.5 us  [the longest x1 36.9 us: body(): x0 = [lax.all_gather(own0, 'expert', axis=0, tiled=False)]]
    ppermute x19 -> x1, starting transfers between devices: 54.1 us -> 0.01 us  [body(): came = lax.ppermute(send, 'batch', [(i, i ^ 1) for i in range(nb)])]
    all_to_all x1 -> x3, blocking collectives: 13.9 us -> 51.9 us  [over_batch(): lax.all_to_all(block, 'batch', split_axis=0, concat_axis=0, tiled=True)]
    all_to_all x2 -> x0, waiting for transfers between devices: 24.9 us -> none  [over_expert(): lax.all_to_all(blocks, 'expert', split_axis=0, concat_axis=0, tiled=True)]
    all_to_all x2 -> x0, starting transfers between devices: 7.6 us -> none  [over_expert(): lax.all_to_all(blocks, 'expert', split_axis=0, concat_axis=0, tiled=True)]
    all_to_all x1, waiting for transfers between devices: 0.01 us -> 7.26 us  [body(): lax.all_to_all(flat, 'batch', split_axis=0, concat_axis=0, tiled=True, ax...]
    ppermute x4, waiting for transfers between devices: 0.23 us -> 5.87 us  [hop(): came = lax.ppermute(send, 'batch', [(j, j ^ 1 << bit) for j in range(8)])]
  transfers between devices with their start and end apart: 51 -> 34, of which waited for: 19 -> 12; matrix products, arithmetic and copies ran while one was open for 15% -> 16% of each run, Pallas kernels for 31% -> 35%
where the time goes in v3:
time: 486 us; the launch traced here: 478 us
  Pallas kernels  165 us (34%)
  waiting for transfers between devices  107 us (22%)
  blocking collectives  51.9 us (11%)
  starting transfers between devices  47.7 us (10%)
  other arithmetic  46.9 us (10%)
  local copies, waits for them, and re-layouts  43.8 us (9%)
  between operations  15.2 us (3%)
    all_to_all x3, blocking collectives, over_batch(): lax.all_to_all(block, 'batch', split_axis=0, concat_axis=0, tiled=True)  51.9 us
    pallas_call x2, Pallas kernels, mixture_backward(): pl.pallas_call(functools.partial(mixture_backward_kernel, chunk, parts, l...  47 us
    pallas_call x2, Pallas kernels, mixture_forward(): pl.pallas_call(functools.partial(mixture_forward_kernel, chunk, len(x_par...  44.7 us
    all_gather x1, waiting for transfers between devices, body(): x0 = [lax.all_gather(own0, 'expert', axis=0, tiled=False)]  36.9 us
    pallas_call x1, Pallas kernels, attention_backward(): pl.pallas_call(functools.partial(attention_backward_kernel, len(waits)),...  26.8 us
    pallas_call x1, Pallas kernels, attention_forward(): pl.pallas_call(functools.partial(attention_forward_kernel, len(waits)), i...  23.7 us
    pallas_call x1, Pallas kernels, weight_grads(): pl.pallas_call(weight_grads_kernel, grid=(experts,), in_specs=[pl.BlockSp...  23.3 us
    all_gather x1, waiting for transfers between devices, body(): g_all = lax.all_gather(cot, 'expert', axis=0, tiled=False)  19.6 us
  transfers between devices with their start and end apart: 34, of which 12 were waited for; matrix products, arithmetic and copies ran while one was open for 16% of the time, Pallas kernels for 35%

profile of v3, /device:TPU:0, one launch (start us, length us, event | category | flops | bytes accessed | tf_op | source)
XLA Modules:
  0.0 477.9 jit_solution(8494490951079887325)
XLA Ops:
  7.3 1.9 convert_element_type.319
  10.2 3.0 collective-permute-start
  13.2 2.6 collective-permute-start.1
  18.1 1.5 collective-permute-start.4
  21.2 1.5 collective-permute-done.refs_1_
  22.7 1.8 collective-permute-start.6
  24.5 8.7 %collective-permute-done.1.refs_2_ = bf16[256,512]{1,0:T(8,128)(2,1)} collective-permute-done((bf16[256,512]{1,0:T(8,128)(2,1)}, bf16[256,512]{1,0:T(8,128)(2,1)}, u32[]{:S(2)}, u32[]{:S(2)}) %collective-permute-start.1) | collective-permute-done | bytes 262176 | tf_op jit(solution)/shard_map/ppermute | solution.py:937
  34.3 1.4 collective-permute-start.8
  36.6 1.5 collective-permute-start.9
  39.1 5.6 %collective-permute-done.7 = bf16[4,32,512]{2,1,0:T(8,128)(2,1)S(1)} collective-permute-done((bf16[4,32,512]{2,1,0:T(8,128)(2,1)}, bf16[4,32,512]{2,1,0:T(8,128)(2,1)S(1)}, u32[]{:S(2)}, u32[]{:S(2)}) %collective-permute-start.7) | collective-permute-done | bytes 131104 | tf_op jit(solution)/shard_map/ppermute | solution.py:1005
  48.5 23.7 %attention_forward.1 = (bf16[1024,512]{1,0:T(8,128)(2,1)}, bf16[12,1024,128]{2,1,0:T(8,128)(2,1)}, f32[8,1,1024]{2,1,0:T(1,128)}, bf16[1024,512]{1,0:T(8,128)(2,...) custom-call(s32[2]{0:T(128)} %pad_add_fusion.z_ref, ...), custom_call_target="tpu_custom_call" | custom-call | flops 1000000 | bytes 100000 | tf_op jit(solution)/shard_map/attention_forward/pallas_call | solution.py:443
  72.2 13.9 %all_to_all.40.refs_1_ = bf16[8,4,16,512]{3,2,1,0:T(8,128)(2,1)} all-to-all(bf16[8,4,16,512]{3,2,1,0:T(8,128)(2,1)} %get-tuple-element.45), channel_id=1, replica_groups=mesh['batch'=8,'expert'=4] {'batch'}, dimensions={0} | all-to-all | bytes 1048576 | tf_op jit(solution)/shard_map/all_to_all | solution.py:1027
  86.2 24.5 %all_to_all.41.refs_2_.refs_3_ = bf16[8,3,4,16,512]{4,3,2,1,0:T(8,128)(2,1)S(1)} all-to-all(bf16[8,3,4,16,512]{4,3,2,1,0:T(8,128)(2,1)} %after.12), channel_id=1, replica_groups=mesh['batch'=8,'expert'=4] {'batch'}, dimensions={0} | all-to-all | bytes 3145728 | tf_op jit(solution)/shard_map/all_to_all | solution.py:1027
  112.1 19.6 %all-gather.6.cloned.1.call-done.refs_1_ = bf16[4,8,4,32,512]{4,3,2,1,0:T(8,128)(2,1)} async-done(((bf16[1,8,4,32,512]{4,3,2,1,0:T(8,128)(2,1)}), bf16[4,8,4,32,512]{4,3,2,1,0:T(8,128)(2,1)}) %all-gather.6.cloned.1.call-update) | async-done | bytes 4194320 | tf_op jit(solution)/shard_map/all_gather | solution.py:1009
  131.6 2.3 copy_bitcast_fusion
  133.9 3.7 all-to-all-start.2
  140.8 36.9 %all-gather.10.cloned.1.call-done = bf16[32,4,16,512]{3,2,1,0:T(8,128)(2,1)} async-done(((bf16[8,4,16,512]{3,2,1,0:T(8,128)(2,1)}), bf16[32,4,16,512]{3,2,1,0:T(8,128)(2,1)}) %all-gather.10.cloned.1.call-update) | async-done | bytes 2097168 | tf_op jit(solution)/shard_map/all_gather | solution.py:1033
  178.7 22.3 %mixture_forward.2 = (bf16[4,8,2,4,16,512]{5,4,3,2,1,0:T(8,128)(2,1)}, bf16[4,384,512]{2,1,0:T(8,128)(2,1)}, bf16[4,384,2048]{2,1,0:T(8,128)(2,1)}, bf16[4,384,2...) custom-call(s32[2]{0:T(128)} %pad_add_fusion.z_ref, ...), custom_call_target="tpu_custom_call" | custom-call | flops 1000000 | bytes 100000 | tf_op jit(solution)/shard_map/mixture_forward/pallas_call | solution.py:788
  201.0 23.5 %mixture_backward.2 = (bf16[4,8,4,16,512]{4,3,2,1,0:T(8,128)(2,1)}, bf16[4,384,512]{2,1,0:T(8,128)(2,1)}, bf16[4,384,2048]{2,1,0:T(8,128)(2,1)}, f32[16,512]{1,0:T(8,128)}) custom-call(s32[2]{0:T(128)} %pad_add_fusion.z_ref, bf16[4,8,4,16,512]{4,3,2,1,0:T(8,128)(2,1)} %bitcast.204, bf16[4,8,4,32,512]{4,3,2,1,0:T(8,128)(2,1)} %all-gather.6.cloned.1.call-done.refs_1_, ...), custom_call_target="tpu_custom_call" | custom-call | flops 1000000 | bytes 100000 | tf_op jit(solution)/shard_map/mixture_backward/pallas_call | solution.py:823
  224.9 22.4 %mixture_forward.3 = (bf16[4,8,2,4,16,512]{5,4,3,2,1,0:T(8,128)(2,1)}, bf16[4,384,512]{2,1,0:T(8,128)(2,1)}, bf16[4,384,2048]{2,1,0:T(8,128)(2,1)}, bf16[4,384,2...) custom-call(s32[2]{0:T(128)} %pad_add_fusion.z_ref, ...), custom_call_target="tpu_custom_call", output_to_operand_aliasing={{0}: (2, {})} | custom-call | flops 1000000 | bytes 100000 | tf_op jit(solution)/shard_map/mixture_forward/pallas_call | solution.py:788
  247.2 23.4 %mixture_backward.3 = (bf16[4,8,4,16,512]{4,3,2,1,0:T(8,128)(2,1)}, bf16[4,384,512]{2,1,0:T(8,128)(2,1)}, bf16[4,384,2048]{2,1,0:T(8,128)(2,1)}, f32[16,512]{1,0:T(8,128)}) custom-call(s32[2]{0:T(128)} %pad_add_fusion.z_ref, bf16[4,8,4,16,512]{4,3,2,1,0:T(8,128)(2,1)} %bitcast.199, bf16[4,8,4,32,512]{4,3,2,1,0:T(8,128)(2,1)} %all-gather.6.cloned.1.call-done.refs_1_, ...), custom_call_target="tpu_custom_call" | custom-call | flops 1000000 | bytes 100000 | tf_op jit(solution)/shard_map/mixture_backward/pallas_call | solution.py:823
  271.8 13.5 %all_to_all.42.refs_0_ = bf16[8,4,16,512]{3,2,1,0:T(8,128)(2,1)} all-to-all(bf16[8,4,16,512]{3,2,1,0:T(8,128)(2,1)S(1)} %bitcast.212), channel_id=1, replica_groups=mesh['batch'=8,'expert'=4] {'batch'}, dimensions={0} | all-to-all | bytes 1048576 | tf_op jit(solution)/shard_map/all_to_all | solution.py:1027
  285.3 23.3 %weight_grads.1 = (bf16[2,2,2,2,2,512,256]{6,5,4,3,2,1,0:T(8,128)(2,1)}, bf16[2,2,2,2,2,512,256]{6,5,4,3,2,1,0:T(8,128)(2,1)}) custom-call(s32[2]{0:T(128)} %pad_add_fusion.z_ref, bf16[4,384,512]{2,1,0:T(8,128)(2,1)} %get-tuple-element.64.m0, bf16[4,384,512]{2,1,0:T(8,128)(2,1)} %get-tuple-element.65.m1, bf16[4,384,2048]{2,1,0:T(8,128)(2,1)} %get-tuple-element.66.p0, ...), custom_call_target="tpu_custom_call" | custom-call | flops 1000000 | bytes 100000 | tf_op jit(solution)/shard_map/weight_grads/pallas_call | solution.py:875
  308.6 6.7 %reduce-scatter.6.cloned.1.call-done = bf16[1,8,4,16,512]{4,3,2,1,0:T(8,128)(2,1)} async-done(((bf16[4,8,4,16,512]{4,3,2,1,0:T(8,128)(2,1)}), bf16[1,8,4,16,512]{4,3,2,1,0:T(8,128)(2,1)}) %reduce-scatter.6.cloned.1.call-update) | async-done | bytes 524304 | tf_op jit(solution)/shard_map/reduce_scatter | solution.py:1051
  316.1 5.8 %fusion.40 = (bf16[1,1,2,2,2,512,256]{6,5,4,3,2,1,0:T(8,128)(2,1)S(1)}, bf16[1,1,2,2,2,512,256]{6,5,4,3,2,1,0:T(8,128)(2,1)}, bf16[1,1,2,2,2,512,256]{6,5,4,3,2,...) fusion(bf16[2,2,2,2,2,512,256]{6,5,4,3,2,1,0:T(8,128)(2,1)} %get-tuple-element.72), kind=kLoop, calls=%fused_computation.129 | loop fusion | bytes 16777216 | tf_op jit(solution)/shard_map/slice | solution.py:952
  321.9 4.1 all-to-all-start.4
  326.0 2.8 collective-permute-done.10
  328.8 5.2 %fusion.41 = (bf16[1,1,2,2,2,512,256]{6,5,4,3,2,1,0:T(8,128)(2,1)}, bf16[1,1,2,2,2,512,256]{6,5,4,3,2,1,0:T(8,128)(2,1)}, bf16[1,1,2,2,2,512,256]{6,5,4,3,2,1,0:...) fusion(bf16[2,2,2,2,2,512,256]{6,5,4,3,2,1,0:T(8,128)(2,1)} %collective-permute-done.10), kind=kLoop, calls=%fused_computation.130 | loop fusion | bytes 16777216 | tf_op jit(solution)/shard_map/slice | solution.py:952
  334.3 1.5 collective-permute-start.11
  338.5 1.5 collective-permute-start.12
  340.0 26.8 %attention_backward.1 = (bf16[1024,512]{1,0:T(8,128)(2,1)}, bf16[512,2048]{1,0:T(8,128)(2,1)}, f32[1,512]{1,0:T(1,128)}, f32[1,512]{1,0:T(1,128)}) custom-call(bf16[8,4,16,512]{3,2,1,0:T(8,128)(2,1)} %all_to_all.42.refs_0_, bf16[8,4,16,512]{3,2,1,0:T(8,128)(2,1)} %all-to-all-done.4.refs_1_, bf16[8,4,32,512]{3,2,1,0:T(8,128)(2,1)} %copy-done.5, ...), custom_call_target="tpu_custom_call" | custom-call | flops 1000000 | bytes 100000 | tf_op jit(solution)/shard_map/attention_backward/pallas_call | solution.py:557
  367.7 2.8 fusion.14.refs_0_
  371.0 2.5 fusion.12.refs_0_
  373.4 1.5 collective-permute-start.18
  375.0 3.2 fusion.6.refs_1_
  378.2 2.7 fusion.5.refs_2_
  380.9 1.8 fusion.1
  384.2 2.3 constant_dynamic-slice_fusion
  386.5 1.5 collective-permute-start.16
  389.9 5.9 %collective-permute-done.21 = bf16[2,2,512,256]{3,2,1,0:T(8,128)(2,1)} collective-permute-done((bf16[2,2,512,256]{3,2,1,0:T(8,128)(2,1)}, bf16[2,2,512,256]{3,2,1,0:T(8,128)(2,1)}, u32[]{:S(2)}, u32[]{:S(2)}) %collective-permute-start.21) | collective-permute-done | bytes 1048608 | tf_op jit(solution)/shard_map/ppermute | solution.py:960
  395.8 2.1 fusion.3
  398.9 1.5 collective-permute-start.22
  400.3 2.7 fusion.4
  403.6 2.5 fusion.2
  406.2 3.5 all-to-all-start.5
  409.7 1.9 dynamic-slice_bitcast_fusion.3
  411.6 2.0 collective-permute-start.19
  413.6 2.1 collective-permute-done.15
  415.7 1.5 collective-permute-start.17
  417.2 2.2 pad_maximum_fusion
  419.4 2.8 gather_fusion.1
  422.2 3.7 convert_add_fusion.5
  425.9 2.0 fusion.22
  427.9 7.3 %all-to-all-done.5 = bf16[4,64,2176]{2,1,0:T(8,128)(2,1)S(1)} async-done(((bf16[4,64,2176]{2,1,0:T(8,128)(2,1)}), bf16[4,64,2176]{2,1,0:T(8,128)(2,1)S(1)}, u32[]{:S(2)}, u32[]{:S(2)}) %all-to-all-start.5) | async-done | bytes 1114144 | tf_op jit(solution)/shard_map/all_to_all | solution.py:1083
  436.1 4.8 %all-to-all-start.7 = ((bf16[4,16,2176]{2,1,0:T(8,128)(2,1)}), bf16[4,16,2176]{2,1,0:T(8,128)(2,1)S(1)}, u32[]{:S(2)}, u32[]{:S(2)}) async-start(bf16[4,16,2176]{2,1,0:T(8,128)(2,1)} %bitcast.60), calls=%async_computation.10 | async-start | bytes 557056 | tf_op jit(solution)/shard_map/all_to_all | solution.py:1088
  440.9 2.0 fusion.21
  442.8 2.0 fusion.20
  444.8 3.0 all-to-all-done.7
  447.8 3.7 all-to-all-start.6
  452.7 1.4 maximum_convert_fusion
  454.1 1.7 slice_bitcast_fusion
  455.8 1.8 copy.97
  460.2 6.7 %all-to-all-done.6 = bf16[8,2,4,16,512]{4,3,2,1,0:T(8,128)(2,1)S(1)} async-done(((bf16[8,2,4,16,512]{4,3,2,1,0:T(8,128)(2,1)}), bf16[8,2,4,16,512]{4,3,2,1,0:T(8,128)(2,1)S(1)}, u32[]{:S(2)}, u32[]{:S(2)}) %all-to-all-start.6) | async-done | bytes 1048608 | tf_op jit(solution)/shard_map/all_to_all | solution.py:1027
  468.8 1.8 add.285
  (194 shorter events, 35.2 us)
Async XLA Ops:
  7.2 132.4 %copy-start = (bf16[512,16]{0,1:T(8,128)(2,1)S(1)}, bf16[512,16]{0,1:T(8,128)(2,1)}, u32[]{:S(2)}) copy-start(bf16[512,16]{0,1:T(8,128)(2,1)} %param.15) | copy-start | bytes 49156
  7.2 124.4 %all-gather.6.cloned.1.call-start = ((), (), s32[]{:S(2)}) async-start(), calls=%async_computation.11 | async-start | bytes 5242880 | tf_op jit(solution)/shard_map/all_gather | solution.py:1009
  7.3 9.9 %copy-start.20 = (f32[2,2,256,512]{3,2,1,0:T(8,128)S(1)}, f32[2,2,256,512]{3,2,1,0:T(8,128)}, u32[]{:S(2)}) copy-start(f32[2,2,256,512]{3,2,1,0:T(8,128)} %param.12) | copy-start | bytes 6291460
  10.2 12.5 %collective-permute-start = (bf16[256,512]{1,0:T(8,128)(2,1)}, bf16[256,512]{1,0:T(8,128)(2,1)S(1)}, u32[]{:S(2)}, u32[]{:S(2)}) collective-permute-start(bf16[256,512]{1,0:T(8,128)(2,1)} %get-tuple-element.140), channel_id=1, source_target_pairs={{0,1},{1,2},{2,3},{3,0},{4,5},{5,6},{6,7},{7,4},{8,9},{9,10},{10,1... | collective-permute-start | bytes 786440 | tf_op jit(solution)/shard_map/ppermute | solution.py:937
  13.2 20.0 %collective-permute-start.1 = (bf16[256,512]{1,0:T(8,128)(2,1)}, bf16[256,512]{1,0:T(8,128)(2,1)}, u32[]{:S(2)}, u32[]{:S(2)}) collective-permute-start(bf16[256,512]{1,0:T(8,128)(2,1)} %get-tuple-element.139), channel_id=1, source_target_pairs={{0,2},{1,3},{2,0},{3,1},{4,6},{5,7},{6,4},{7,5},{8,10},{9,11},{10,... | collective-permute-start | bytes 786440 | tf_op jit(solution)/shard_map/ppermute | solution.py:937
  15.8 18.5 %collective-permute-start.2 = (bf16[256,512]{1,0:T(8,128)(2,1)}, bf16[256,512]{1,0:T(8,128)(2,1)}, u32[]{:S(2)}, u32[]{:S(2)}) collective-permute-start(bf16[256,512]{1,0:T(8,128)(2,1)} %get-tuple-element.138), channel_id=1, source_target_pairs={{0,3},{1,0},{2,1},{3,2},{4,7},{5,4},{6,5},{7,6},{8,11},{9,8},{10,9... | collective-permute-start | bytes 786440 | tf_op jit(solution)/shard_map/ppermute | solution.py:937
  18.1 2.6 collective-permute-start.3
  18.1 18.6 %collective-permute-start.4 = (bf16[4,32,512]{2,1,0:T(8,128)(2,1)}, bf16[4,32,512]{2,1,0:T(8,128)(2,1)}, u32[]{:S(2)}, u32[]{:S(2)}) collective-permute-start(bf16[4,32,512]{2,1,0:T(8,128)(2,1)} %get-tuple-element.132), channel_id=1, source_target_pairs={{0,8},{4,12},{8,0},{12,4},{16,24},{20,28},{24,16},{28,20},{1,9},{5... | collective-permute-start | bytes 393224 | tf_op jit(solution)/shard_map/ppermute | solution.py:1005
  20.7 15.0 %copy-start.29 = (bf16[4,32,512]{2,1,0:T(8,128)(2,1)}, bf16[4,32,512]{2,1,0:T(8,128)(2,1)S(1)}, u32[]{:S(2)}) copy-start(bf16[4,32,512]{2,1,0:T(8,128)(2,1)S(1)} %collective-permute-done.3.refs_0_) | copy-start | bytes 393220
  20.7 18.3 %collective-permute-start.5 = (bf16[4,32,512]{2,1,0:T(8,128)(2,1)}, bf16[4,32,512]{2,1,0:T(8,128)(2,1)S(1)}, u32[]{:S(2)}, u32[]{:S(2)}) collective-permute-start(bf16[4,32,512]{2,1,0:T(8,128)(2,1)} %get-tuple-element.131), channel_id=1, source_target_pairs={{0,12},{4,8},{8,4},{12,0},{16,28},{20,24},{24,20},{28,16},{1,13},{... | collective-permute-start | bytes 393224 | tf_op jit(solution)/shard_map/ppermute | solution.py:1005
  22.7 13.0 %copy-start.28 = (bf16[256,512]{1,0:T(8,128)(2,1)}, bf16[256,512]{1,0:T(8,128)(2,1)S(1)}, u32[]{:S(2)}) copy-start(bf16[256,512]{1,0:T(8,128)(2,1)S(1)} %collective-permute-done.refs_1_) | copy-start | bytes 786436
  22.7 16.4 %collective-permute-start.6 = (bf16[4,32,512]{2,1,0:T(8,128)(2,1)}, bf16[4,32,512]{2,1,0:T(8,128)(2,1)S(1)}, u32[]{:S(2)}, u32[]{:S(2)}) collective-permute-start(bf16[4,32,512]{2,1,0:T(8,128)(2,1)} %get-tuple-element.130), channel_id=1, source_target_pairs={{0,16},{4,20},{8,24},{12,28},{16,0},{20,4},{24,8},{28,12},{1,17},{... | collective-permute-start | bytes 393224 | tf_op jit(solution)/shard_map/ppermute | solution.py:1005
  33.2 11.5 %collective-permute-start.7 = (bf16[4,32,512]{2,1,0:T(8,128)(2,1)}, bf16[4,32,512]{2,1,0:T(8,128)(2,1)S(1)}, u32[]{:S(2)}, u32[]{:S(2)}) collective-permute-start(bf16[4,32,512]{2,1,0:T(8,128)(2,1)} %get-tuple-element.129), channel_id=1, source_target_pairs={{0,20},{4,16},{8,28},{12,24},{16,4},{20,0},{24,12},{28,8},{1,21},{... | collective-permute-start | bytes 393224 | tf_op jit(solution)/shard_map/ppermute | solution.py:1005
  34.3 10.5 %collective-permute-start.8 = (bf16[4,32,512]{2,1,0:T(8,128)(2,1)}, bf16[4,32,512]{2,1,0:T(8,128)(2,1)S(1)}, u32[]{:S(2)}, u32[]{:S(2)}) collective-permute-start(bf16[4,32,512]{2,1,0:T(8,128)(2,1)} %get-tuple-element.128), channel_id=1, source_target_pairs={{0,24},{4,28},{8,16},{12,20},{16,8},{20,12},{24,0},{28,4},{1,25},{... | collective-permute-start | bytes 393224 | tf_op jit(solution)/shard_map/ppermute | solution.py:1005
  35.7 9.8 %copy-start.34 = (pred[8]{0:T(512)(128)(4,1)S(1)}, pred[8]{0:T(512)(128)(4,1)}, u32[]{:S(2)}) copy-start(pred[8]{0:T(512)(128)(4,1)} %compare_and_fusion.1) | copy-start | bytes 28
  36.6 8.1 %collective-permute-start.9 = (bf16[4,32,512]{2,1,0:T(8,128)(2,1)}, bf16[4,32,512]{2,1,0:T(8,128)(2,1)S(1)}, u32[]{:S(2)}, u32[]{:S(2)}) collective-permute-start(bf16[4,32,512]{2,1,0:T(8,128)(2,1)} %get-tuple-element.127), channel_id=1, source_target_pairs={{0,28},{4,24},{8,20},{12,16},{16,12},{20,8},{24,4},{28,0},{1,29},{... | collective-permute-start | bytes 393224 | tf_op jit(solution)/shard_map/ppermute | solution.py:1005
  46.7 131.0 %all-gather.10.cloned.1.call-start = ((), (), s32[]{:S(2)}) async-start(), calls=%async_computation.16 | async-start | bytes 2621440 | tf_op jit(solution)/shard_map/all_gather | solution.py:1033
  86.1 138.5 %all-gather.8.cloned.1.call-start = ((), (), s32[]{:S(2)}) async-start(), calls=%async_computation.15 | async-start | bytes 2621440 | tf_op jit(solution)/shard_map/all_gather | solution.py:1035
  86.1 25.5 %copy-start.33 = (s32[2,3]{1,0:T(2,128)S(1)}, s32[2,3]{1,0:T(2,128)}, u32[]{:S(2)}) copy-start(s32[2,3]{1,0:T(2,128)} %param.20) | copy-start | bytes 76
  110.6 23.3 %copy-start.2 = (bf16[8,3,4,16,512]{4,3,2,1,0:T(8,128)(2,1)}, bf16[8,3,4,16,512]{4,3,2,1,0:T(8,128)(2,1)S(1)}, u32[]{:S(2)}) copy-start(bf16[8,3,4,16,512]{4,3,2,1,0:T(8,128)(2,1)S(1)} %all_to_all.41.refs_2_.refs_3_) | copy-start | bytes 4718596
  112.1 26.5 %copy-start.35 = (s32[2,16]{1,0:T(2,128)S(1)}, s32[2,16]{1,0:T(2,128)}, u32[]{:S(2)}) copy-start(s32[2,16]{1,0:T(2,128)} %param.21) | copy-start | bytes 388
  133.9 43.8 %all-to-all-start.2 = ((bf16[8,4,32,512]{3,2,1,0:T(8,128)(2,1)}), bf16[8,4,32,512]{3,2,1,0:T(8,128)(2,1)S(1)}, u32[]{:S(2)}, u32[]{:S(2)}) async-start(bf16[8,4,32,512]{3,2,1,0:T(8,128)(2,1)} %copy_bitcast_fusion), calls=%async_computation.2 | async-start | bytes 2097152 | tf_op jit(solution)/shard_map/all_to_all | solution.py:1027
  137.6 133.0 %reduce-scatter.4.cloned.1.call-start = ((), (), s32[]{:S(2)}) async-start(), calls=%async_computation.12 | async-start | bytes 2621440 | tf_op jit(solution)/shard_map/reduce_scatter | solution.py:1045
  138.4 39.3 %copy-start.30 = (f32[2,3,256]{2,1,0:T(4,128)}, f32[2,3,256]{2,1,0:T(4,128)S(1)}, u32[]{:S(2)}) copy-start(f32[2,3,256]{2,1,0:T(4,128)S(1)} %copy.91.refs_4_.refs_3_.refs_5_) | copy-start | bytes 18436
  224.6 90.7 %reduce-scatter.6.cloned.1.call-start = ((), (), s32[]{:S(2)}) async-start(), calls=%async_computation.13 | async-start | bytes 2621440 | tf_op jit(solution)/shard_map/reduce_scatter | solution.py:1051
  270.7 174.1 %reduce-scatter.8.cloned.1.call-start = ((), (), s32[]{:S(2)}) async-start(), calls=%async_computation.14 | async-start | bytes 5242880 | tf_op jit(solution)/shard_map/reduce_scatter | solution.py:1055
  315.3 13.5 %collective-permute-start.10 = (bf16[2,2,2,2,2,512,256]{6,5,4,3,2,1,0:T(8,128)(2,1)}, bf16[2,2,2,2,2,512,256]{6,5,4,3,2,1,0:T(8,128)(2,1)}, u32[]{:S(2)}, u32[]{:S(2)}) collective-permute-start(bf16[2,2,2,2,2,512,256]{6,5,4,3,2,1,0:T(8,128)(2,1)} %after.16), channel_id=1, source_target_pairs={{0,4},{4,0},{8,12},{12,8},{16,20},{20,16},{24,28},{28,24},{1,5},{5... | collective-permute-start | bytes 25165832 | tf_op jit(solution)/shard_map/ppermute | solution.py:1058
  321.9 49.1 %copy-start.9 = (bf16[1,1,2,2,2,512,256]{6,5,4,3,2,1,0:T(8,128)(2,1)}, bf16[1,1,2,2,2,512,256]{6,5,4,3,2,1,0:T(8,128)(2,1)S(1)}, u32[]{:S(2)}) copy-start(bf16[1,1,2,2,2,512,256]{6,5,4,3,2,1,0:T(8,128)(2,1)S(1)} %get-tuple-element.117) | copy-start | bytes 6291460
  321.9 18.2 %all-to-all-start.4 = ((bf16[8,4,16,512]{3,2,1,0:T(8,128)(2,1)}), bf16[8,4,16,512]{3,2,1,0:T(8,128)(2,1)}, u32[]{:S(2)}, u32[]{:S(2)}) async-start(bf16[8,4,16,512]{3,2,1,0:T(8,128)(2,1)} %bitcast.36.refs_1_), calls=%async_computation.7 | async-start | bytes 1048576 | tf_op jit(solution)/shard_map/all_to_all | solution.py:1027
  326.0 8.0 %copy-start.15 = (bf16[1,1,2,2,2,512,256]{6,5,4,3,2,1,0:T(8,128)(2,1)S(1)}, bf16[1,1,2,2,2,512,256]{6,5,4,3,2,1,0:T(8,128)(2,1)}, u32[]{:S(2)}) copy-start(bf16[1,1,2,2,2,512,256]{6,5,4,3,2,1,0:T(8,128)(2,1)} %get-tuple-element.120) | copy-start | bytes 6291460
  334.0 4.5 copy-start.17
  334.0 4.5 copy-start.19
  334.0 1.8 copy-start.32
  334.0 3.2 copy-start.13
  334.3 5.8 %copy-start.24 = (bf16[2,2,512,256]{3,2,1,0:T(8,128)(2,1)}, bf16[2,2,512,256]{3,2,1,0:T(8,128)(2,1)S(1)}, u32[]{:S(2)}) copy-start(bf16[2,2,512,256]{3,2,1,0:T(8,128)(2,1)S(1)} %fusion.7.refs_12_) | copy-start | bytes 3145732
  334.3 40.7 %collective-permute-start.11 = (bf16[2,2,512,256]{3,2,1,0:T(8,128)(2,1)S(1)}, bf16[2,2,512,256]{3,2,1,0:T(8,128)(2,1)}, u32[]{:S(2)}, u32[]{:S(2)}) collective-permute-start(bf16[2,2,512,256]{3,2,1,0:T(8,128)(2,1)S(1)} %fusion.7.refs_12_), channel_id=1, source_target_pairs={{0,8},{4,12},{8,0},{12,4},{16,24},{20,28},{24,16},{28,20},{1,9},{5... | collective-permute-start | bytes 3145736 | tf_op jit(solution)/shard_map/ppermute | solution.py:960
  338.5 39.7 %collective-permute-start.12 = (bf16[2,2,512,256]{3,2,1,0:T(8,128)(2,1)}, bf16[2,2,512,256]{3,2,1,0:T(8,128)(2,1)}, u32[]{:S(2)}, u32[]{:S(2)}) collective-permute-start(bf16[2,2,512,256]{3,2,1,0:T(8,128)(2,1)} %fusion.8.refs_13_), channel_id=1, source_target_pairs={{0,16},{4,20},{8,24},{12,28},{16,0},{20,4},{24,8},{28,12},{1,17},{... | collective-permute-start | bytes 3145736 | tf_op jit(solution)/shard_map/ppermute | solution.py:960
  370.5 25.3 %collective-permute-start.21 = (bf16[2,2,512,256]{3,2,1,0:T(8,128)(2,1)}, bf16[2,2,512,256]{3,2,1,0:T(8,128)(2,1)}, u32[]{:S(2)}, u32[]{:S(2)}) collective-permute-start(bf16[2,2,512,256]{3,2,1,0:T(8,128)(2,1)} %after.21), channel_id=1, source_target_pairs={{0,16},{4,20},{8,24},{12,28},{16,0},{20,4},{24,8},{28,12},{1,17},{... | collective-permute-start | bytes 3145736 | tf_op jit(solution)/shard_map/ppermute | solution.py:960
  373.4 4.8 copy-start.14
  373.4 4.8 copy-start.18
  373.4 25.4 %collective-permute-start.18 = (bf16[2,2,512,256]{3,2,1,0:T(8,128)(2,1)}, bf16[2,2,512,256]{3,2,1,0:T(8,128)(2,1)}, u32[]{:S(2)}, u32[]{:S(2)}) collective-permute-start(bf16[2,2,512,256]{3,2,1,0:T(8,128)(2,1)} %after.20), channel_id=1, source_target_pairs={{0,8},{4,12},{8,0},{12,4},{16,24},{20,28},{24,16},{28,20},{1,9},{5... | collective-permute-start | bytes 3145736 | tf_op jit(solution)/shard_map/ppermute | solution.py:960
  384.1 18.9 %collective-permute-start.13 = (bf16[4,64,2176]{2,1,0:T(8,128)(2,1)S(1)}, bf16[4,64,2176]{2,1,0:T(8,128)(2,1)}, u32[]{:S(2)}, u32[]{:S(2)}) collective-permute-start(bf16[4,64,2176]{2,1,0:T(8,128)(2,1)S(1)} %dynamic-slice_bitcast_fusion), channel_id=1, source_target_pairs={{0,4},{4,0},{8,12},{12,8},{16,20},{20,16},{24,28},{28,24},{1,5},{5... | collective-permute-start | bytes 3342344 | tf_op jit(solution)/shard_map/ppermute | solution.py:943
  384.2 4.0 copy-start.4
  384.2 4.9 %copy-start.3 = (bf16[2,2,512,256]{3,2,1,0:T(8,128)(2,1)S(1)}, bf16[2,2,512,256]{3,2,1,0:T(8,128)(2,1)}, u32[]{:S(2)}) copy-start(bf16[2,2,512,256]{3,2,1,0:T(8,128)(2,1)} %fusion.6.refs_1_) | copy-start | bytes 3145732
  384.2 11.6 %copy-start.11 = (bf16[1,1,2,2,2,512,256]{6,5,4,3,2,1,0:T(8,128)(2,1)S(1)}, bf16[1,1,2,2,2,512,256]{6,5,4,3,2,1,0:T(8,128)(2,1)}, u32[]{:S(2)}) copy-start(bf16[1,1,2,2,2,512,256]{6,5,4,3,2,1,0:T(8,128)(2,1)} %get-tuple-element.118) | copy-start | bytes 6291460
  386.5 25.1 %collective-permute-start.16 = (bf16[256,512]{1,0:T(8,128)(2,1)}, bf16[256,512]{1,0:T(8,128)(2,1)}, u32[]{:S(2)}, u32[]{:S(2)}) collective-permute-start(bf16[256,512]{1,0:T(8,128)(2,1)} %get-tuple-element.135), channel_id=1, source_target_pairs={{0,3},{1,0},{2,1},{3,2},{4,7},{5,4},{6,5},{7,6},{8,11},{9,8},{10,9... | collective-permute-start | bytes 786440 | tf_op jit(solution)/shard_map/ppermute | solution.py:937
  388.0 27.7 %collective-permute-start.15 = (bf16[256,512]{1,0:T(8,128)(2,1)}, bf16[256,512]{1,0:T(8,128)(2,1)}, u32[]{:S(2)}, u32[]{:S(2)}) collective-permute-start(bf16[256,512]{1,0:T(8,128)(2,1)} %get-tuple-element.136), channel_id=1, source_target_pairs={{0,2},{1,3},{2,0},{3,1},{4,6},{5,7},{6,4},{7,5},{8,10},{9,11},{10,... | collective-permute-start | bytes 786440 | tf_op jit(solution)/shard_map/ppermute | solution.py:937
  395.8 4.5 copy-start.10
  395.8 4.5 copy-start.12
  395.8 21.4 %collective-permute-start.14 = (bf16[256,512]{1,0:T(8,128)(2,1)}, bf16[256,512]{1,0:T(8,128)(2,1)}, u32[]{:S(2)}, u32[]{:S(2)}) collective-permute-start(bf16[256,512]{1,0:T(8,128)(2,1)} %get-tuple-element.137), channel_id=1, source_target_pairs={{0,1},{1,2},{2,3},{3,0},{4,5},{5,6},{6,7},{7,4},{8,9},{9,10},{10,1... | collective-permute-start | bytes 786440 | tf_op jit(solution)/shard_map/ppermute | solution.py:937
  397.9 5.1 %copy-start.22 = (bf16[2,2,512,256]{3,2,1,0:T(8,128)(2,1)}, bf16[2,2,512,256]{3,2,1,0:T(8,128)(2,1)S(1)}, u32[]{:S(2)}) copy-start(bf16[2,2,512,256]{3,2,1,0:T(8,128)(2,1)S(1)} %fusion.3) | copy-start | bytes 3145732
  398.9 4.8 %copy-start.7 = (bf16[512,2176]{1,0:T(8,128)(2,1)S(1)}, bf16[512,2176]{1,0:T(8,128)(2,1)}, u32[]{:S(2)}) copy-start(bf16[512,2176]{1,0:T(8,128)(2,1)} %copy-done.6) | copy-start | bytes 6684676
  398.9 27.0 %collective-permute-start.22 = (bf16[2,512,256]{2,1,0:T(8,128)(2,1)}, bf16[2,512,256]{2,1,0:T(8,128)(2,1)}, u32[]{:S(2)}, u32[]{:S(2)}) collective-permute-start(bf16[2,512,256]{2,1,0:T(8,128)(2,1)} %dynamic-slice_bitcast_fusion.1), channel_id=1, source_target_pairs={{0,8},{4,12},{8,0},{12,4},{16,24},{20,28},{24,16},{28,20},{1,9},{5... | collective-permute-start | bytes 1572872 | tf_op jit(solution)/shard_map/ppermute | solution.py:943
  403.0 37.9 %collective-permute-start.20 = (bf16[2,512,256]{2,1,0:T(8,128)(2,1)}, bf16[2,512,256]{2,1,0:T(8,128)(2,1)}, u32[]{:S(2)}, u32[]{:S(2)}) collective-permute-start(bf16[2,512,256]{2,1,0:T(8,128)(2,1)} %dynamic-slice_bitcast_fusion.2), channel_id=1, source_target_pairs={{0,8},{4,12},{8,0},{12,4},{16,24},{20,28},{24,16},{28,20},{1,9},{5... | collective-permute-start | bytes 1572872 | tf_op jit(solution)/shard_map/ppermute | solution.py:943
  406.2 29.0 %all-to-all-start.5 = ((bf16[4,64,2176]{2,1,0:T(8,128)(2,1)}), bf16[4,64,2176]{2,1,0:T(8,128)(2,1)S(1)}, u32[]{:S(2)}, u32[]{:S(2)}) async-start(bf16[4,64,2176]{2,1,0:T(8,128)(2,1)} %fusion.2), calls=%async_computation.8 | async-start | bytes 2228224 | tf_op jit(solution)/shard_map/all_to_all | solution.py:1083
  411.6 31.2 %collective-permute-start.19 = (bf16[2,512,256]{2,1,0:T(8,128)(2,1)}, bf16[2,512,256]{2,1,0:T(8,128)(2,1)}, u32[]{:S(2)}, u32[]{:S(2)}) collective-permute-start(bf16[2,512,256]{2,1,0:T(8,128)(2,1)} %dynamic-slice_bitcast_fusion.3), channel_id=1, source_target_pairs={{0,16},{4,20},{8,24},{12,28},{16,0},{20,4},{24,8},{28,12},{1,17},{... | collective-permute-start | bytes 1572872 | tf_op jit(solution)/shard_map/ppermute | solution.py:943
  415.7 35.8 %collective-permute-start.17 = (bf16[2,512,256]{2,1,0:T(8,128)(2,1)}, bf16[2,512,256]{2,1,0:T(8,128)(2,1)}, u32[]{:S(2)}, u32[]{:S(2)}) collective-permute-start(bf16[2,512,256]{2,1,0:T(8,128)(2,1)} %dynamic-slice_bitcast_fusion.4), channel_id=1, source_target_pairs={{0,16},{4,20},{8,24},{12,28},{16,0},{20,4},{24,8},{28,12},{1,17},{... | collective-permute-start | bytes 1572872 | tf_op jit(solution)/shard_map/ppermute | solution.py:943
  422.2 3.7 copy-start.23
  436.1 6.8 %copy-start.21 = (bf16[2,2,512,256]{3,2,1,0:T(8,128)(2,1)S(1)}, bf16[2,2,512,256]{3,2,1,0:T(8,128)(2,1)}, u32[]{:S(2)}) copy-start(bf16[2,2,512,256]{3,2,1,0:T(8,128)(2,1)} %fusion.4) | copy-start | bytes 3145732
  436.1 11.7 %all-to-all-start.7 = ((bf16[4,16,2176]{2,1,0:T(8,128)(2,1)}), bf16[4,16,2176]{2,1,0:T(8,128)(2,1)S(1)}, u32[]{:S(2)}, u32[]{:S(2)}) async-start(bf16[4,16,2176]{2,1,0:T(8,128)(2,1)} %bitcast.60), calls=%async_computation.10 | async-start | bytes 557056 | tf_op jit(solution)/shard_map/all_to_all | solution.py:1088
  444.8 7.9 %copy-start.25 = (bf16[1,2,512,256]{3,2,1,0:T(8,128)(2,1)S(1)}, bf16[1,2,512,256]{3,2,1,0:T(8,128)(2,1)}, u32[]{:S(2)}) copy-start(bf16[1,2,512,256]{3,2,1,0:T(8,128)(2,1)} %fusion.22) | copy-start | bytes 1572868
  444.8 7.9 %copy-start.27 = (bf16[1,2,512,256]{3,2,1,0:T(8,128)(2,1)S(1)}, bf16[1,2,512,256]{3,2,1,0:T(8,128)(2,1)}, u32[]{:S(2)}) copy-start(bf16[1,2,512,256]{3,2,1,0:T(8,128)(2,1)} %fusion.21) | copy-start | bytes 1572868
  447.8 19.1 %all-to-all-start.6 = ((bf16[8,2,4,16,512]{4,3,2,1,0:T(8,128)(2,1)}), bf16[8,2,4,16,512]{4,3,2,1,0:T(8,128)(2,1)S(1)}, u32[]{:S(2)}, u32[]{:S(2)}) async-start(bf16[8,2,4,16,512]{4,3,2,1,0:T(8,128)(2,1)} %after.18), calls=%async_computation.9 | async-start | bytes 2097152 | tf_op jit(solution)/shard_map/all_to_all | solution.py:1027
  467.4 3.2 copy-start.1
  (6 other events, 7.3 us)
Sparse Core Ops, SparseCore 0:
  46.8 84.7 all-gather.5
  133.2 44.4 all-gather.9
  179.3 44.6 all-gather.7
  226.7 42.5 reduce-scatter.3
  272.1 43.1 reduce-scatter.5
  317.5 76.6 reduce-scatter.7

commit v4 on v3

--- a/solution.py
+++ b/solution.py
@@ -731,7 +731,7 @@
     @pl.when(e == experts - 1)
     def _():
         dctrl = jnp.zeros(dctrl_ref.shape, F32)
-        ctrl8 = ctrl_ref[:8, :].astype(F32)
+        ctrl8 = ctrl_ref[...].astype(F32)[:8]
         ctrl_twice = jnp.concatenate([ctrl8, ctrl8], 0).astype(BF16)
         for m in range(micro):
             for q in range(quarters):
@@ -930,11 +930,14 @@
     return (rising + falling + own(z)).astype(BF16)
 
 
-def to_planes(parts, z, count):
-    got = [pick(parts, z)]
+def for_planes(parts, z, count):
+    return [pick(parts, lax.rem(z + k, count)) for k in range(count)]
+
+
+def to_planes(picked, count):
+    got = picked[:1]
     for k in range(1, count):
-        part = pick(parts, lax.rem(z + k, count))
-        got.append(lax.ppermute(part, "expert", [(i, (i + k) % count) for i in range(count)]))
+        got.append(lax.ppermute(picked[k], "expert", [(i, (i + k) % count) for i in range(count)]))
     return got
 
 
@@ -944,27 +947,143 @@
     return (pick(blocks, mine).astype(F32) + other.astype(F32)).astype(BF16)
 
 
-def first_halves(keep, came):
-    own = lax.axis_index("batch")
-    mine = [lax.rem(own >> bit, 2) for bit in (1, 2)]
-
-    def part(half, expert, index):
-        return (pick(keep[half, expert], index).astype(F32) + pick(came[half, expert], index).astype(F32)).astype(BF16)
-
-    experts = range(keep.shape[1])
-    return ([[part(i, e, mine[i]) for e in experts] for i in range(2)],
-            [[part(i, e, 1 - mine[i]) for e in experts] for i in range(2)])
-
-
-def hop(keep, send, bit):
-    came = lax.ppermute(send, "batch", [(j, j ^ (1 << bit)) for j in range(8)])
-    return (keep.astype(F32) + came.astype(F32)).astype(BF16)
-
-
-def second_hop(held):
-    both = [swap_halves(part, 2 - i, 8) for i in range(2) for part in held[i]]
-    both = jnp.stack(both).astype(F32)
-    return both[:, 0], both[:, 1].transpose(0, 2, 1)
+def hop_bits(half):
+    return (1, 2) if half == 0 else (2, 1)
+
+
+def add_blocks(*refs):
+    total = refs[0][...].astype(F32)
+    for ref in refs[1:]:
+        total += ref[...].reshape(total.shape).astype(F32)
+    return total
+
+
+def first_sends_kernel(pos_ref, *refs):
+    ins, outs = refs[:8], refs[-4:]
+    for i, out in enumerate(outs):
+        out[...] = add_blocks(*ins[2 * i:2 * i + 2]).astype(BF16).reshape(out.shape)
+
+
+def first_sends(pos, keep, came, waits=()):
+    halves, experts, _, _, _, rows, cols = keep.shape
+    pieces = [(i, e) for i in range(halves) for e in range(experts)]
+
+    def place(i, e):
+        bit = hop_bits(i)[0]
+        return lambda h, w, pos: (i, e, 1 - lax.rem(pos[1] >> bit, 2), h, w, 0, 0)
+
+    block = (1, 1, 1, 1, 1, rows, cols)
+    out = pl.BlockSpec((1, 1, rows, cols), lambda h, w, pos: (h, w, 0, 0))
+    return pl.pallas_call(
+        first_sends_kernel,
+        grid_spec=pltpu.PrefetchScalarGridSpec(
+            num_scalar_prefetch=1, grid=(2, 2),
+            in_specs=[pl.BlockSpec(block, place(i, e)) for i, e in pieces for _ in range(2)]
+            + [pl.BlockSpec(memory_space=pl.ANY)] * len(waits),
+            out_specs=(out,) * len(pieces)),
+        out_shape=(jax.ShapeDtypeStruct((2, 2, rows, cols), BF16),) * len(pieces),
+        compiler_params=pltpu.CompilerParams(vmem_limit_bytes=VMEM_LIMIT),
+        cost_estimate=SMALL_COST,
+        name="first_sends",
+    )(pos, *[array for _ in pieces for array in (keep, came)], *waits)
+
+
+def second_sends_kernel(pos_ref, *refs):
+    ins, outs = refs[:-4], refs[-4:]
+    for i, out in enumerate(outs):
+        out[...] = add_blocks(*ins[3 * i:3 * i + 3]).astype(BF16).reshape(out.shape)
+
+
+def own_place(i, e, last):
+    first, second = hop_bits(i)
+
+    def place(w, pos):
+        mine = lax.rem(pos[1] >> second, 2)
+        return (i, e, lax.rem(pos[1] >> first, 2), jnp.where(last == 1, 1 - mine, mine), w, 0, 0)
+
+    def place_got(w, pos):
+        return place(w, pos)[3:]
+
+    return place, place_got
+
+
+def second_sends(pos, keep, came, got):
+    halves, experts, _, _, _, rows, cols = keep.shape
+    pieces = [(i, e) for i in range(halves) for e in range(experts)]
+    specs = []
+    for i, e in pieces:
+        place, place_got = own_place(i, e, 1)
+        specs += [pl.BlockSpec((1, 1, 1, 1, 1, rows, cols), place)] * 2
+        specs += [pl.BlockSpec((1, 1, rows, cols), place_got)]
+    out = pl.BlockSpec((1, rows, cols), lambda w, pos: (w, 0, 0))
+    return pl.pallas_call(
+        second_sends_kernel,
+        grid_spec=pltpu.PrefetchScalarGridSpec(
+            num_scalar_prefetch=1, grid=(2,), in_specs=specs, out_specs=(out,) * len(pieces)),
+        out_shape=(jax.ShapeDtypeStruct((2, rows, cols), BF16),) * len(pieces),
+        compiler_params=pltpu.CompilerParams(vmem_limit_bytes=VMEM_LIMIT),
+        cost_estimate=SMALL_COST,
+        name="second_sends",
+    )(pos, *[array for n in range(len(pieces)) for array in (keep, came, got[n])])
+
+
+def expert_sums_kernel(pos_ref, *refs):
+    ins, (first_ref, second_ref) = refs[:-2], refs[-2:]
+    for i in range(len(ins) // 4):
+        total = add_blocks(*ins[4 * i:4 * i + 4]).reshape(ins[4 * i].shape[-3:])
+        first_ref[i] = total[0]
+        second_ref[i] = total[1].T
+
+
+def expert_sums(pos, keep, came, got, got_last):
+    halves, experts, _, _, _, rows, cols = keep.shape
+    pieces = [(i, e) for i in range(halves) for e in range(experts)]
+    specs = []
+    for i, e in pieces:
+        place, place_got = own_place(i, e, 0)
+        specs += [pl.BlockSpec((1, 1, 1, 1, 2, rows, cols), place)] * 2
+        specs += [pl.BlockSpec((1, 2, rows, cols), place_got)]
+        specs += [pl.BlockSpec((2, rows, cols), lambda w, pos: (0, 0, 0))]
+    out = lambda shape: pl.BlockSpec(shape, lambda w, pos: (0, 0, 0))
+    shapes = (len(pieces), rows, cols), (len(pieces), cols, rows)
+    return pl.pallas_call(
+        expert_sums_kernel,
+        grid_spec=pltpu.PrefetchScalarGridSpec(
+            num_scalar_prefetch=1, grid=(1,), in_specs=specs, out_specs=tuple(out(s) for s in shapes)),
+        out_shape=tuple(jax.ShapeDtypeStruct(s, F32) for s in shapes),
+        compiler_params=pltpu.CompilerParams(vmem_limit_bytes=VMEM_LIMIT),
+        cost_estimate=SMALL_COST,
+        name="expert_sums",
+    )(pos, *[array for n in range(len(pieces)) for array in (keep, came, got[n], got_last[n])])
+
+
+def cross(block, bit):
+    return lax.ppermute(block, "batch", [(j, j ^ (1 << bit)) for j in range(8)])
+
+
+def add_home_kernel(z_ref, *refs):
+    n = len(refs) - 4
+    parts, (base_ref, out_ref, came, sems) = refs[:n], refs[n:]
+    copies = [
+        pltpu.make_async_copy(parts[k], came.at[lax.rem(z_ref[0] - k + n, n)], sems.at[k]) for k in range(n)]
+    for copy in copies:
+        copy.start()
+    for copy in copies:
+        copy.wait()
+    out_ref[...] = base_ref[...] + came[...].astype(F32)
+
+
+def add_home(z, parts, base):
+    vmem = pl.BlockSpec(memory_space=pltpu.VMEM)
+    return pl.pallas_call(
+        add_home_kernel,
+        out_shape=jax.ShapeDtypeStruct(base.shape, F32),
+        in_specs=[pl.BlockSpec(memory_space=pltpu.SMEM)] + [pl.BlockSpec(memory_space=pl.ANY)] * len(parts) + [vmem],
+        scratch_shapes=[pltpu.VMEM(base.shape, BF16), pltpu.SemaphoreType.DMA((len(parts),))],
+        compiler_params=pltpu.CompilerParams(vmem_limit_bytes=VMEM_LIMIT),
+        cost_estimate=SMALL_COST,
+        name="add_home",
+    )(z, *parts, base)
 
 
 def body(
@@ -995,7 +1114,7 @@
 
     own = lax.axis_index("batch")
     z_arr = jnp.stack([z, own]).astype(jnp.int32)
-    x_parts = to_planes(tokens.reshape(planes, local_len, width).astype(BF16), z, planes)
+    x_parts = to_planes(for_planes(tokens.reshape(planes, local_len, width).astype(BF16), z, planes), planes)
 
     cot = cotangent.reshape(planes, nb, piece, width)
     pieces = []
@@ -1004,7 +1123,7 @@
         if k:
             part = lax.ppermute(part, "batch", [(i, i ^ k) for i in range(nb)])
         pieces.append(part)
-    pieces[1] = after(pieces[1], *x_parts[1:])
+    pieces[-1] = after(pieces[-1], x_parts[2])
     cot = jnp.take(jnp.stack(pieces), own ^ jnp.arange(nb), axis=0)
     g_all = lax.all_gather(cot, "expert", axis=0, tiled=False)
 
@@ -1056,20 +1175,19 @@
     send = after(send, back1)
     back1 = over_batch(back1)
     came = lax.ppermute(send, "batch", [(i, i ^ 1) for i in range(nb)])
-    keeps, sends = first_halves(keep, came)
-
+    sends = first_sends(z_arr, keep, came, waits=(back1,))
     gin, dw, dg1, dg2 = attention_backward(
         back0, back1, cot_own, x, attn, ctx, qkv, lse, query_key_value_weight, output_weight, g1, g2,
-        waits=(sends[0][0], sends[1][0]))
-    sends = [[part if e == 0 else after(part, dg1) for e, part in enumerate(parts)] for parts in sends]
-    held = [[hop(keeps[i][e], sends[i][e], 1 + i) for e in range(len(sends[i]))] for i in range(2)]
-    gin = after(gin, held[0][0], held[1][0])
-    dw = after(dw, held[0][0], held[1][0])
-    grad_first, grad_second = second_hop(held)
-
-    got = jnp.stack(to_planes(gin.reshape(planes, local_len, width), z, planes))
-    gin = jnp.take(got, lax.rem(z - jnp.arange(planes) + planes, planes), axis=0)
-    grad_in = cotangent + gin.reshape(tokens.shape).astype(F32)
+        waits=sends)
+    firsts = [hop_bits(n // 2)[0] for n in range(4)]
+    got = [cross(sends[n], firsts[n]) for n in range(4)]
+    parts = to_planes(for_planes(gin.reshape(planes, local_len, width), z, planes), planes)
+    seconds = second_sends(z_arr, keep, came, got)
+    dw = after(dw, seconds[0])
+    got_last = [cross(part, hop_bits(n // 2)[1]) for n, part in enumerate(seconds)]
+    grad_first, grad_second = expert_sums(z_arr, keep, came, got, got_last)
+
+    grad_in = add_home(z_arr, parts, cotangent.reshape(planes, local_len, width)).reshape(tokens.shape)
 
     dctrl_all = jnp.zeros((planes, experts, width), F32)
     dctrl_all = lax.dynamic_update_slice(dctrl_all, dctrl[None, :experts], (z, 0, 0))
@@ -1082,7 +1200,8 @@
     chips = [[c + 2 * i for i in range(nb // 2)] for c in range(2)]
     flat = lax.all_to_all(flat, "batch", split_axis=0, concat_axis=0, tiled=True, axis_index_groups=chips)
     flat = jnp.sum(flat.astype(F32), 0).astype(BF16)
-    spread = over_batch(after(spread, flat))
+    flat = after(flat, grad_in)
+    spread = over_batch(after(spread, flat, *got_last))
     out = tokens + spread.transpose(2, 0, 1, 3, 4).reshape(tokens.shape).astype(F32)
     flat = flat.reshape(planes, -1, flat.shape[1])
     flat = lax.all_to_all(flat, "expert", split_axis=0, concat_axis=0, tiled=True)

time: 486 us -> 473 us (0.973)
  other arithmetic: 46.9 us -> 15 us
  Pallas kernels: 165 us -> 188 us
  local copies, waits for them, and re-layouts: 43.8 us -> 24.9 us
  blocking collectives: 51.9 us -> 67.3 us
    ppermute x10 -> x14, waiting for transfers between devices: 18.3 us -> 47.7 us  [the longest x6 30.8 us: to_planes(): lax.ppermute(picked[k], 'expert', [(i, (i + k) % count) for i in range(co...]
    pallas_call x0 -> x4, Pallas kernels: none -> 22.7 us  [the longest x1 6.73 us: expert_sums(): pl.pallas_call(expert_sums_kernel, grid_spec=pltpu.PrefetchScalarGridSpec...]
    all_gather x1, waiting for transfers between devices: 19.6 us -> 0.01 us  [body(): g_all = lax.all_gather(cot, 'expert', axis=0, tiled=False)]
    convert_element_type x9 -> x0, other arithmetic: 18.9 us -> none  [the longest x4 10.6 us: hop(): return (keep.astype(F32) + came.astype(F32)).astype(BF16)]
    all_to_all x3 -> x4, blocking collectives: 51.9 us -> 67.3 us  [over_batch(): lax.all_to_all(block, 'batch', split_axis=0, concat_axis=0, tiled=True)]
    slice x2 -> x0, local copies, waits for them, and re-layouts: 10.9 us -> none  [the longest x1 5.78 us: part(): keep[half, expert]]
    another operation x5 -> x0, other arithmetic: 9.31 us -> none  [the longest x4 7.1 us: second_hop(): both = jnp.stack(both).astype(F32)]
    ppermute x10 -> x14, starting transfers between devices: 13.7 us -> 22.7 us  [the longest x6 12.7 us: to_planes(): lax.ppermute(picked[k], 'expert', [(i, (i + k) % count) for i in range(co...]
  transfers between devices with their start and end apart: 34 -> 33, of which waited for: 12 -> 14; matrix products, arithmetic and copies ran while one was open for 16% -> 5% of each run, Pallas kernels for 35% -> 40%
where the time goes in v4:
time: 473 us; the launch traced here: 465 us
  Pallas kernels  188 us (40%)
  waiting for transfers between devices  106 us (22%)
  blocking collectives  67.3 us (14%)
  starting transfers between devices  49 us (10%)
  local copies, waits for them, and re-layouts  24.9 us (5%)
  other arithmetic  15 us (3%)
  between operations  14.9 us (3%)
    all_to_all x4, blocking collectives, over_batch(): lax.all_to_all(block, 'batch', split_axis=0, concat_axis=0, tiled=True)  67.3 us
    pallas_call x2, Pallas kernels, mixture_backward(): pl.pallas_call(functools.partial(mixture_backward_kernel, chunk, parts, l...  46.8 us
    pallas_call x2, Pallas kernels, mixture_forward(): pl.pallas_call(functools.partial(mixture_forward_kernel, chunk, len(x_par...  44.8 us
    all_gather x1, waiting for transfers between devices, body(): x0 = [lax.all_gather(own0, 'expert', axis=0, tiled=False)]  31.4 us
    ppermute x6, waiting for transfers between devices, to_planes(): lax.ppermute(picked[k], 'expert', [(i, (i + k) % count) for i in range(co...  30.8 us
    pallas_call x1, Pallas kernels, attention_backward(): pl.pallas_call(functools.partial(attention_backward_kernel, len(waits)),...  26.5 us
    pallas_call x1, Pallas kernels, attention_forward(): pl.pallas_call(functools.partial(attention_forward_kernel, len(waits)), i...  23.7 us
    pallas_call x1, Pallas kernels, weight_grads(): pl.pallas_call(weight_grads_kernel, grid=(experts,), in_specs=[pl.BlockSp...  23.4 us
  transfers between devices with their start and end apart: 33, of which 14 were waited for; matrix products, arithmetic and copies ran while one was open for 5% of the time, Pallas kernels for 40%

profile of v4, /device:TPU:0, one launch (start us, length us, event | category | flops | bytes accessed | tf_op | source)
XLA Modules:
  0.0 465.0 jit_solution(6489802899679168555)
XLA Ops:
  7.3 1.9 convert_element_type.117
  9.2 1.0 dynamic-slice_bitcast_fusion.5
  10.2 4.0 collective-permute-start.1
  15.1 1.5 collective-permute-start.4
  17.0 1.5 collective-permute-start.6
  19.8 0.9 bitcast_dynamic-update-slice_fusion.6
  20.8 1.0 collective-permute-done.4
  21.7 2.4 collective-permute-start.8
  24.2 0.9 bitcast_dynamic-update-slice_fusion.5
  25.1 1.1 collective-permute-start.9
  26.2 0.9 bitcast_dynamic-update-slice_fusion.4
  27.2 0.9 bitcast_dynamic-update-slice_fusion.3
  28.1 2.4 collective-permute-done.7
  34.4 1.1 bitcast_select_fusion
  35.7 1.6 collective-permute-start
  37.3 2.2 collective-permute-start.2
  40.1 1.1 broadcast_select_fusion.refs_4_
  41.3 5.4 %collective-permute-done.refs_1_ = bf16[256,512]{1,0:T(8,128)(2,1)S(1)} collective-permute-done((bf16[256,512]{1,0:T(8,128)(2,1)S(1)}, bf16[256,512]{1,0:T(8,128)(2,1)S(1)}, u32[]{:S(2)}, u32[]{:S(2)}) %collective-permute-start) | collective-permute-done | bytes 262176 | tf_op jit(solution)/shard_map/ppermute | solution.py:940
  46.7 12.8 %collective-permute-done.2.refs_3_ = bf16[256,512]{1,0:T(8,128)(2,1)S(1)} collective-permute-done((bf16[256,512]{1,0:T(8,128)(2,1)S(1)}, bf16[256,512]{1,0:T(8,128)(2,1)S(1)}, u32[]{:S(2)}, u32[]{:S(2)}) %collective-permute-start.2) | collective-permute-done | bytes 262176 | tf_op jit(solution)/shard_map/ppermute | solution.py:940
  60.2 23.7 %attention_forward.1 = (bf16[1024,512]{1,0:T(8,128)(2,1)}, bf16[12,1024,128]{2,1,0:T(8,128)(2,1)}, f32[8,1,1024]{2,1,0:T(1,128)}, bf16[1024,512]{1,0:T(8,128)(2,...) custom-call(s32[2]{0:T(128)} %pad_add_fusion.z_ref.pos_ref, ...), custom_call_target="tpu_custom_call" | custom-call | flops 1000000 | bytes 100000 | tf_op jit(solution)/shard_map/attention_forward/pallas_call | solution.py:443
  83.9 15.9 %all_to_all.40.refs_1_ = bf16[8,4,16,512]{3,2,1,0:T(8,128)(2,1)} all-to-all(bf16[8,4,16,512]{3,2,1,0:T(8,128)(2,1)} %get-tuple-element.55), channel_id=1, replica_groups=mesh['batch'=8,'expert'=4] {'batch'}, dimensions={0} | all-to-all | bytes 1048576 | tf_op jit(solution)/shard_map/all_to_all | solution.py:1146
  99.9 24.5 %all_to_all.41.refs_2_.refs_3_ = bf16[8,3,4,16,512]{4,3,2,1,0:T(8,128)(2,1)S(1)} all-to-all(bf16[8,3,4,16,512]{4,3,2,1,0:T(8,128)(2,1)} %after.10), channel_id=1, replica_groups=mesh['batch'=8,'expert'=4] {'batch'}, dimensions={0} | all-to-all | bytes 3145728 | tf_op jit(solution)/shard_map/all_to_all | solution.py:1146
  124.4 0.9 slice.46
  125.8 2.4 copy_bitcast_fusion
  128.2 3.6 all-to-all-start.2
  134.7 31.4 %all-gather.10.cloned.1.call-done = bf16[32,4,16,512]{3,2,1,0:T(8,128)(2,1)} async-done(((bf16[8,4,16,512]{3,2,1,0:T(8,128)(2,1)}), bf16[32,4,16,512]{3,2,1,0:T(8,128)(2,1)}) %all-gather.10.cloned.1.call-update) | async-done | bytes 2097168 | tf_op jit(solution)/shard_map/all_gather | solution.py:1152
  166.2 1.0 copy-done.3
  167.1 22.4 %mixture_forward.2 = (bf16[4,8,2,4,16,512]{5,4,3,2,1,0:T(8,128)(2,1)}, bf16[4,384,512]{2,1,0:T(8,128)(2,1)}, bf16[4,384,2048]{2,1,0:T(8,128)(2,1)}, bf16[4,384,2...) custom-call(s32[2]{0:T(128)} %pad_add_fusion.z_ref.pos_ref, ...), custom_call_target="tpu_custom_call" | custom-call | flops 1000000 | bytes 100000 | tf_op jit(solution)/shard_map/mixture_forward/pallas_call | solution.py:788
  189.5 23.4 %mixture_backward.2 = (bf16[4,8,4,16,512]{4,3,2,1,0:T(8,128)(2,1)}, bf16[4,384,512]{2,1,0:T(8,128)(2,1)}, bf16[4,384,2048]{2,1,0:T(8,128)(2,1)}, f32[16,512]{1,0:T(8,128)}) custom-call(s32[2]{0:T(128)} %pad_add_fusion.z_ref.pos_ref, bf16[4,8,4,16,512]{4,3,2,1,0:T(8,128)(2,1)} %bitcast.142, bf16[4,8,4,32,512]{4,3,2,1,0:T(8,128)(2,1)} %all-gather.6.cloned.1.call-done.refs_1_, ...), custom_call_target="tpu_custom_call" | custom-call | flops 1000000 | bytes 100000 | tf_op jit(solution)/shard_map/mixture_backward/pallas_call | solution.py:823
  213.5 22.4 %mixture_forward.3 = (bf16[4,8,2,4,16,512]{5,4,3,2,1,0:T(8,128)(2,1)}, bf16[4,384,512]{2,1,0:T(8,128)(2,1)}, bf16[4,384,2048]{2,1,0:T(8,128)(2,1)}, bf16[4,384,2...) custom-call(s32[2]{0:T(128)} %pad_add_fusion.z_ref.pos_ref, ...), custom_call_target="tpu_custom_call", output_to_operand_aliasing={{0}: (2, {})} | custom-call | flops 1000000 | bytes 100000 | tf_op jit(solution)/shard_map/mixture_forward/pallas_call | solution.py:788
  235.9 23.4 %mixture_backward.3 = (bf16[4,8,4,16,512]{4,3,2,1,0:T(8,128)(2,1)}, bf16[4,384,512]{2,1,0:T(8,128)(2,1)}, bf16[4,384,2048]{2,1,0:T(8,128)(2,1)}, f32[16,512]{1,0:T(8,128)}) custom-call(s32[2]{0:T(128)} %pad_add_fusion.z_ref.pos_ref, bf16[4,8,4,16,512]{4,3,2,1,0:T(8,128)(2,1)} %bitcast.135, bf16[4,8,4,32,512]{4,3,2,1,0:T(8,128)(2,1)} %all-gather.6.cloned.1.call-done.refs_1_, ...), custom_call_target="tpu_custom_call" | custom-call | flops 1000000 | bytes 100000 | tf_op jit(solution)/shard_map/mixture_backward/pallas_call | solution.py:823
  259.4 1.0 copy-done.14
  260.4 13.3 %all_to_all.42.refs_0_ = bf16[8,4,16,512]{3,2,1,0:T(8,128)(2,1)} all-to-all(bf16[8,4,16,512]{3,2,1,0:T(8,128)(2,1)S(1)} %bitcast.153), channel_id=1, replica_groups=mesh['batch'=8,'expert'=4] {'batch'}, dimensions={0} | all-to-all | bytes 1048576 | tf_op jit(solution)/shard_map/all_to_all | solution.py:1146
  273.7 23.4 %weight_grads.1 = (bf16[2,2,2,2,2,512,256]{6,5,4,3,2,1,0:T(8,128)(2,1)}, bf16[2,2,2,2,2,512,256]{6,5,4,3,2,1,0:T(8,128)(2,1)}) custom-call(s32[2]{0:T(128)} %pad_add_fusion.z_ref.pos_ref, bf16[4,384,512]{2,1,0:T(8,128)(2,1)} %get-tuple-element.74.m0, bf16[4,384,512]{2,1,0:T(8,128)(2,1)} %get-tuple-element.75.m1, bf16[4,384,2048]{2,1,0:T(8,128)(2,1)} %get-tuple-element.76.p0, ...), custom_call_target="tpu_custom_call" | custom-call | flops 1000000 | bytes 100000 | tf_op jit(solution)/shard_map/weight_grads/pallas_call | solution.py:875
  297.1 6.8 %reduce-scatter.6.cloned.1.call-done = bf16[1,8,4,16,512]{4,3,2,1,0:T(8,128)(2,1)} async-done(((bf16[4,8,4,16,512]{4,3,2,1,0:T(8,128)(2,1)}), bf16[1,8,4,16,512]{4,3,2,1,0:T(8,128)(2,1)}) %reduce-scatter.6.cloned.1.call-update) | async-done | bytes 524304 | tf_op jit(solution)/shard_map/reduce_scatter | solution.py:1170
  303.8 1.0 copy-done.5
  304.9 13.6 %all_to_all.43.refs_8_.refs_1_ = bf16[8,4,16,512]{3,2,1,0:T(8,128)(2,1)} all-to-all(bf16[8,4,16,512]{3,2,1,0:T(8,128)(2,1)S(1)} %bitcast.145), channel_id=1, replica_groups=mesh['batch'=8,'expert'=4] {'batch'}, dimensions={0} | all-to-all | bytes 1048576 | tf_op jit(solution)/shard_map/all_to_all | solution.py:1146
  318.5 6.7 %first_sends.1 = (bf16[2,2,512,256]{3,2,1,0:T(8,128)(2,1)}, bf16[2,2,512,256]{3,2,1,0:T(8,128)(2,1)}, bf16[2,2,512,256]{3,2,1,0:T(8,128)(2,1)}, bf16[2,2,512,256]{3,2,1,0:T(8,128)(2,1)}) custom-call(s32[2]{0:T(128)} %pad_add_fusion.z_ref.pos_ref, ...), custom_call_target="tpu_custom_call" | custom-call | flops 1000000 | bytes 100000 | tf_op jit(solution)/shard_map/first_sends/pallas_call | solution.py:977
  325.8 1.5 collective-permute-start.12
  327.8 1.5 collective-permute-start.14
  329.4 26.5 %attention_backward.1 = (bf16[1024,512]{1,0:T(8,128)(2,1)}, bf16[512,2048]{1,0:T(8,128)(2,1)}, f32[1,512]{1,0:T(1,128)}, f32[1,512]{1,0:T(1,128)}) custom-call(bf16[8,4,16,512]{3,2,1,0:T(8,128)(2,1)} %all_to_all.42.refs_0_, bf16[8,4,16,512]{3,2,1,0:T(8,128)(2,1)} %all_to_all.43.refs_8_.refs_1_, bf16[8,4,32,512]{3,2,1,0:T(8,128)(2,1)} %copy-done.3, ...), custom_call_target="tpu_custom_call" | custom-call | flops 1000000 | bytes 100000 | tf_op jit(solution)/shard_map/attention_backward/pallas_call | solution.py:557
  356.8 15.3 %collective-permute-done.12.refs_5_.refs_6_ = bf16[2,2,512,256]{3,2,1,0:T(8,128)(2,1)S(1)} collective-permute-done((bf16[2,2,512,256]{3,2,1,0:T(8,128)(2,1)}, bf16[2,2,512,256]{3,2,1,0:T(8,128)(2,1)S(1)}, u32[]{:S(2)}, u32[]{:S(2)}) %collective-permute-start.12) | collective-permute-done | bytes 1048608 | tf_op jit(solution)/shard_map/ppermute | solution.py:1061
  372.1 1.6 collective-permute-done.14.refs_11_.refs_14_
  373.7 5.0 %second_sends.1 = (bf16[2,512,256]{2,1,0:T(8,128)(2,1)}, bf16[2,512,256]{2,1,0:T(8,128)(2,1)}, bf16[2,512,256]{2,1,0:T(8,128)(2,1)}, bf16[2,512,256]{2,1,0:T(8,128)(2,1)}) custom-call(s32[2]{0:T(128)} %pad_add_fusion.z_ref.pos_ref, bf16[2,2,2,2,2,512,256]{6,5,4,3,2,1,0:T(8,128)(2,1)} %get-tuple-element.82.refs_0_.refs_2_.refs_4_.refs_6_.refs_3_.refs_9_.refs_8_.refs_12_, ...), custom_call_target="tpu_custom_call" | custom-call | flops 1000000 | bytes 100000 | tf_op jit(solution)/shard_map/second_sends/pallas_call | solution.py:1019
  378.7 1.8 fusion.1
  380.6 2.9 collective-permute-done.15
  383.5 2.6 fusion.2
  386.1 3.5 all-to-all-start.5
  390.5 2.2 collective-permute-start.17
  392.6 2.6 collective-permute-start.18
  395.3 2.0 collective-permute-start.19
  397.3 4.3 collective-permute-done.16.refs_1_
  401.6 2.0 collective-permute-start.21
  403.5 8.3 %collective-permute-done.17.refs_2_ = bf16[256,512]{1,0:T(8,128)(2,1)S(1)} collective-permute-done((bf16[256,512]{1,0:T(8,128)(2,1)S(1)}, bf16[256,512]{1,0:T(8,128)(2,1)S(1)}, u32[]{:S(2)}, u32[]{:S(2)}) %collective-permute-start.17) | collective-permute-done | bytes 262176 | tf_op jit(solution)/shard_map/ppermute | solution.py:940
  411.8 1.9 collective-permute-start.22
  414.4 4.3 add_home.1
  418.7 0.9 reduce_sum.21.refs_0_
  419.6 7.5 %all-to-all-start.7 = ((bf16[4,16,2176]{2,1,0:T(8,128)(2,1)}), bf16[4,16,2176]{2,1,0:T(8,128)(2,1)S(1)}, u32[]{:S(2)}, u32[]{:S(2)}) async-start(bf16[4,16,2176]{2,1,0:T(8,128)(2,1)} %bitcast.149), calls=%async_computation.10 | async-start | bytes 557056 | tf_op jit(solution)/shard_map/all_to_all | solution.py:1207
  428.5 6.8 %all-to-all-done.7 = bf16[4,16,2176]{2,1,0:T(8,128)(2,1)S(1)} async-done(((bf16[4,16,2176]{2,1,0:T(8,128)(2,1)}), bf16[4,16,2176]{2,1,0:T(8,128)(2,1)S(1)}, u32[]{:S(2)}, u32[]{:S(2)}) %all-to-all-start.7) | async-done | bytes 278560 | tf_op jit(solution)/shard_map/all_to_all | solution.py:1207
  435.4 3.6 all-to-all-start.6
  439.0 6.7 %expert_sums.1 = (f32[4,512,256]{2,1,0:T(8,128)}, f32[4,256,512]{2,1,0:T(8,128)}) custom-call(s32[2]{0:T(128)} %pad_add_fusion.z_ref.pos_ref, bf16[2,2,2,2,2,512,256]{6,5,4,3,2,1,0:T(8,128)(2,1)} %get-tuple-element.82.refs_0_.refs_2_.refs_4_.refs_6_.refs_3_.refs_9_.refs_8_.refs_12_, ...), custom_call_target="tpu_custom_call" | custom-call | flops 1000000 | bytes 100000 | tf_op jit(solution)/shard_map/expert_sums/pallas_call | solution.py:1049
  448.3 6.0 %all-to-all-done.6 = bf16[8,2,4,16,512]{4,3,2,1,0:T(8,128)(2,1)S(1)} async-done(((bf16[8,2,4,16,512]{4,3,2,1,0:T(8,128)(2,1)}), bf16[8,2,4,16,512]{4,3,2,1,0:T(8,128)(2,1)S(1)}, u32[]{:S(2)}, u32[]{:S(2)}) %all-to-all-start.6) | async-done | bytes 1048608 | tf_op jit(solution)/shard_map/all_to_all | solution.py:1146
  454.8 1.4 copy-done.4
  456.2 1.8 add.151
  (158 shorter events, 20.1 us)
Async XLA Ops:
  7.2 126.3 %copy-start = (bf16[512,16]{0,1:T(8,128)(2,1)S(1)}, bf16[512,16]{0,1:T(8,128)(2,1)}, u32[]{:S(2)}) copy-start(bf16[512,16]{0,1:T(8,128)(2,1)} %param.15) | copy-start | bytes 49156
  7.2 118.7 %all-gather.6.cloned.1.call-start = ((), (), s32[]{:S(2)}) async-start(), calls=%async_computation.11 | async-start | bytes 5242880 | tf_op jit(solution)/shard_map/all_gather | solution.py:1128
  7.3 6.9 %copy-start.6 = (f32[2,2,256,512]{3,2,1,0:T(8,128)S(1)}, f32[2,2,256,512]{3,2,1,0:T(8,128)}, u32[]{:S(2)}) copy-start(f32[2,2,256,512]{3,2,1,0:T(8,128)} %param.12) | copy-start | bytes 6291460
  10.2 21.2 %collective-permute-start.1 = (bf16[256,512]{1,0:T(8,128)(2,1)}, bf16[256,512]{1,0:T(8,128)(2,1)S(1)}, u32[]{:S(2)}, u32[]{:S(2)}) collective-permute-start(bf16[256,512]{1,0:T(8,128)(2,1)} %get-tuple-element.113), channel_id=1, source_target_pairs={{0,2},{1,3},{2,0},{3,1},{4,6},{5,7},{6,4},{7,5},{8,10},{9,11},{10,... | collective-permute-start | bytes 786440 | tf_op jit(solution)/shard_map/ppermute | solution.py:940
  15.1 4.5 collective-permute-start.3
  15.1 6.6 %collective-permute-start.4 = (bf16[4,32,512]{2,1,0:T(8,128)(2,1)}, bf16[4,32,512]{2,1,0:T(8,128)(2,1)}, u32[]{:S(2)}, u32[]{:S(2)}) collective-permute-start(bf16[4,32,512]{2,1,0:T(8,128)(2,1)} %get-tuple-element.106), channel_id=1, source_target_pairs={{0,8},{4,12},{8,0},{12,4},{16,24},{20,28},{24,16},{28,20},{1,9},{5... | collective-permute-start | bytes 393224 | tf_op jit(solution)/shard_map/ppermute | solution.py:1124
  16.6 8.5 %collective-permute-start.5 = (bf16[4,32,512]{2,1,0:T(8,128)(2,1)}, bf16[4,32,512]{2,1,0:T(8,128)(2,1)}, u32[]{:S(2)}, u32[]{:S(2)}) collective-permute-start(bf16[4,32,512]{2,1,0:T(8,128)(2,1)} %get-tuple-element.105), channel_id=1, source_target_pairs={{0,12},{4,8},{8,4},{12,0},{16,28},{20,24},{24,20},{28,16},{1,13},{... | collective-permute-start | bytes 393224 | tf_op jit(solution)/shard_map/ppermute | solution.py:1124
  17.0 10.2 %collective-permute-start.6 = (bf16[4,32,512]{2,1,0:T(8,128)(2,1)}, bf16[4,32,512]{2,1,0:T(8,128)(2,1)}, u32[]{:S(2)}, u32[]{:S(2)}) collective-permute-start(bf16[4,32,512]{2,1,0:T(8,128)(2,1)} %get-tuple-element.104), channel_id=1, source_target_pairs={{0,16},{4,20},{8,24},{12,28},{16,0},{20,4},{24,8},{28,12},{1,17},{... | collective-permute-start | bytes 393224 | tf_op jit(solution)/shard_map/ppermute | solution.py:1124
  19.7 10.8 %collective-permute-start.7 = (bf16[4,32,512]{2,1,0:T(8,128)(2,1)}, bf16[4,32,512]{2,1,0:T(8,128)(2,1)S(1)}, u32[]{:S(2)}, u32[]{:S(2)}) collective-permute-start(bf16[4,32,512]{2,1,0:T(8,128)(2,1)} %get-tuple-element.103), channel_id=1, source_target_pairs={{0,20},{4,16},{8,28},{12,24},{16,4},{20,0},{24,12},{28,8},{1,21},{... | collective-permute-start | bytes 393224 | tf_op jit(solution)/shard_map/ppermute | solution.py:1124
  21.7 12.7 %copy-start.29 = (pred[8]{0:T(512)(128)(4,1)S(1)}, pred[8]{0:T(512)(128)(4,1)}, u32[]{:S(2)}) copy-start(pred[8]{0:T(512)(128)(4,1)} %compare_and_fusion) | copy-start | bytes 28
  21.7 8.8 %collective-permute-start.8 = (bf16[4,32,512]{2,1,0:T(8,128)(2,1)}, bf16[4,32,512]{2,1,0:T(8,128)(2,1)S(1)}, u32[]{:S(2)}, u32[]{:S(2)}) collective-permute-start(bf16[4,32,512]{2,1,0:T(8,128)(2,1)} %get-tuple-element.102), channel_id=1, source_target_pairs={{0,24},{4,28},{8,16},{12,20},{16,8},{20,12},{24,0},{28,4},{1,25},{... | collective-permute-start | bytes 393224 | tf_op jit(solution)/shard_map/ppermute | solution.py:1124
  25.1 6.3 %collective-permute-start.9 = (bf16[4,32,512]{2,1,0:T(8,128)(2,1)S(1)}, bf16[4,32,512]{2,1,0:T(8,128)(2,1)S(1)}, u32[]{:S(2)}, u32[]{:S(2)}) collective-permute-start(bf16[4,32,512]{2,1,0:T(8,128)(2,1)S(1)} %get-tuple-element.101), channel_id=1, source_target_pairs={{0,28},{4,24},{8,20},{12,16},{16,12},{20,8},{24,4},{28,0},{1,29},{... | collective-permute-start | bytes 393224 | tf_op jit(solution)/shard_map/ppermute | solution.py:1124
  31.4 0.7 copy-start.17
  32.0 0.7 copy-start.16
  34.4 1.2 copy-start.20
  34.4 2.9 copy-start.19
  35.6 130.6 %all-gather.10.cloned.1.call-start = ((), (), s32[]{:S(2)}) async-start(), calls=%async_computation.16 | async-start | bytes 2621440 | tf_op jit(solution)/shard_map/all_gather | solution.py:1152
  35.7 11.1 %collective-permute-start = (bf16[256,512]{1,0:T(8,128)(2,1)S(1)}, bf16[256,512]{1,0:T(8,128)(2,1)S(1)}, u32[]{:S(2)}, u32[]{:S(2)}) collective-permute-start(bf16[256,512]{1,0:T(8,128)(2,1)S(1)} %copy-done.20), channel_id=1, source_target_pairs={{0,1},{1,2},{2,3},{3,0},{4,5},{5,6},{6,7},{7,4},{8,9},{9,10},{10,1... | collective-permute-start | bytes 786440 | tf_op jit(solution)/shard_map/ppermute | solution.py:940
  37.3 22.2 %collective-permute-start.2 = (bf16[256,512]{1,0:T(8,128)(2,1)S(1)}, bf16[256,512]{1,0:T(8,128)(2,1)S(1)}, u32[]{:S(2)}, u32[]{:S(2)}) collective-permute-start(bf16[256,512]{1,0:T(8,128)(2,1)S(1)} %copy-done.19), channel_id=1, source_target_pairs={{0,3},{1,0},{2,1},{3,2},{4,7},{5,4},{6,5},{7,6},{8,11},{9,8},{10,9... | collective-permute-start | bytes 786440 | tf_op jit(solution)/shard_map/ppermute | solution.py:940
  46.7 12.8 %copy-start.21 = (bf16[256,512]{1,0:T(8,128)(2,1)}, bf16[256,512]{1,0:T(8,128)(2,1)S(1)}, u32[]{:S(2)}) copy-start(bf16[256,512]{1,0:T(8,128)(2,1)S(1)} %collective-permute-done.refs_1_) | copy-start | bytes 786436
  59.5 0.7 copy-start.22
  99.8 113.1 %all-gather.8.cloned.1.call-start = ((), (), s32[]{:S(2)}) async-start(), calls=%async_computation.15 | async-start | bytes 2621440 | tf_op jit(solution)/shard_map/all_gather | solution.py:1154
  99.9 25.5 %copy-start.28 = (s32[2,3]{1,0:T(2,128)S(1)}, s32[2,3]{1,0:T(2,128)}, u32[]{:S(2)}) copy-start(s32[2,3]{1,0:T(2,128)} %param.20) | copy-start | bytes 76
  124.4 3.8 copy-start.2
  125.8 6.6 %copy-start.30 = (s32[2,16]{1,0:T(2,128)S(1)}, s32[2,16]{1,0:T(2,128)}, u32[]{:S(2)}) copy-start(s32[2,16]{1,0:T(2,128)} %param.21) | copy-start | bytes 388
  128.2 37.9 %all-to-all-start.2 = ((bf16[8,4,32,512]{3,2,1,0:T(8,128)(2,1)}), bf16[8,4,32,512]{3,2,1,0:T(8,128)(2,1)S(1)}, u32[]{:S(2)}, u32[]{:S(2)}) async-start(bf16[8,4,32,512]{3,2,1,0:T(8,128)(2,1)} %copy_bitcast_fusion), calls=%async_computation.2 | async-start | bytes 2097152 | tf_op jit(solution)/shard_map/all_to_all | solution.py:1146
  131.8 127.5 %reduce-scatter.4.cloned.1.call-start = ((), (), s32[]{:S(2)}) async-start(), calls=%async_computation.12 | async-start | bytes 2621440 | tf_op jit(solution)/shard_map/reduce_scatter | solution.py:1164
  132.3 33.8 %copy-start.18 = (f32[2,3,256]{2,1,0:T(4,128)}, f32[2,3,256]{2,1,0:T(4,128)S(1)}, u32[]{:S(2)}) copy-start(f32[2,3,256]{2,1,0:T(4,128)S(1)} %copy.86.refs_4_.refs_3_.refs_5_) | copy-start | bytes 18436
  166.2 1.0 copy-start.3
  213.0 90.8 %reduce-scatter.6.cloned.1.call-start = ((), (), s32[]{:S(2)}) async-start(), calls=%async_computation.13 | async-start | bytes 2621440 | tf_op jit(solution)/shard_map/reduce_scatter | solution.py:1170
  259.4 1.0 copy-start.14
  259.4 167.8 %reduce-scatter.8.cloned.1.call-start = ((), (), s32[]{:S(2)}) async-start(), calls=%async_computation.14 | async-start | bytes 5242880 | tf_op jit(solution)/shard_map/reduce_scatter | solution.py:1174
  303.8 14.6 %collective-permute-start.10 = (bf16[2,2,2,2,2,512,256]{6,5,4,3,2,1,0:T(8,128)(2,1)}, bf16[2,2,2,2,2,512,256]{6,5,4,3,2,1,0:T(8,128)(2,1)}, u32[]{:S(2)}, u32[]{:S(2)}) collective-permute-start(bf16[2,2,2,2,2,512,256]{6,5,4,3,2,1,0:T(8,128)(2,1)} %after.14), channel_id=1, source_target_pairs={{0,4},{4,0},{8,12},{12,8},{16,20},{20,16},{24,28},{28,24},{1,5},{5... | collective-permute-start | bytes 25165832 | tf_op jit(solution)/shard_map/ppermute | solution.py:1177
  303.8 1.0 copy-start.5
  318.5 10.8 %copy-start.26 = (f32[16,512]{1,0:T(8,128)S(1)}, f32[16,512]{1,0:T(8,128)}, u32[]{:S(2)}) copy-start(f32[16,512]{1,0:T(8,128)} %get-tuple-element.61.refs_2_) | copy-start | bytes 98308
  318.5 10.8 %copy-start.27 = (f32[16,512]{1,0:T(8,128)S(1)}, f32[16,512]{1,0:T(8,128)}, u32[]{:S(2)}) copy-start(f32[16,512]{1,0:T(8,128)} %get-tuple-element.90) | copy-start | bytes 98308
  325.2 31.6 %collective-permute-start.11 = (bf16[2,2,512,256]{3,2,1,0:T(8,128)(2,1)}, bf16[2,2,512,256]{3,2,1,0:T(8,128)(2,1)S(1)}, u32[]{:S(2)}, u32[]{:S(2)}) collective-permute-start(bf16[2,2,512,256]{3,2,1,0:T(8,128)(2,1)} %get-tuple-element.84.refs_12_), channel_id=1, source_target_pairs={{0,8},{4,12},{8,0},{12,4},{16,24},{20,28},{24,16},{28,20},{1,9},{5... | collective-permute-start | bytes 3145736 | tf_op jit(solution)/shard_map/ppermute | solution.py:1061
  325.8 46.3 %collective-permute-start.12 = (bf16[2,2,512,256]{3,2,1,0:T(8,128)(2,1)}, bf16[2,2,512,256]{3,2,1,0:T(8,128)(2,1)S(1)}, u32[]{:S(2)}, u32[]{:S(2)}) collective-permute-start(bf16[2,2,512,256]{3,2,1,0:T(8,128)(2,1)} %get-tuple-element.85.refs_13_), channel_id=1, source_target_pairs={{0,8},{4,12},{8,0},{12,4},{16,24},{20,28},{24,16},{28,20},{1,9},{5... | collective-permute-start | bytes 3145736 | tf_op jit(solution)/shard_map/ppermute | solution.py:1061
  327.3 44.8 %collective-permute-start.13 = (bf16[2,2,512,256]{3,2,1,0:T(8,128)(2,1)}, bf16[2,2,512,256]{3,2,1,0:T(8,128)(2,1)S(1)}, u32[]{:S(2)}, u32[]{:S(2)}) collective-permute-start(bf16[2,2,512,256]{3,2,1,0:T(8,128)(2,1)} %get-tuple-element.86.refs_14_), channel_id=1, source_target_pairs={{0,16},{4,20},{8,24},{12,28},{16,0},{20,4},{24,8},{28,12},{1,17},{... | collective-permute-start | bytes 3145736 | tf_op jit(solution)/shard_map/ppermute | solution.py:1061
  327.8 45.9 %collective-permute-start.14 = (bf16[2,2,512,256]{3,2,1,0:T(8,128)(2,1)}, bf16[2,2,512,256]{3,2,1,0:T(8,128)(2,1)}, u32[]{:S(2)}, u32[]{:S(2)}) collective-permute-start(bf16[2,2,512,256]{3,2,1,0:T(8,128)(2,1)} %get-tuple-element.87.refs_15_), channel_id=1, source_target_pairs={{0,16},{4,20},{8,24},{12,28},{16,0},{20,4},{24,8},{28,12},{1,17},{... | collective-permute-start | bytes 3145736 | tf_op jit(solution)/shard_map/ppermute | solution.py:1061
  356.8 16.9 %copy-start.7 = (bf16[2,2,512,256]{3,2,1,0:T(8,128)(2,1)}, bf16[2,2,512,256]{3,2,1,0:T(8,128)(2,1)S(1)}, u32[]{:S(2)}) copy-start(bf16[2,2,512,256]{3,2,1,0:T(8,128)(2,1)S(1)} %collective-permute-done.11.refs_2_) | copy-start | bytes 3145732
  372.1 1.6 copy-start.8
  372.1 1.6 copy-start.9
  380.5 3.0 collective-permute-start.15
  383.5 6.2 %copy-start.15 = (bf16[1024,512]{1,0:T(8,128)(2,1)S(1)}, bf16[1024,512]{1,0:T(8,128)(2,1)}, u32[]{:S(2)}) copy-start(bf16[1024,512]{1,0:T(8,128)(2,1)} %get-tuple-element.93) | copy-start | bytes 3145732
  386.1 32.6 %all-to-all-start.5 = ((bf16[4,64,2176]{2,1,0:T(8,128)(2,1)}), bf16[4,64,2176]{2,1,0:T(8,128)(2,1)S(1)}, u32[]{:S(2)}, u32[]{:S(2)}) async-start(bf16[4,64,2176]{2,1,0:T(8,128)(2,1)} %fusion.2), calls=%async_computation.8 | async-start | bytes 2228224 | tf_op jit(solution)/shard_map/all_to_all | solution.py:1201
  390.4 11.1 %collective-permute-start.16 = (bf16[256,512]{1,0:T(8,128)(2,1)S(1)}, bf16[256,512]{1,0:T(8,128)(2,1)S(1)}, u32[]{:S(2)}, u32[]{:S(2)}) collective-permute-start(bf16[256,512]{1,0:T(8,128)(2,1)S(1)} %get-tuple-element.110), channel_id=1, source_target_pairs={{0,1},{1,2},{2,3},{3,0},{4,5},{5,6},{6,7},{7,4},{8,9},{9,10},{10,1... | collective-permute-start | bytes 786440 | tf_op jit(solution)/shard_map/ppermute | solution.py:940
  390.5 21.3 %collective-permute-start.17 = (bf16[256,512]{1,0:T(8,128)(2,1)S(1)}, bf16[256,512]{1,0:T(8,128)(2,1)S(1)}, u32[]{:S(2)}, u32[]{:S(2)}) collective-permute-start(bf16[256,512]{1,0:T(8,128)(2,1)S(1)} %get-tuple-element.109), channel_id=1, source_target_pairs={{0,2},{1,3},{2,0},{3,1},{4,6},{5,7},{6,4},{7,5},{8,10},{9,11},{10,... | collective-permute-start | bytes 786440 | tf_op jit(solution)/shard_map/ppermute | solution.py:940
  392.6 21.0 %collective-permute-start.18 = (bf16[256,512]{1,0:T(8,128)(2,1)S(1)}, bf16[256,512]{1,0:T(8,128)(2,1)S(1)}, u32[]{:S(2)}, u32[]{:S(2)}) collective-permute-start(bf16[256,512]{1,0:T(8,128)(2,1)S(1)} %get-tuple-element.108), channel_id=1, source_target_pairs={{0,3},{1,0},{2,1},{3,2},{4,7},{5,4},{6,5},{7,6},{8,11},{9,8},{10,9... | collective-permute-start | bytes 786440 | tf_op jit(solution)/shard_map/ppermute | solution.py:940
  395.3 31.9 %collective-permute-start.19 = (bf16[2,512,256]{2,1,0:T(8,128)(2,1)}, bf16[2,512,256]{2,1,0:T(8,128)(2,1)S(1)}, u32[]{:S(2)}, u32[]{:S(2)}) collective-permute-start(bf16[2,512,256]{2,1,0:T(8,128)(2,1)} %get-tuple-element.89.refs_1_), channel_id=1, source_target_pairs={{0,16},{4,20},{8,24},{12,28},{16,0},{20,4},{24,8},{28,12},{1,17},{... | collective-permute-start | bytes 1572872 | tf_op jit(solution)/shard_map/ppermute | solution.py:1061
  397.3 29.9 %collective-permute-start.20 = (bf16[2,512,256]{2,1,0:T(8,128)(2,1)}, bf16[2,512,256]{2,1,0:T(8,128)(2,1)S(1)}, u32[]{:S(2)}, u32[]{:S(2)}) collective-permute-start(bf16[2,512,256]{2,1,0:T(8,128)(2,1)} %get-tuple-element.94), channel_id=1, source_target_pairs={{0,16},{4,20},{8,24},{12,28},{16,0},{20,4},{24,8},{28,12},{1,17},{... | collective-permute-start | bytes 1572872 | tf_op jit(solution)/shard_map/ppermute | solution.py:1061
  401.5 12.1 %copy-start.23 = (bf16[256,512]{1,0:T(8,128)(2,1)}, bf16[256,512]{1,0:T(8,128)(2,1)S(1)}, u32[]{:S(2)}) copy-start(bf16[256,512]{1,0:T(8,128)(2,1)S(1)} %collective-permute-done.16.refs_1_) | copy-start | bytes 786436
  401.6 25.6 %collective-permute-start.21 = (bf16[2,512,256]{2,1,0:T(8,128)(2,1)}, bf16[2,512,256]{2,1,0:T(8,128)(2,1)S(1)}, u32[]{:S(2)}, u32[]{:S(2)}) collective-permute-start(bf16[2,512,256]{2,1,0:T(8,128)(2,1)} %get-tuple-element.95), channel_id=1, source_target_pairs={{0,8},{4,12},{8,0},{12,4},{16,24},{20,28},{24,16},{28,20},{1,9},{5... | collective-permute-start | bytes 1572872 | tf_op jit(solution)/shard_map/ppermute | solution.py:1061
  411.8 1.9 copy-start.24
  411.8 15.4 %collective-permute-start.22 = (bf16[2,512,256]{2,1,0:T(8,128)(2,1)}, bf16[2,512,256]{2,1,0:T(8,128)(2,1)S(1)}, u32[]{:S(2)}, u32[]{:S(2)}) collective-permute-start(bf16[2,512,256]{2,1,0:T(8,128)(2,1)} %get-tuple-element.96), channel_id=1, source_target_pairs={{0,8},{4,12},{8,0},{12,4},{16,24},{20,28},{24,16},{28,20},{1,9},{5... | collective-permute-start | bytes 1572872 | tf_op jit(solution)/shard_map/ppermute | solution.py:1061
  413.7 0.7 copy-start.25
  419.6 15.8 %all-to-all-start.7 = ((bf16[4,16,2176]{2,1,0:T(8,128)(2,1)}), bf16[4,16,2176]{2,1,0:T(8,128)(2,1)S(1)}, u32[]{:S(2)}, u32[]{:S(2)}) async-start(bf16[4,16,2176]{2,1,0:T(8,128)(2,1)} %bitcast.149), calls=%async_computation.10 | async-start | bytes 557056 | tf_op jit(solution)/shard_map/all_to_all | solution.py:1207
  427.2 0.8 copy-start.10
  427.2 1.0 copy-start.11
  427.2 1.2 copy-start.12
  427.2 1.3 copy-start.13
  435.4 18.9 %all-to-all-start.6 = ((bf16[8,2,4,16,512]{4,3,2,1,0:T(8,128)(2,1)}), bf16[8,2,4,16,512]{4,3,2,1,0:T(8,128)(2,1)S(1)}, u32[]{:S(2)}, u32[]{:S(2)}) async-start(bf16[8,2,4,16,512]{4,3,2,1,0:T(8,128)(2,1)} %after.17), calls=%async_computation.9 | async-start | bytes 2097152 | tf_op jit(solution)/shard_map/all_to_all | solution.py:1146
  454.6 1.6 copy-start.4
  454.8 3.2 copy-start.1
Sparse Core Ops, SparseCore 0:
  35.7 82.7 all-gather.5
  120.1 46.0 all-gather.9
  167.7 44.6 all-gather.7
  215.2 42.5 reduce-scatter.3
  260.6 43.1 reduce-scatter.5
  306.0 76.0 reduce-scatter.7

commit v5 on v4

--- a/solution.py
+++ b/solution.py
@@ -1200,7 +1200,7 @@
     chips = [[c + 2 * i for i in range(nb // 2)] for c in range(2)]
     flat = lax.all_to_all(flat, "batch", split_axis=0, concat_axis=0, tiled=True, axis_index_groups=chips)
     flat = jnp.sum(flat.astype(F32), 0).astype(BF16)
-    flat = after(flat, grad_in)
+    flat = after(flat, *parts[1:])
     spread = over_batch(after(spread, flat, *got_last))
     out = tokens + spread.transpose(2, 0, 1, 3, 4).reshape(tokens.shape).astype(F32)
     flat = flat.reshape(planes, -1, flat.shape[1])

time: 473 us -> 468 us (0.989)
    unnamed x69 -> x67, local copies, waits for them, and re-layouts: 12.2 us -> 12 us
  transfers between devices with their start and end apart: 33 -> 33, of which waited for: 14 -> 15; matrix products, arithmetic and copies ran while one was open for 5% -> 5% of each run, Pallas kernels for 40% -> 41%
where the time goes in v5:
time: 468 us; the launch traced here: 461 us
  Pallas kernels  188 us (40%)
  waiting for transfers between devices  102 us (22%)
  blocking collectives  67.3 us (14%)
  starting transfers between devices  48.9 us (10%)
  local copies, waits for them, and re-layouts  24.8 us (5%)
  other arithmetic  15.1 us (3%)
  between operations  14.9 us (3%)
    all_to_all x4, blocking collectives, over_batch(): lax.all_to_all(block, 'batch', split_axis=0, concat_axis=0, tiled=True)  67.3 us
    pallas_call x2, Pallas kernels, mixture_backward(): pl.pallas_call(functools.partial(mixture_backward_kernel, chunk, parts, l...  46.8 us
    pallas_call x2, Pallas kernels, mixture_forward(): pl.pallas_call(functools.partial(mixture_forward_kernel, chunk, len(x_par...  44.8 us
    all_gather x1, waiting for transfers between devices, body(): x0 = [lax.all_gather(own0, 'expert', axis=0, tiled=False)]  31.4 us
    ppermute x6, waiting for transfers between devices, to_planes(): lax.ppermute(picked[k], 'expert', [(i, (i + k) % count) for i in range(co...  30.8 us
    pallas_call x1, Pallas kernels, attention_backward(): pl.pallas_call(functools.partial(attention_backward_kernel, len(waits)),...  26.5 us
    pallas_call x1, Pallas kernels, attention_forward(): pl.pallas_call(functools.partial(attention_forward_kernel, len(waits)), i...  23.7 us
    pallas_call x1, Pallas kernels, weight_grads(): pl.pallas_call(weight_grads_kernel, grid=(experts,), in_specs=[pl.BlockSp...  23.4 us
  transfers between devices with their start and end apart: 33, of which 15 were waited for; matrix products, arithmetic and copies ran while one was open for 5% of the time, Pallas kernels for 41%

profile of v5, /device:TPU:0, one launch (start us, length us, event | category | flops | bytes accessed | tf_op | source)
XLA Modules:
  0.0 460.7 jit_solution(11065227233946217427)
XLA Ops:
  7.3 1.9 convert_element_type.117
  9.2 1.0 dynamic-slice_bitcast_fusion.5
  10.2 4.0 collective-permute-start.1
  15.1 1.5 collective-permute-start.4
  17.0 1.5 collective-permute-start.6
  20.7 1.0 collective-permute-done.4
  21.7 2.4 collective-permute-start.8
  24.2 0.9 bitcast_dynamic-update-slice_fusion.5
  25.1 1.1 collective-permute-start.9
  26.2 0.9 bitcast_dynamic-update-slice_fusion.4
  27.2 0.9 bitcast_dynamic-update-slice_fusion.3
  28.1 2.4 collective-permute-done.7
  34.4 1.1 bitcast_select_fusion
  35.7 1.6 collective-permute-start
  37.3 2.2 collective-permute-start.2
  40.2 1.1 broadcast_select_fusion.refs_4_
  41.3 5.4 %collective-permute-done.refs_1_ = bf16[256,512]{1,0:T(8,128)(2,1)S(1)} collective-permute-done((bf16[256,512]{1,0:T(8,128)(2,1)S(1)}, bf16[256,512]{1,0:T(8,128)(2,1)S(1)}, u32[]{:S(2)}, u32[]{:S(2)}) %collective-permute-start) | collective-permute-done | bytes 262176 | tf_op jit(solution)/shard_map/ppermute | solution.py:940
  46.7 12.8 %collective-permute-done.2.refs_3_ = bf16[256,512]{1,0:T(8,128)(2,1)S(1)} collective-permute-done((bf16[256,512]{1,0:T(8,128)(2,1)S(1)}, bf16[256,512]{1,0:T(8,128)(2,1)S(1)}, u32[]{:S(2)}, u32[]{:S(2)}) %collective-permute-start.2) | collective-permute-done | bytes 262176 | tf_op jit(solution)/shard_map/ppermute | solution.py:940
  60.2 23.7 %attention_forward.1 = (bf16[1024,512]{1,0:T(8,128)(2,1)}, bf16[12,1024,128]{2,1,0:T(8,128)(2,1)}, f32[8,1,1024]{2,1,0:T(1,128)}, bf16[1024,512]{1,0:T(8,128)(2,...) custom-call(s32[2]{0:T(128)} %pad_add_fusion.z_ref.pos_ref, ...), custom_call_target="tpu_custom_call" | custom-call | flops 1000000 | bytes 100000 | tf_op jit(solution)/shard_map/attention_forward/pallas_call | solution.py:443
  83.9 15.9 %all_to_all.40.refs_1_ = bf16[8,4,16,512]{3,2,1,0:T(8,128)(2,1)} all-to-all(bf16[8,4,16,512]{3,2,1,0:T(8,128)(2,1)} %get-tuple-element.55), channel_id=1, replica_groups=mesh['batch'=8,'expert'=4] {'batch'}, dimensions={0} | all-to-all | bytes 1048576 | tf_op jit(solution)/shard_map/all_to_all | solution.py:1146
  99.9 24.5 %all_to_all.41.refs_2_.refs_3_ = bf16[8,3,4,16,512]{4,3,2,1,0:T(8,128)(2,1)S(1)} all-to-all(bf16[8,3,4,16,512]{4,3,2,1,0:T(8,128)(2,1)} %after.10), channel_id=1, replica_groups=mesh['batch'=8,'expert'=4] {'batch'}, dimensions={0} | all-to-all | bytes 3145728 | tf_op jit(solution)/shard_map/all_to_all | solution.py:1146
  124.4 0.9 slice.46
  125.8 2.4 copy_bitcast_fusion
  128.2 3.6 all-to-all-start.2
  134.7 31.4 %all-gather.10.cloned.1.call-done = bf16[32,4,16,512]{3,2,1,0:T(8,128)(2,1)} async-done(((bf16[8,4,16,512]{3,2,1,0:T(8,128)(2,1)}), bf16[32,4,16,512]{3,2,1,0:T(8,128)(2,1)}) %all-gather.10.cloned.1.call-update) | async-done | bytes 2097168 | tf_op jit(solution)/shard_map/all_gather | solution.py:1152
  166.1 1.0 copy-done.3
  167.1 22.4 %mixture_forward.2 = (bf16[4,8,2,4,16,512]{5,4,3,2,1,0:T(8,128)(2,1)}, bf16[4,384,512]{2,1,0:T(8,128)(2,1)}, bf16[4,384,2048]{2,1,0:T(8,128)(2,1)}, bf16[4,384,2...) custom-call(s32[2]{0:T(128)} %pad_add_fusion.z_ref.pos_ref, ...), custom_call_target="tpu_custom_call" | custom-call | flops 1000000 | bytes 100000 | tf_op jit(solution)/shard_map/mixture_forward/pallas_call | solution.py:788
  189.4 23.4 %mixture_backward.2 = (bf16[4,8,4,16,512]{4,3,2,1,0:T(8,128)(2,1)}, bf16[4,384,512]{2,1,0:T(8,128)(2,1)}, bf16[4,384,2048]{2,1,0:T(8,128)(2,1)}, f32[16,512]{1,0:T(8,128)}) custom-call(s32[2]{0:T(128)} %pad_add_fusion.z_ref.pos_ref, bf16[4,8,4,16,512]{4,3,2,1,0:T(8,128)(2,1)} %bitcast.140, bf16[4,8,4,32,512]{4,3,2,1,0:T(8,128)(2,1)} %all-gather.6.cloned.1.call-done.refs_1_, ...), custom_call_target="tpu_custom_call" | custom-call | flops 1000000 | bytes 100000 | tf_op jit(solution)/shard_map/mixture_backward/pallas_call | solution.py:823
  213.4 22.4 %mixture_forward.3 = (bf16[4,8,2,4,16,512]{5,4,3,2,1,0:T(8,128)(2,1)}, bf16[4,384,512]{2,1,0:T(8,128)(2,1)}, bf16[4,384,2048]{2,1,0:T(8,128)(2,1)}, bf16[4,384,2...) custom-call(s32[2]{0:T(128)} %pad_add_fusion.z_ref.pos_ref, ...), custom_call_target="tpu_custom_call", output_to_operand_aliasing={{0}: (2, {})} | custom-call | flops 1000000 | bytes 100000 | tf_op jit(solution)/shard_map/mixture_forward/pallas_call | solution.py:788
  235.8 23.4 %mixture_backward.3 = (bf16[4,8,4,16,512]{4,3,2,1,0:T(8,128)(2,1)}, bf16[4,384,512]{2,1,0:T(8,128)(2,1)}, bf16[4,384,2048]{2,1,0:T(8,128)(2,1)}, f32[16,512]{1,0:T(8,128)}) custom-call(s32[2]{0:T(128)} %pad_add_fusion.z_ref.pos_ref, bf16[4,8,4,16,512]{4,3,2,1,0:T(8,128)(2,1)} %bitcast.135, bf16[4,8,4,32,512]{4,3,2,1,0:T(8,128)(2,1)} %all-gather.6.cloned.1.call-done.refs_1_, ...), custom_call_target="tpu_custom_call" | custom-call | flops 1000000 | bytes 100000 | tf_op jit(solution)/shard_map/mixture_backward/pallas_call | solution.py:823
  259.4 1.0 copy-done.14
  260.3 13.3 %all_to_all.42.refs_0_ = bf16[8,4,16,512]{3,2,1,0:T(8,128)(2,1)} all-to-all(bf16[8,4,16,512]{3,2,1,0:T(8,128)(2,1)S(1)} %bitcast.151), channel_id=1, replica_groups=mesh['batch'=8,'expert'=4] {'batch'}, dimensions={0} | all-to-all | bytes 1048576 | tf_op jit(solution)/shard_map/all_to_all | solution.py:1146
  273.7 23.4 %weight_grads.1 = (bf16[2,2,2,2,2,512,256]{6,5,4,3,2,1,0:T(8,128)(2,1)}, bf16[2,2,2,2,2,512,256]{6,5,4,3,2,1,0:T(8,128)(2,1)}) custom-call(s32[2]{0:T(128)} %pad_add_fusion.z_ref.pos_ref, bf16[4,384,512]{2,1,0:T(8,128)(2,1)} %get-tuple-element.74.m0, bf16[4,384,512]{2,1,0:T(8,128)(2,1)} %get-tuple-element.75.m1, bf16[4,384,2048]{2,1,0:T(8,128)(2,1)} %get-tuple-element.76.p0, ...), custom_call_target="tpu_custom_call" | custom-call | flops 1000000 | bytes 100000 | tf_op jit(solution)/shard_map/weight_grads/pallas_call | solution.py:875
  297.0 6.8 %reduce-scatter.6.cloned.1.call-done = bf16[1,8,4,16,512]{4,3,2,1,0:T(8,128)(2,1)} async-done(((bf16[4,8,4,16,512]{4,3,2,1,0:T(8,128)(2,1)}), bf16[1,8,4,16,512]{4,3,2,1,0:T(8,128)(2,1)}) %reduce-scatter.6.cloned.1.call-update) | async-done | bytes 524304 | tf_op jit(solution)/shard_map/reduce_scatter | solution.py:1170
  303.8 1.0 copy-done.5
  304.8 13.6 %all_to_all.43.refs_8_.refs_1_ = bf16[8,4,16,512]{3,2,1,0:T(8,128)(2,1)} all-to-all(bf16[8,4,16,512]{3,2,1,0:T(8,128)(2,1)S(1)} %bitcast.143), channel_id=1, replica_groups=mesh['batch'=8,'expert'=4] {'batch'}, dimensions={0} | all-to-all | bytes 1048576 | tf_op jit(solution)/shard_map/all_to_all | solution.py:1146
  318.4 6.7 %first_sends.1 = (bf16[2,2,512,256]{3,2,1,0:T(8,128)(2,1)}, bf16[2,2,512,256]{3,2,1,0:T(8,128)(2,1)}, bf16[2,2,512,256]{3,2,1,0:T(8,128)(2,1)}, bf16[2,2,512,256]{3,2,1,0:T(8,128)(2,1)}) custom-call(s32[2]{0:T(128)} %pad_add_fusion.z_ref.pos_ref, ...), custom_call_target="tpu_custom_call" | custom-call | flops 1000000 | bytes 100000 | tf_op jit(solution)/shard_map/first_sends/pallas_call | solution.py:977
  325.7 1.5 collective-permute-start.12
  327.8 1.5 collective-permute-start.14
  329.3 26.5 %attention_backward.1 = (bf16[1024,512]{1,0:T(8,128)(2,1)}, bf16[512,2048]{1,0:T(8,128)(2,1)}, f32[1,512]{1,0:T(1,128)}, f32[1,512]{1,0:T(1,128)}) custom-call(bf16[8,4,16,512]{3,2,1,0:T(8,128)(2,1)} %all_to_all.42.refs_0_, bf16[8,4,16,512]{3,2,1,0:T(8,128)(2,1)} %all_to_all.43.refs_8_.refs_1_, bf16[8,4,32,512]{3,2,1,0:T(8,128)(2,1)} %copy-done.3, ...), custom_call_target="tpu_custom_call" | custom-call | flops 1000000 | bytes 100000 | tf_op jit(solution)/shard_map/attention_backward/pallas_call | solution.py:557
  356.8 15.3 %collective-permute-done.12.refs_5_.refs_6_ = bf16[2,2,512,256]{3,2,1,0:T(8,128)(2,1)S(1)} collective-permute-done((bf16[2,2,512,256]{3,2,1,0:T(8,128)(2,1)}, bf16[2,2,512,256]{3,2,1,0:T(8,128)(2,1)S(1)}, u32[]{:S(2)}, u32[]{:S(2)}) %collective-permute-start.12) | collective-permute-done | bytes 1048608 | tf_op jit(solution)/shard_map/ppermute | solution.py:1061
  372.1 1.6 collective-permute-done.14.refs_11_.refs_14_
  373.6 4.9 %second_sends.1 = (bf16[2,512,256]{2,1,0:T(8,128)(2,1)}, bf16[2,512,256]{2,1,0:T(8,128)(2,1)}, bf16[2,512,256]{2,1,0:T(8,128)(2,1)}, bf16[2,512,256]{2,1,0:T(8,128)(2,1)}) custom-call(s32[2]{0:T(128)} %pad_add_fusion.z_ref.pos_ref, bf16[2,2,2,2,2,512,256]{6,5,4,3,2,1,0:T(8,128)(2,1)} %get-tuple-element.82.refs_0_.refs_2_.refs_4_.refs_6_.refs_3_.refs_9_.refs_8_.refs_12_, ...), custom_call_target="tpu_custom_call" | custom-call | flops 1000000 | bytes 100000 | tf_op jit(solution)/shard_map/second_sends/pallas_call | solution.py:1019
  378.6 1.8 fusion.1
  380.6 2.9 collective-permute-done.15
  383.4 2.6 fusion.2
  386.0 3.5 all-to-all-start.5
  390.5 2.2 collective-permute-start.17
  392.6 2.6 collective-permute-start.18
  395.2 2.0 collective-permute-start.19
  397.3 4.3 collective-permute-done.16.refs_1_
  401.6 2.0 collective-permute-start.21
  403.5 8.3 %collective-permute-done.17.refs_2_ = bf16[256,512]{1,0:T(8,128)(2,1)S(1)} collective-permute-done((bf16[256,512]{1,0:T(8,128)(2,1)S(1)}, bf16[256,512]{1,0:T(8,128)(2,1)S(1)}, u32[]{:S(2)}, u32[]{:S(2)}) %collective-permute-start.17) | collective-permute-done | bytes 262176 | tf_op jit(solution)/shard_map/ppermute | solution.py:940
  412.5 1.9 collective-permute-start.22
  414.4 0.9 reduce_sum.21.refs_0_
  415.3 7.5 %all-to-all-start.7 = ((bf16[4,16,2176]{2,1,0:T(8,128)(2,1)}), bf16[4,16,2176]{2,1,0:T(8,128)(2,1)S(1)}, u32[]{:S(2)}, u32[]{:S(2)}) async-start(bf16[4,16,2176]{2,1,0:T(8,128)(2,1)} %bitcast.147), calls=%async_computation.10 | async-start | bytes 557056 | tf_op jit(solution)/shard_map/all_to_all | solution.py:1207
  422.8 4.1 collective-permute-done.20.refs_3_.refs_7_
  428.0 3.0 all-to-all-done.7
  431.0 3.6 all-to-all-start.6
  434.6 4.3 add_home.1
  438.9 6.7 %expert_sums.1 = (f32[4,512,256]{2,1,0:T(8,128)}, f32[4,256,512]{2,1,0:T(8,128)}) custom-call(s32[2]{0:T(128)} %pad_add_fusion.z_ref.pos_ref, bf16[2,2,2,2,2,512,256]{6,5,4,3,2,1,0:T(8,128)(2,1)} %get-tuple-element.82.refs_0_.refs_2_.refs_4_.refs_6_.refs_3_.refs_9_.refs_8_.refs_12_, ...), custom_call_target="tpu_custom_call" | custom-call | flops 1000000 | bytes 100000 | tf_op jit(solution)/shard_map/expert_sums/pallas_call | solution.py:1049
  448.2 1.7 all-to-all-done.6
  450.4 1.4 copy-done.4
  451.8 1.8 add.151
  (156 shorter events, 21.0 us)
Async XLA Ops:
  7.2 126.3 %copy-start = (bf16[512,16]{0,1:T(8,128)(2,1)S(1)}, bf16[512,16]{0,1:T(8,128)(2,1)}, u32[]{:S(2)}) copy-start(bf16[512,16]{0,1:T(8,128)(2,1)} %param.15) | copy-start | bytes 49156
  7.2 118.6 %all-gather.6.cloned.1.call-start = ((), (), s32[]{:S(2)}) async-start(), calls=%async_computation.11 | async-start | bytes 5242880 | tf_op jit(solution)/shard_map/all_gather | solution.py:1128
  7.3 6.9 %copy-start.6 = (f32[2,2,256,512]{3,2,1,0:T(8,128)S(1)}, f32[2,2,256,512]{3,2,1,0:T(8,128)}, u32[]{:S(2)}) copy-start(f32[2,2,256,512]{3,2,1,0:T(8,128)} %param.12) | copy-start | bytes 6291460
  10.2 21.2 %collective-permute-start.1 = (bf16[256,512]{1,0:T(8,128)(2,1)}, bf16[256,512]{1,0:T(8,128)(2,1)S(1)}, u32[]{:S(2)}, u32[]{:S(2)}) collective-permute-start(bf16[256,512]{1,0:T(8,128)(2,1)} %get-tuple-element.113), channel_id=1, source_target_pairs={{0,2},{1,3},{2,0},{3,1},{4,6},{5,7},{6,4},{7,5},{8,10},{9,11},{10,... | collective-permute-start | bytes 786440 | tf_op jit(solution)/shard_map/ppermute | solution.py:940
  15.1 4.5 collective-permute-start.3
  15.1 6.6 %collective-permute-start.4 = (bf16[4,32,512]{2,1,0:T(8,128)(2,1)}, bf16[4,32,512]{2,1,0:T(8,128)(2,1)}, u32[]{:S(2)}, u32[]{:S(2)}) collective-permute-start(bf16[4,32,512]{2,1,0:T(8,128)(2,1)} %get-tuple-element.106), channel_id=1, source_target_pairs={{0,8},{4,12},{8,0},{12,4},{16,24},{20,28},{24,16},{28,20},{1,9},{5... | collective-permute-start | bytes 393224 | tf_op jit(solution)/shard_map/ppermute | solution.py:1124
  16.6 8.5 %collective-permute-start.5 = (bf16[4,32,512]{2,1,0:T(8,128)(2,1)}, bf16[4,32,512]{2,1,0:T(8,128)(2,1)}, u32[]{:S(2)}, u32[]{:S(2)}) collective-permute-start(bf16[4,32,512]{2,1,0:T(8,128)(2,1)} %get-tuple-element.105), channel_id=1, source_target_pairs={{0,12},{4,8},{8,4},{12,0},{16,28},{20,24},{24,20},{28,16},{1,13},{... | collective-permute-start | bytes 393224 | tf_op jit(solution)/shard_map/ppermute | solution.py:1124
  17.0 10.2 %collective-permute-start.6 = (bf16[4,32,512]{2,1,0:T(8,128)(2,1)}, bf16[4,32,512]{2,1,0:T(8,128)(2,1)}, u32[]{:S(2)}, u32[]{:S(2)}) collective-permute-start(bf16[4,32,512]{2,1,0:T(8,128)(2,1)} %get-tuple-element.104), channel_id=1, source_target_pairs={{0,16},{4,20},{8,24},{12,28},{16,0},{20,4},{24,8},{28,12},{1,17},{... | collective-permute-start | bytes 393224 | tf_op jit(solution)/shard_map/ppermute | solution.py:1124
  19.6 10.8 %collective-permute-start.7 = (bf16[4,32,512]{2,1,0:T(8,128)(2,1)}, bf16[4,32,512]{2,1,0:T(8,128)(2,1)S(1)}, u32[]{:S(2)}, u32[]{:S(2)}) collective-permute-start(bf16[4,32,512]{2,1,0:T(8,128)(2,1)} %get-tuple-element.103), channel_id=1, source_target_pairs={{0,20},{4,16},{8,28},{12,24},{16,4},{20,0},{24,12},{28,8},{1,21},{... | collective-permute-start | bytes 393224 | tf_op jit(solution)/shard_map/ppermute | solution.py:1124
  21.7 12.7 %copy-start.28 = (pred[8]{0:T(512)(128)(4,1)S(1)}, pred[8]{0:T(512)(128)(4,1)}, u32[]{:S(2)}) copy-start(pred[8]{0:T(512)(128)(4,1)} %compare_and_fusion) | copy-start | bytes 28
  21.7 8.8 %collective-permute-start.8 = (bf16[4,32,512]{2,1,0:T(8,128)(2,1)}, bf16[4,32,512]{2,1,0:T(8,128)(2,1)S(1)}, u32[]{:S(2)}, u32[]{:S(2)}) collective-permute-start(bf16[4,32,512]{2,1,0:T(8,128)(2,1)} %get-tuple-element.102), channel_id=1, source_target_pairs={{0,24},{4,28},{8,16},{12,20},{16,8},{20,12},{24,0},{28,4},{1,25},{... | collective-permute-start | bytes 393224 | tf_op jit(solution)/shard_map/ppermute | solution.py:1124
  25.1 6.3 %collective-permute-start.9 = (bf16[4,32,512]{2,1,0:T(8,128)(2,1)S(1)}, bf16[4,32,512]{2,1,0:T(8,128)(2,1)S(1)}, u32[]{:S(2)}, u32[]{:S(2)}) collective-permute-start(bf16[4,32,512]{2,1,0:T(8,128)(2,1)S(1)} %get-tuple-element.101), channel_id=1, source_target_pairs={{0,28},{4,24},{8,20},{12,16},{16,12},{20,8},{24,4},{28,0},{1,29},{... | collective-permute-start | bytes 393224 | tf_op jit(solution)/shard_map/ppermute | solution.py:1124
  31.4 0.7 copy-start.19
  32.0 0.7 copy-start.16
  34.4 1.2 copy-start.22
  34.4 2.9 copy-start.21
  35.6 130.5 %all-gather.10.cloned.1.call-start = ((), (), s32[]{:S(2)}) async-start(), calls=%async_computation.16 | async-start | bytes 2621440 | tf_op jit(solution)/shard_map/all_gather | solution.py:1152
  35.7 11.1 %collective-permute-start = (bf16[256,512]{1,0:T(8,128)(2,1)S(1)}, bf16[256,512]{1,0:T(8,128)(2,1)S(1)}, u32[]{:S(2)}, u32[]{:S(2)}) collective-permute-start(bf16[256,512]{1,0:T(8,128)(2,1)S(1)} %copy-done.22), channel_id=1, source_target_pairs={{0,1},{1,2},{2,3},{3,0},{4,5},{5,6},{6,7},{7,4},{8,9},{9,10},{10,1... | collective-permute-start | bytes 786440 | tf_op jit(solution)/shard_map/ppermute | solution.py:940
  37.3 22.2 %collective-permute-start.2 = (bf16[256,512]{1,0:T(8,128)(2,1)S(1)}, bf16[256,512]{1,0:T(8,128)(2,1)S(1)}, u32[]{:S(2)}, u32[]{:S(2)}) collective-permute-start(bf16[256,512]{1,0:T(8,128)(2,1)S(1)} %copy-done.21), channel_id=1, source_target_pairs={{0,3},{1,0},{2,1},{3,2},{4,7},{5,4},{6,5},{7,6},{8,11},{9,8},{10,9... | collective-permute-start | bytes 786440 | tf_op jit(solution)/shard_map/ppermute | solution.py:940
  46.7 12.8 %copy-start.23 = (bf16[256,512]{1,0:T(8,128)(2,1)}, bf16[256,512]{1,0:T(8,128)(2,1)S(1)}, u32[]{:S(2)}) copy-start(bf16[256,512]{1,0:T(8,128)(2,1)S(1)} %collective-permute-done.refs_1_) | copy-start | bytes 786436
  59.5 0.7 copy-start.24
  99.8 113.0 %all-gather.8.cloned.1.call-start = ((), (), s32[]{:S(2)}) async-start(), calls=%async_computation.15 | async-start | bytes 2621440 | tf_op jit(solution)/shard_map/all_gather | solution.py:1154
  99.9 25.4 %copy-start.27 = (s32[2,3]{1,0:T(2,128)S(1)}, s32[2,3]{1,0:T(2,128)}, u32[]{:S(2)}) copy-start(s32[2,3]{1,0:T(2,128)} %param.20) | copy-start | bytes 76
  124.4 3.8 copy-start.2
  125.8 6.6 %copy-start.29 = (s32[2,16]{1,0:T(2,128)S(1)}, s32[2,16]{1,0:T(2,128)}, u32[]{:S(2)}) copy-start(s32[2,16]{1,0:T(2,128)} %param.21) | copy-start | bytes 388
  128.2 37.9 %all-to-all-start.2 = ((bf16[8,4,32,512]{3,2,1,0:T(8,128)(2,1)}), bf16[8,4,32,512]{3,2,1,0:T(8,128)(2,1)S(1)}, u32[]{:S(2)}, u32[]{:S(2)}) async-start(bf16[8,4,32,512]{3,2,1,0:T(8,128)(2,1)} %copy_bitcast_fusion), calls=%async_computation.2 | async-start | bytes 2097152 | tf_op jit(solution)/shard_map/all_to_all | solution.py:1146
  131.8 127.5 %reduce-scatter.4.cloned.1.call-start = ((), (), s32[]{:S(2)}) async-start(), calls=%async_computation.12 | async-start | bytes 2621440 | tf_op jit(solution)/shard_map/reduce_scatter | solution.py:1164
  132.3 33.8 %copy-start.20 = (f32[2,3,256]{2,1,0:T(4,128)}, f32[2,3,256]{2,1,0:T(4,128)S(1)}, u32[]{:S(2)}) copy-start(f32[2,3,256]{2,1,0:T(4,128)S(1)} %copy.86.refs_4_.refs_3_.refs_5_) | copy-start | bytes 18436
  166.1 1.0 copy-start.3
  212.9 90.9 %reduce-scatter.6.cloned.1.call-start = ((), (), s32[]{:S(2)}) async-start(), calls=%async_computation.13 | async-start | bytes 2621440 | tf_op jit(solution)/shard_map/reduce_scatter | solution.py:1170
  259.3 1.0 copy-start.14
  259.3 163.5 %reduce-scatter.8.cloned.1.call-start = ((), (), s32[]{:S(2)}) async-start(), calls=%async_computation.14 | async-start | bytes 5242880 | tf_op jit(solution)/shard_map/reduce_scatter | solution.py:1174
  303.8 14.6 %collective-permute-start.10 = (bf16[2,2,2,2,2,512,256]{6,5,4,3,2,1,0:T(8,128)(2,1)}, bf16[2,2,2,2,2,512,256]{6,5,4,3,2,1,0:T(8,128)(2,1)}, u32[]{:S(2)}, u32[]{:S(2)}) collective-permute-start(bf16[2,2,2,2,2,512,256]{6,5,4,3,2,1,0:T(8,128)(2,1)} %after.14), channel_id=1, source_target_pairs={{0,4},{4,0},{8,12},{12,8},{16,20},{20,16},{24,28},{28,24},{1,5},{5... | collective-permute-start | bytes 25165832 | tf_op jit(solution)/shard_map/ppermute | solution.py:1177
  303.8 1.0 copy-start.5
  318.4 10.8 %copy-start.25 = (f32[16,512]{1,0:T(8,128)S(1)}, f32[16,512]{1,0:T(8,128)}, u32[]{:S(2)}) copy-start(f32[16,512]{1,0:T(8,128)} %get-tuple-element.61.refs_2_) | copy-start | bytes 98308
  318.4 10.8 %copy-start.26 = (f32[16,512]{1,0:T(8,128)S(1)}, f32[16,512]{1,0:T(8,128)}, u32[]{:S(2)}) copy-start(f32[16,512]{1,0:T(8,128)} %get-tuple-element.90) | copy-start | bytes 98308
  325.1 31.6 %collective-permute-start.11 = (bf16[2,2,512,256]{3,2,1,0:T(8,128)(2,1)}, bf16[2,2,512,256]{3,2,1,0:T(8,128)(2,1)S(1)}, u32[]{:S(2)}, u32[]{:S(2)}) collective-permute-start(bf16[2,2,512,256]{3,2,1,0:T(8,128)(2,1)} %get-tuple-element.84.refs_12_), channel_id=1, source_target_pairs={{0,8},{4,12},{8,0},{12,4},{16,24},{20,28},{24,16},{28,20},{1,9},{5... | collective-permute-start | bytes 3145736 | tf_op jit(solution)/shard_map/ppermute | solution.py:1061
  325.7 46.3 %collective-permute-start.12 = (bf16[2,2,512,256]{3,2,1,0:T(8,128)(2,1)}, bf16[2,2,512,256]{3,2,1,0:T(8,128)(2,1)S(1)}, u32[]{:S(2)}, u32[]{:S(2)}) collective-permute-start(bf16[2,2,512,256]{3,2,1,0:T(8,128)(2,1)} %get-tuple-element.85.refs_13_), channel_id=1, source_target_pairs={{0,8},{4,12},{8,0},{12,4},{16,24},{20,28},{24,16},{28,20},{1,9},{5... | collective-permute-start | bytes 3145736 | tf_op jit(solution)/shard_map/ppermute | solution.py:1061
  327.2 44.8 %collective-permute-start.13 = (bf16[2,2,512,256]{3,2,1,0:T(8,128)(2,1)}, bf16[2,2,512,256]{3,2,1,0:T(8,128)(2,1)S(1)}, u32[]{:S(2)}, u32[]{:S(2)}) collective-permute-start(bf16[2,2,512,256]{3,2,1,0:T(8,128)(2,1)} %get-tuple-element.86.refs_14_), channel_id=1, source_target_pairs={{0,16},{4,20},{8,24},{12,28},{16,0},{20,4},{24,8},{28,12},{1,17},{... | collective-permute-start | bytes 3145736 | tf_op jit(solution)/shard_map/ppermute | solution.py:1061
  327.8 45.9 %collective-permute-start.14 = (bf16[2,2,512,256]{3,2,1,0:T(8,128)(2,1)}, bf16[2,2,512,256]{3,2,1,0:T(8,128)(2,1)}, u32[]{:S(2)}, u32[]{:S(2)}) collective-permute-start(bf16[2,2,512,256]{3,2,1,0:T(8,128)(2,1)} %get-tuple-element.87.refs_15_), channel_id=1, source_target_pairs={{0,16},{4,20},{8,24},{12,28},{16,0},{20,4},{24,8},{28,12},{1,17},{... | collective-permute-start | bytes 3145736 | tf_op jit(solution)/shard_map/ppermute | solution.py:1061
  356.7 16.9 %copy-start.7 = (bf16[2,2,512,256]{3,2,1,0:T(8,128)(2,1)}, bf16[2,2,512,256]{3,2,1,0:T(8,128)(2,1)S(1)}, u32[]{:S(2)}) copy-start(bf16[2,2,512,256]{3,2,1,0:T(8,128)(2,1)S(1)} %collective-permute-done.11.refs_2_) | copy-start | bytes 3145732
  372.1 1.6 copy-start.8
  372.1 1.6 copy-start.9
  380.5 3.0 collective-permute-start.15
  383.4 6.2 %copy-start.15 = (bf16[1024,512]{1,0:T(8,128)(2,1)S(1)}, bf16[1024,512]{1,0:T(8,128)(2,1)}, u32[]{:S(2)}) copy-start(bf16[1024,512]{1,0:T(8,128)(2,1)} %get-tuple-element.93) | copy-start | bytes 3145732
  386.0 28.3 %all-to-all-start.5 = ((bf16[4,64,2176]{2,1,0:T(8,128)(2,1)}), bf16[4,64,2176]{2,1,0:T(8,128)(2,1)S(1)}, u32[]{:S(2)}, u32[]{:S(2)}) async-start(bf16[4,64,2176]{2,1,0:T(8,128)(2,1)} %fusion.2), calls=%async_computation.8 | async-start | bytes 2228224 | tf_op jit(solution)/shard_map/all_to_all | solution.py:1201
  390.4 11.1 %collective-permute-start.16 = (bf16[256,512]{1,0:T(8,128)(2,1)S(1)}, bf16[256,512]{1,0:T(8,128)(2,1)S(1)}, u32[]{:S(2)}, u32[]{:S(2)}) collective-permute-start(bf16[256,512]{1,0:T(8,128)(2,1)S(1)} %get-tuple-element.111), channel_id=1, source_target_pairs={{0,1},{1,2},{2,3},{3,0},{4,5},{5,6},{6,7},{7,4},{8,9},{9,10},{10,1... | collective-permute-start | bytes 786440 | tf_op jit(solution)/shard_map/ppermute | solution.py:940
  390.5 21.3 %collective-permute-start.17 = (bf16[256,512]{1,0:T(8,128)(2,1)S(1)}, bf16[256,512]{1,0:T(8,128)(2,1)S(1)}, u32[]{:S(2)}, u32[]{:S(2)}) collective-permute-start(bf16[256,512]{1,0:T(8,128)(2,1)S(1)} %get-tuple-element.110), channel_id=1, source_target_pairs={{0,2},{1,3},{2,0},{3,1},{4,6},{5,7},{6,4},{7,5},{8,10},{9,11},{10,... | collective-permute-start | bytes 786440 | tf_op jit(solution)/shard_map/ppermute | solution.py:940
  392.6 22.7 %collective-permute-start.18 = (bf16[256,512]{1,0:T(8,128)(2,1)}, bf16[256,512]{1,0:T(8,128)(2,1)}, u32[]{:S(2)}, u32[]{:S(2)}) collective-permute-start(bf16[256,512]{1,0:T(8,128)(2,1)} %get-tuple-element.109), channel_id=1, source_target_pairs={{0,3},{1,0},{2,1},{3,2},{4,7},{5,4},{6,5},{7,6},{8,11},{9,8},{10,9... | collective-permute-start | bytes 786440 | tf_op jit(solution)/shard_map/ppermute | solution.py:940
  395.2 27.6 %collective-permute-start.19 = (bf16[2,512,256]{2,1,0:T(8,128)(2,1)}, bf16[2,512,256]{2,1,0:T(8,128)(2,1)S(1)}, u32[]{:S(2)}, u32[]{:S(2)}) collective-permute-start(bf16[2,512,256]{2,1,0:T(8,128)(2,1)} %get-tuple-element.89.refs_1_), channel_id=1, source_target_pairs={{0,16},{4,20},{8,24},{12,28},{16,0},{20,4},{24,8},{28,12},{1,17},{... | collective-permute-start | bytes 1572872 | tf_op jit(solution)/shard_map/ppermute | solution.py:1061
  397.2 29.6 %collective-permute-start.20 = (bf16[2,512,256]{2,1,0:T(8,128)(2,1)}, bf16[2,512,256]{2,1,0:T(8,128)(2,1)S(1)}, u32[]{:S(2)}, u32[]{:S(2)}) collective-permute-start(bf16[2,512,256]{2,1,0:T(8,128)(2,1)} %get-tuple-element.94), channel_id=1, source_target_pairs={{0,16},{4,20},{8,24},{12,28},{16,0},{20,4},{24,8},{28,12},{1,17},{... | collective-permute-start | bytes 1572872 | tf_op jit(solution)/shard_map/ppermute | solution.py:1061
  401.5 13.8 %copy-start.17 = (bf16[256,512]{1,0:T(8,128)(2,1)}, bf16[256,512]{1,0:T(8,128)(2,1)S(1)}, u32[]{:S(2)}) copy-start(bf16[256,512]{1,0:T(8,128)(2,1)S(1)} %collective-permute-done.16.refs_1_) | copy-start | bytes 786436
  401.6 25.3 %collective-permute-start.21 = (bf16[2,512,256]{2,1,0:T(8,128)(2,1)}, bf16[2,512,256]{2,1,0:T(8,128)(2,1)S(1)}, u32[]{:S(2)}, u32[]{:S(2)}) collective-permute-start(bf16[2,512,256]{2,1,0:T(8,128)(2,1)} %get-tuple-element.95), channel_id=1, source_target_pairs={{0,8},{4,12},{8,0},{12,4},{16,24},{20,28},{24,16},{28,20},{1,9},{5... | collective-permute-start | bytes 1572872 | tf_op jit(solution)/shard_map/ppermute | solution.py:1061
  411.8 0.7 copy-start.18
  412.5 14.4 %collective-permute-start.22 = (bf16[2,512,256]{2,1,0:T(8,128)(2,1)}, bf16[2,512,256]{2,1,0:T(8,128)(2,1)S(1)}, u32[]{:S(2)}, u32[]{:S(2)}) collective-permute-start(bf16[2,512,256]{2,1,0:T(8,128)(2,1)} %get-tuple-element.96), channel_id=1, source_target_pairs={{0,8},{4,12},{8,0},{12,4},{16,24},{20,28},{24,16},{28,20},{1,9},{5... | collective-permute-start | bytes 1572872 | tf_op jit(solution)/shard_map/ppermute | solution.py:1061
  415.3 15.7 %all-to-all-start.7 = ((bf16[4,16,2176]{2,1,0:T(8,128)(2,1)}), bf16[4,16,2176]{2,1,0:T(8,128)(2,1)S(1)}, u32[]{:S(2)}, u32[]{:S(2)}) async-start(bf16[4,16,2176]{2,1,0:T(8,128)(2,1)} %bitcast.147), calls=%async_computation.10 | async-start | bytes 557056 | tf_op jit(solution)/shard_map/all_to_all | solution.py:1207
  422.8 4.1 copy-start.10
  426.9 0.8 copy-start.11
  426.9 1.0 copy-start.12
  426.9 1.1 copy-start.13
  431.0 18.9 %all-to-all-start.6 = ((bf16[8,2,4,16,512]{4,3,2,1,0:T(8,128)(2,1)}), bf16[8,2,4,16,512]{4,3,2,1,0:T(8,128)(2,1)S(1)}, u32[]{:S(2)}, u32[]{:S(2)}) async-start(bf16[8,2,4,16,512]{4,3,2,1,0:T(8,128)(2,1)} %after.17), calls=%async_computation.9 | async-start | bytes 2097152 | tf_op jit(solution)/shard_map/all_to_all | solution.py:1146
  450.2 1.6 copy-start.4
  450.4 3.2 copy-start.1
Sparse Core Ops, SparseCore 0:
  35.7 82.7 all-gather.5
  120.1 45.9 all-gather.9
  167.6 44.7 all-gather.7
  215.1 42.5 reduce-scatter.3
  260.6 43.1 reduce-scatter.5
  305.9 76.0 reduce-scatter.7
